TPU v7x, 32 devices: a whole 2x2x4 slice. The times are simulated.
32 devices in a mesh: energy: 8 (over z, x), space: 4 (over y, core).
Axes of the slice: x: 2, y: 2, z: 4, core: 2. Of those that a mesh axis runs over, the one named last changes fastest.
Arguments:
- lesser_prev: float32 [2, 8, 4, 128, 128], P(None, 'energy', 'space'), may hold values from -6 to 6
- retarded: float32 [2, 8, 4, 128, 128], P(None, 'energy', 'space'), may hold values from -1.5 to 1.5, as said below
- coupling: float32 [2, 4, 128, 128], P(None, 'space'), may hold values from -1.5 to 1.5, as said below
- gradient_table: float32 [4, 2, 128, 128], replicated, may hold values from -0.5 to 0.5
- material: int32 [4], replicated, may hold values from 0 to 3
- offsets: int32 [8], replicated, may hold values from -2 to 2
- weights: float32 [8], replicated, may hold values from 0.05 to 0.3
Outputs:
- lesser_left: float32 [2, 8, 4, 128, 128], P(None, 'energy', 'space')
Inputs may be any that keep to these rules, and one draw needn't show every extreme that they name: `retarded`: each block is a complex diagonal of modulus below one plus small full-rank noise. `coupling`: each block is the identity plus small full-rank complex noise.
All inputs are finite; a program needn't handle non-finite values.
Results may differ from a plain program's by a relative error of at most 0.0001.
Values sent between devices are 32-bit elements; how exact they have to be, the bound alone decides.
No kernel may reach another device: no remote copies, remote signals or barrier semaphores. Data moves between devices by JAX's collectives and lax.ppermute only.
A program may use at most 64 MiB of HBM per device.

v0:
```python
import jax
import jax.numpy as jnp
from jax import lax
from jax.sharding import PartitionSpec as P

HIGHEST_PRECISION = lax.Precision.HIGHEST


def with_halo(cells, sides, width):
    for axis, dim in sides:
        count = lax.axis_size(axis)
        ends = count - 1
        head = lax.slice_in_dim(cells, 0, width, axis=dim)
        tail = lax.slice_in_dim(cells, cells.shape[dim] - width, cells.shape[dim], axis=dim)
        cells = jnp.concatenate(
            [
                lax.ppermute(tail, axis, [(i, (i + 1) % count) for i in range(ends)]),
                cells,
                lax.ppermute(head, axis, [((i + 1) % count, i) for i in range(ends)]),
            ],
            axis=dim,
        )
    return cells


def carried_in(value, axis, join, neutral):
    count, mine = (lax.axis_size(axis), lax.axis_index(axis))
    pieces = jax.tree.map(lambda part: lax.all_gather(part, axis), value)
    so_far = jax.tree.map(
        lambda part, zero: jnp.full_like(part, 0) + jnp.asarray(zero, part.dtype), value, neutral
    )

    def step(position, so_far):
        longer = join(so_far, jax.tree.map(lambda part: part[position], pieces))
        return jax.tree.map(lambda new, old: jnp.where(position < mine, new, old), longer, so_far)

    return lax.fori_loop(0, count - 1, step, so_far)


def real_product(left, right):
    return jnp.matmul(left, right, precision=HIGHEST_PRECISION)


def complex_product(left, right):
    real_part = real_product(left[0], right[0]) - real_product(left[1], right[1])
    imag_part = real_product(left[0], right[1]) + real_product(left[1], right[0])
    return jnp.stack([real_part, imag_part])


def dagger(matrix):
    return jnp.stack([jnp.swapaxes(matrix[0], -1, -2), -jnp.swapaxes(matrix[1], -1, -2)])


def sandwich(outer, inner):
    return complex_product(complex_product(outer, inner), dagger(outer))


def compose(earlier, following):
    return (
        complex_product(following[0], earlier[0]),
        sandwich(following[0], earlier[1]) + following[1],
    )


def phonon_matrix(offsets, weights, count):
    grid = jnp.arange(count, dtype=jnp.int32)
    hits = (grid[None, None, :] == grid[None, :, None] + offsets[:, None, None]).astype(jnp.float32)
    return jnp.einsum("k,kef->ef", weights, hits, precision=HIGHEST_PRECISION)


def per_device(lesser_prev, retarded, coupling, gradient_table, material, offsets, weights):
    energy_count = lesser_prev.shape[1]
    slab_count = lesser_prev.shape[2]
    orbitals = lesser_prev.shape[3]
    total_energy = energy_count * lax.axis_size("energy")
    first_slab = lax.axis_index("space") * slab_count
    padded_kind = jnp.concatenate([material[:1], material])
    slab_kinds = lax.dynamic_slice_in_dim(padded_kind, first_slab, slab_count + 1)
    kind_range = jnp.arange(gradient_table.shape[0], dtype=jnp.int32)
    picks = (slab_kinds[:, None] == kind_range[None, :]).astype(jnp.float32)
    links_all = jnp.einsum("sk,kcab->csab", picks, gradient_table, precision=HIGHEST_PRECISION)
    own_links = links_all[:, None, 1:]
    prior_links = links_all[:, None, :-1]
    kernel = phonon_matrix(offsets, weights, total_energy)
    padded = with_halo(lesser_prev, (("space", 2),), 1)
    gain = complex_product(retarded, coupling[:, None])
    centre = padded[:, :, 1:-1]
    right_term = sandwich(own_links, padded[:, :, 2:])
    left_term = complex_product(
        complex_product(dagger(prior_links), padded[:, :, :-2]), prior_links
    )
    field = centre + right_term + left_term
    flattened = field.reshape(2, energy_count, slab_count * orbitals * orbitals)
    columns = lax.all_to_all(flattened, "energy", split_axis=2, concat_axis=1, tiled=True)
    smeared = jnp.einsum("ef,cfx->cex", kernel, columns, precision=HIGHEST_PRECISION)
    returned = lax.all_to_all(smeared, "energy", split_axis=1, concat_axis=2, tiled=True)
    sigma = returned.reshape(field.shape)
    source = sandwich(retarded, sigma)
    total_gain = gain[:, :, 0]
    total_source = source[:, :, 0]
    identity = jnp.eye(orbitals, dtype=jnp.float32)
    identity_gain = jnp.stack([identity, jnp.zeros_like(identity)])[:, None]
    prefix = carried_in(
        (total_gain, total_source), "space", compose, (identity_gain, jnp.zeros_like(total_source))
    )
    incoming = prefix[1]
    state = incoming
    state = sandwich(gain[:, :, 0], state) + source[:, :, 0]
    results = [state]
    return jnp.stack(results, axis=2)


def solution(mesh):
    placed = (
        P(None, "energy", "space", None, None),
        P(None, "energy", "space", None, None),
        P(None, "space", None, None),
        P(),
        P(),
        P(),
        P(),
    )
    return jax.shard_map(
        per_device,
        mesh=mesh,
        in_specs=placed,
        out_specs=P(None, "energy", "space", None, None),
        check_vma=False,
    )
```

profile of v0, /device:TPU:1, one launch (start us, length us, event | category | flops | bytes accessed | tf_op | source)
XLA Modules:
  0.0 173.6 jit_solution(6021915840077084823)
XLA Ops:
  0.0 4.7 %collective-permute-start.1 = (f32[2,1,1,128,128]{4,3,2,1,0:T(8,128)}, f32[2,1,1,128,128]{4,3,2,1,0:T(8,128)S(1)}, u32[]{:S(2)}, u32[]{:S(2)}) collective-permute-start(f32[2,1,1,128,128]{4,3,2,1,0:T(8,128)} %param.9), channel_id=1, source_target_pairs={{0,1},{1,2},{2,3},{4,5},{5,6},{6,7},{8,9},{9,10},{10,11},{12,13},{... | collective-permute-start | bytes 393224 | tf_op jit(solution)/shard_map/ppermute | solution.py:17
  4.7 1.9 %collective-permute-start = (f32[2,1,1,128,128]{4,3,2,1,0:T(8,128)}, f32[2,1,1,128,128]{4,3,2,1,0:T(8,128)S(1)}, u32[]{:S(2)}, u32[]{:S(2)}) collective-permute-start(f32[2,1,1,128,128]{4,3,2,1,0:T(8,128)} %param.9), channel_id=1, source_target_pairs={{1,0},{2,1},{3,2},{5,4},{6,5},{7,6},{9,8},{10,9},{11,10},{13,12},{... | collective-permute-start | bytes 393224 | tf_op jit(solution)/shard_map/ppermute | solution.py:19
  6.6 1.1 fusion.69
  7.7 1.1 fusion.61
  8.8 1.4 pad_add_fusion
  10.2 0.9 convolution_bitcast_fusion.1
  11.4 0.7 iota_add_fusion
  12.2 1.1 convolution_subtract_fusion.10
  13.3 0.8 fusion.105
  14.1 0.3 fusion.80
  14.4 0.3 convolution_subtract_fusion.7
  15.1 0.3 fusion.79
  15.4 0.3 convolution_add_fusion.7
  18.0 0.9 fusion.42
  19.0 4.6 %copy.20 = f32[2,1,1,128,128]{0,4,3,2,1:T(8,128)} copy(f32[2,1,1,128,128]{4,3,2,1,0:T(8,128)S(1)} %fusion.42) | data formatting | bytes 262144 | tf_op jit(solution)/shard_map/reshape | solution.py:93
  23.6 0.6 broadcast.29
  24.2 74.5 %reduce = f32[16384,2]{1,0:T(8,128)} reduce(f32[16384,1,2]{2,1,0:T(1,128)} %bitcast.278, f32[]{:T(128)} %broadcast.29), dimensions={1}, to_apply=%bitcast.191.reduce_sub_computation | reduce | bytes 262148
  98.7 8.3 %reshape.249 = f32[8,1,4096]{2,1,0:T(1,128)} reshape(f32[16384,2]{1,0:T(8,128)} %reduce) | data formatting | bytes 262144
  107.0 5.5 %all-to-all-start = ((f32[8,1,4096]{2,1,0:T(1,128)}), f32[8,1,4096]{2,1,0:T(1,128)S(1)}, u32[]{:S(2)}, u32[]{:S(2)}) async-start(f32[8,1,4096]{2,1,0:T(1,128)} %reshape.249), calls=%async_computation | async-start | bytes 262144 | tf_op jit(solution)/shard_map/all_to_all | solution.py:94
  112.8 6.0 %all-to-all-done = f32[8,1,4096]{2,1,0:T(1,128)S(1)} async-done(((f32[8,1,4096]{2,1,0:T(1,128)}), f32[8,1,4096]{2,1,0:T(1,128)S(1)}, u32[]{:S(2)}, u32[]{:S(2)}) %all-to-all-start) | async-done | bytes 131104 | tf_op jit(solution)/shard_map/all_to_all | solution.py:94
  118.7 1.0 reduce.1
  119.7 16.5 %reshape.250 = f32[16384,1,2]{2,1,0:T(1,128)} reshape(f32[8,4096]{1,0:T(8,128)S(1)} %reduce.1) | data formatting | bytes 262144
  136.2 5.2 %copy.21 = f32[2,8,2048]{2,1,0:T(8,128)S(1)} copy(f32[2,8,2048]{0,2,1:T(8,128)} %bitcast.279) | data formatting | bytes 262144 | tf_op jit(solution)/shard_map/all_to_all | solution.py:94
  141.7 0.8 copy.14
  142.4 3.4 %all-to-all-start.1 = ((f32[2,8,2048]{2,0,1:T(2,128)}), f32[2,8,2048]{2,0,1:T(2,128)S(1)}, u32[]{:S(2)}, u32[]{:S(2)}) async-start(f32[2,8,2048]{2,0,1:T(2,128)} %copy.14), calls=%async_computation.1 | async-start | bytes 262144 | tf_op jit(solution)/shard_map/all_to_all | solution.py:96
  145.9 9.3 %all-gather = f32[8,1,1,128,128]{4,3,2,1,0:T(8,128)S(1)} all-gather(f32[2,1,1,128,128]{4,3,2,1,0:T(8,128)S(1)} %pad_maximum_fusion), channel_id=2, replica_groups=mesh['energy'=8,'space'=4] {'space'}, dimensions={0}, use_global_device_ids=true | all-gather | bytes 655360 | tf_op jit(solution)/shard_map/all_gather | solution.py:28
  155.3 0.3 fusion.71
  155.6 0.3 fusion.73
  155.8 0.3 convolution_subtract_fusion.5
  156.1 0.3 fusion.56
  156.4 0.3 fusion.58
  156.7 0.3 convolution_add_fusion.5
  157.0 0.3 fusion.36
  157.3 0.3 fusion.35
  157.6 7.3 %all-gather.1 = f32[8,1,1,128,128]{4,3,2,1,0:T(8,128)S(1)} all-gather(f32[2,1,1,128,128]{4,3,2,1,0:T(8,128)S(1)} %pad_maximum_fusion.1), channel_id=3, replica_groups=mesh['energy'=8,'space'=4] {'space'}, dimensions={0}, use_global_device_ids=true | all-gather | bytes 655360 | tf_op jit(solution)/shard_map/all_gather | solution.py:28
  164.9 6.1 %while.14 = (s32[]{:T(128)}, f32[2,1,128,128]{3,2,1,0:T(8,128)S(1)}, s32[]{:T(128)}, f32[4,2,1,128,128]{4,3,2,1,0:T(8,128)S(1)}, f32[4,2,1,128,128]{4,3,1,2,0:T(8,128)S(1)}, /*index=5*/s32[]{:T(128)}, s32[]{:T(128)}, s32[]{}) while((s32[]{:T(128)}, f32[2,1,128,128]{3,2,1,0:T(8,128)S(1)}, s32[]{:T(128)}, ...), condition=%wide.region_1.2_spmd.clone, body=%wide.region_0.1_spmd.clone.sunk | while | flops 201588736 | bytes 2621610 | solution.py:37
  165.8 0.3 fusion.199
  166.1 0.3 fusion.200
  166.3 0.3 fusion.196
  166.6 0.3 fusion.198
  167.8 0.3 fusion.199
  168.1 0.3 fusion.200
  168.4 0.3 fusion.196
  168.7 0.3 fusion.198
  170.2 0.3 fusion.200
  170.4 0.3 fusion.196
  170.7 0.3 fusion.198
  173.0 0.7 maximum_add_fusion.2
  (57 shorter events, 8.5 us)
Async XLA Ops:
  0.0 10.2 %copy-start = (f32[4,2,128,128]{3,2,1,0:T(8,128)S(1)}, f32[4,2,128,128]{3,2,1,0:T(8,128)}, u32[]{:S(2)}) copy-start(f32[4,2,128,128]{3,2,1,0:T(8,128)} %param.12) | copy-start | bytes 1572868
  0.0 14.1 %collective-permute-start.1 = (f32[2,1,1,128,128]{4,3,2,1,0:T(8,128)}, f32[2,1,1,128,128]{4,3,2,1,0:T(8,128)S(1)}, u32[]{:S(2)}, u32[]{:S(2)}) collective-permute-start(f32[2,1,1,128,128]{4,3,2,1,0:T(8,128)} %param.9), channel_id=1, source_target_pairs={{0,1},{1,2},{2,3},{4,5},{5,6},{6,7},{8,9},{9,10},{10,11},{12,13},{... | collective-permute-start | bytes 393224 | tf_op jit(solution)/shard_map/ppermute | solution.py:17
  4.7 11.4 %collective-permute-start = (f32[2,1,1,128,128]{4,3,2,1,0:T(8,128)}, f32[2,1,1,128,128]{4,3,2,1,0:T(8,128)S(1)}, u32[]{:S(2)}, u32[]{:S(2)}) collective-permute-start(f32[2,1,1,128,128]{4,3,2,1,0:T(8,128)} %param.9), channel_id=1, source_target_pairs={{1,0},{2,1},{3,2},{5,4},{6,5},{7,6},{9,8},{10,9},{11,10},{13,12},{... | collective-permute-start | bytes 393224 | tf_op jit(solution)/shard_map/ppermute | solution.py:19
  98.7 13.8 %copy-start.1 = (f32[2,1,1,128,128]{4,3,2,1,0:T(8,128)S(1)}, f32[2,1,1,128,128]{4,3,2,1,0:T(8,128)}, u32[]{:S(2)}) copy-start(f32[2,1,1,128,128]{4,3,2,1,0:T(8,128)} %param.10) | copy-start | bytes 393220
  98.7 13.8 %copy-start.2 = (f32[2,1,128,128]{3,2,1,0:T(8,128)S(1)}, f32[2,1,128,128]{3,2,1,0:T(8,128)}, u32[]{:S(2)}) copy-start(f32[2,1,128,128]{3,2,1,0:T(8,128)} %param.11) | copy-start | bytes 393220
  107.0 11.7 %all-to-all-start = ((f32[8,1,4096]{2,1,0:T(1,128)}), f32[8,1,4096]{2,1,0:T(1,128)S(1)}, u32[]{:S(2)}, u32[]{:S(2)}) async-start(f32[8,1,4096]{2,1,0:T(1,128)} %reshape.249), calls=%async_computation | async-start | bytes 262144 | tf_op jit(solution)/shard_map/all_to_all | solution.py:94
  142.4 12.7 %all-to-all-start.1 = ((f32[2,8,2048]{2,0,1:T(2,128)}), f32[2,8,2048]{2,0,1:T(2,128)S(1)}, u32[]{:S(2)}, u32[]{:S(2)}) async-start(f32[2,8,2048]{2,0,1:T(2,128)} %copy.14), calls=%async_computation.1 | async-start | bytes 262144 | tf_op jit(solution)/shard_map/all_to_all | solution.py:96
where the time goes:
time: 174 us
  other arithmetic  79.7 us (46%)
  local copies, waits for them, and re-layouts  36.1 us (21%)
  matrix products  19.2 us (11%)
  blocking collectives  16.6 us (10%)
  starting transfers between devices  15.5 us (9%)
  waiting for transfers between devices  5.97 us (3%)
    unnamed x2, other arithmetic  74.5 us
    unnamed x9, local copies, waits for them, and re-layouts  25.3 us
    dot_general x60, matrix products, real_product(): return jnp.matmul(left, right, precision=HIGHEST_PRECISION)  17.2 us
    all_gather x2, blocking collectives, carried_in(): pieces = jax.tree.map(lambda part: lax.all_gather(part, axis), value)  16.6 us
    all_to_all x1, waiting for transfers between devices, per_device(): lax.all_to_all(flattened, 'energy', split_axis=2, concat_axis=1, tiled=True)  5.97 us
    all_to_all x1, starting transfers between devices, per_device(): lax.all_to_all(flattened, 'energy', split_axis=2, concat_axis=1, tiled=True)  5.53 us
    all_to_all x1, local copies, waits for them, and re-layouts, per_device(): lax.all_to_all(flattened, 'energy', split_axis=2, concat_axis=1, tiled=True)  5.22 us
    ppermute x1, starting transfers between devices, with_halo(): lax.ppermute(tail, axis, [(i, (i + 1) % count) for i in range(ends)])  4.66 us
  transfers between devices with their start and end apart: 4, of which 1 were waited for; matrix products, arithmetic and copies ran while one was open for 6% of the time, Pallas kernels for 0%

commit v1 on v0

v1 whole, which is shorter than its diff:
```python
import functools

import jax
import jax.numpy as jnp
from jax import lax
from jax.experimental import pallas as pl
from jax.experimental.pallas import tpu as pltpu
from jax.sharding import PartitionSpec as P

F32 = jnp.float32
BF16 = jnp.bfloat16
VMEM = pl.BlockSpec(memory_space=pltpu.VMEM)
SMEM = pl.BlockSpec(memory_space=pltpu.SMEM)
NN = (((1,), (0,)), ((), ()))
NT = (((1,), (1,)), ((), ()))


def split(value):
    high = value.astype(BF16)
    return high, (value - high.astype(F32)).astype(BF16)


def rows(block):
    return jnp.concatenate([block[0], block[1]], axis=1)


def full(row):
    half = row.shape[1] // 2
    turned = jnp.concatenate([-row[:, half:], row[:, :half]], axis=1)
    return jnp.concatenate([row, turned], axis=0)


def product(left, right, dims):
    def dot(a, b):
        return lax.dot_general(a, b, dims, preferred_element_type=F32)

    return dot(left[0], right[0]) + (dot(left[0], right[1]) + dot(left[1], right[0]))


def times(left, right_block):
    return product(left, [full(part) for part in split(rows(right_block))], NN)


def times_dagger(left, right_block):
    return product(left, [full(part) for part in split(rows(right_block))], NT)


def smear_kernel(group, offsets, weights, own, other_a, other_b, *outs):
    count = lax.axis_size("energy")
    mine = lax.axis_index("energy")
    place, rank = mine // group, mine % group
    source_a, source_b, has_a, has_b = partners(place, count // group, mine, group)

    def coefficient(target, source, valid):
        total = jnp.float32(0)
        for mode in range(offsets.shape[0]):
            total += jnp.where(target + offsets[mode] == source, weights[mode], jnp.float32(0))
        return jnp.where(valid, total, jnp.float32(0))

    for step in range(group):
        target = place * group + (rank + step) % group
        outs[step][...] = (
            coefficient(target, mine, True) * own[...]
            + coefficient(target, source_a, has_a) * other_a[...]
            + coefficient(target, source_b, has_b) * other_b[...]
        )


def partners(place, places, mine, group):
    even = place % 2 == 0
    side_a = jnp.where(even, 1, -1)
    has_a = (place + side_a < places) & (place + side_a >= 0)
    has_b = (place - side_a < places) & (place - side_a >= 0)
    return mine + side_a * group, mine - side_a * group, has_a, has_b


def matchings(places, group):
    result = []
    for first in (0, 1):
        pairs = []
        for place in range(places):
            other = place + 1 if place % 2 == first else place - 1
            for rank in range(group):
                mine = place * group + rank
                if 0 <= other < places:
                    pairs.append((mine, other * group + rank))
                elif group % 2 == 0:
                    pairs.append((mine, mine ^ 1))
        result.append(pairs)
    return result


def factor_kernel(count, material, table, *refs):
    retarded, coupling, outs = refs[:count], refs[count : 2 * count], refs[2 * count : 2 * count + 2]
    held_r, held_c = refs[2 * count + 2 :]
    mine = lax.axis_index("space")
    size = table.shape[-1]
    for slot in range(count):
        held_r[slot] = retarded[slot][...]
        held_c[slot] = coupling[slot][...]

    def store(slab, which, value, valid):
        slot = jnp.bitwise_xor(mine, lax.rem(slab + count, count))
        value = jnp.where(valid, value, jnp.float32(0))
        for out, part in zip(outs, split(value)):
            out[slot, which * size : (which + 1) * size] = part

    def step(index, state):
        slab = mine - index
        here = jnp.maximum(slab, 0)
        before = jnp.maximum(slab - 1, 0)
        parts = split(state)
        store(slab, 0, state, slab >= 0)
        store(slab + 1, 1, times(parts, table[material[here]]), (slab >= 0) & (slab + 1 < count))
        store(slab - 1, 2, times_dagger(parts, table[material[before]]), slab >= 1)
        carried = times(parts, held_c[jnp.bitwise_xor(mine, here)])
        return times(split(carried), held_r[jnp.bitwise_xor(mine, before)])

    state = rows(held_r[0])
    if count <= 4:
        for index in range(count):
            state = step(index, state)
    else:
        lax.fori_loop(0, count, step, state)


def field_kernel(slots, has_start, *refs):
    fields, (high, low), rest = refs[: len(slots)], refs[len(slots) : len(slots) + 2], refs[len(slots) + 2 :]
    out = rest[-1]
    size = out.shape[-1]
    total = rows(rest[0]) if has_start else None
    for field, slot in zip(fields, slots):
        factors = (high[slot], low[slot])
        left = split(times(factors, field))
        for which in range(3):
            part = slice(which * size, (which + 1) * size)
            term = product([p[part] for p in left], [full(f[part]) for f in factors], NT)
            total = term if total is None else total + term
    out[0] = total[:, :size]
    out[1] = total[:, size:]


def call(kernel, shapes, specs, *args, scratch=(), flops=0):
    return pl.pallas_call(
        kernel,
        out_shape=shapes,
        in_specs=specs,
        out_specs=jax.tree.map(lambda _: VMEM, shapes),
        scratch_shapes=scratch,
        compiler_params=pltpu.CompilerParams(vmem_limit_bytes=32 * 2**20),
        cost_estimate=pl.CostEstimate(
            flops=flops, bytes_accessed=sum(a.size * a.dtype.itemsize for a in args), transcendentals=0
        ),
    )(*args)


def exchange(value, bit):
    count = lax.axis_size("space")
    return lax.ppermute(value, "space", [(i, i ^ bit) for i in range(count)])


def gather(slots, bits):
    for bit in bits:
        keys = list(slots)
        moved = exchange(jnp.concatenate([slots[key] for key in keys], axis=0), bit)
        parts = jnp.split(moved, len(keys), axis=0)
        slots = slots | {key ^ bit: part for key, part in zip(keys, parts)}
    return slots


def per_device(lesser_prev, retarded, coupling, gradient_table, material, offsets, weights):
    size = lesser_prev.shape[-1]
    energies, slabs = lax.axis_size("energy"), lax.axis_size("space")
    group = max(energies // 4, 1)
    block = jax.ShapeDtypeStruct((2, size, size), F32)
    own = lesser_prev.reshape(2, size, size)
    chip_bits = [1 << b for b in range(1, slabs.bit_length() - 1)]

    pairs_a, pairs_b = matchings(energies // group, group)
    other_a = lax.ppermute(own, "energy", pairs_a)
    other_b = lax.ppermute(own, "energy", pairs_b)
    packed = jnp.concatenate([retarded.reshape(2, size, size), coupling.reshape(2, size, size)], axis=0)
    packed = gather({0: packed}, chip_bits + [1])

    sums = call(
        functools.partial(smear_kernel, group), [block] * group, [SMEM, SMEM, VMEM, VMEM, VMEM],
        offsets, weights, own, other_a, other_b,
    )
    if group == 2 and len(chip_bits) == 1:
        bit = chip_bits[0]
        both = [
            (e * slabs + s, (e ^ 1) * slabs + (s ^ bit)) for e in range(energies) for s in range(slabs)
        ]
        far = lax.ppermute(sums[1], ("energy", "space"), both)
        near = lax.ppermute(sums[1], "energy", [(e, e ^ 1) for e in range(energies)])
        across = exchange(sums[0], bit)
        fields = {0: sums[0] + near, bit: across + far}
    else:
        field = sums[0]
        for step in range(1, group):
            pairs = [(e, e - e % group + (e + step) % group) for e in range(energies)]
            field = field + lax.ppermute(sums[step], "energy", pairs)
        fields = gather({0: field}, chip_bits)
    early = list(fields)
    fields = gather(fields, [1])
    late = [slot for slot in fields if slot not in early]

    order = range(slabs)
    factor_shape = jax.ShapeDtypeStruct((slabs, 3 * size, 2 * size), BF16)
    factors = call(
        functools.partial(factor_kernel, slabs), [factor_shape] * 2, [SMEM] + [VMEM] * (2 * slabs + 1),
        material, gradient_table, *[packed[s][:2] for s in order], *[packed[s][2:] for s in order],
        scratch=[pltpu.VMEM((slabs, 2, size, size), F32)] * 2, flops=10**9,
    )
    first = call(
        functools.partial(field_kernel, early, False), block, [VMEM] * (len(early) + 2),
        *[fields[s] for s in early], *factors, flops=10**9,
    )
    state = call(
        functools.partial(field_kernel, late, True), block, [VMEM] * (len(late) + 3),
        *[fields[s] for s in late], *factors, first, flops=10**9,
    )
    return state.reshape(lesser_prev.shape)


def solution(mesh):
    placed = (
        P(None, "energy", "space", None, None),
        P(None, "energy", "space", None, None),
        P(None, "space", None, None),
        P(),
        P(),
        P(),
        P(),
    )
    return jax.shard_map(
        per_device,
        mesh=mesh,
        in_specs=placed,
        out_specs=P(None, "energy", "space", None, None),
        check_vma=False,
    )
```

time: 174 us -> 28.9 us (0.17)
  other arithmetic: 79.7 us -> 1.11 us
  local copies, waits for them, and re-layouts: 36.1 us -> 1.07 us
  matrix products: 19.2 us -> 0 us
  blocking collectives: 16.6 us -> 0 us
  Pallas kernels: 0 us -> 6.92 us
  starting transfers between devices: 15.5 us -> 13.4 us
    unnamed x2 -> x0, other arithmetic: 74.5 us -> none
    unnamed x9 -> x14, local copies, waits for them, and re-layouts: 25.3 us -> 1 us
    dot_general x63 -> x0, matrix products: 19.2 us -> none  [the longest x60 17.2 us: real_product(): return jnp.matmul(left, right, precision=HIGHEST_PRECISION)]
    all_gather x2 -> x0, blocking collectives: 16.6 us -> none  [carried_in(): pieces = jax.tree.map(lambda part: lax.all_gather(part, axis), value)]
    all_to_all x2 -> x0, starting transfers between devices: 8.9 us -> none  [the longest x1 5.53 us: per_device(): lax.all_to_all(flattened, 'energy', split_axis=2, concat_axis=1, tiled=True)]
    pallas_call x0 -> x4, Pallas kernels: none -> 6.92 us  [call(): pl.pallas_call(kernel, out_shape=shapes, in_specs=specs, out_specs=jax.tr...]
    ppermute x2 -> x8, starting transfers between devices: 6.58 us -> 13.4 us  [the longest x4 8.45 us: exchange(): return lax.ppermute(value, 'space', [(i, i ^ bit) for i in range(count)])]
    all_to_all x2 -> x0, waiting for transfers between devices: 5.97 us -> none  [the longest x1 5.97 us: per_device(): lax.all_to_all(flattened, 'energy', split_axis=2, concat_axis=1, tiled=True)]
  transfers between devices with their start and end apart: 4 -> 8, of which waited for: 1 -> 4; matrix products, arithmetic and copies ran while one was open for 6% -> 0% of each run, Pallas kernels for 0% -> 2%
where the time goes in v1:
time: 28.9 us; the launch traced here: 28.4 us
  starting transfers between devices  13.4 us (46%)
  Pallas kernels  6.92 us (24%)
  waiting for transfers between devices  5.73 us (20%)
  other arithmetic  1.11 us (4%)
  local copies, waits for them, and re-layouts  1.07 us (4%)
    ppermute x4, starting transfers between devices, exchange(): return lax.ppermute(value, 'space', [(i, i ^ bit) for i in range(count)])  8.45 us
    pallas_call x4, Pallas kernels, call(): pl.pallas_call(kernel, out_shape=shapes, in_specs=specs, out_specs=jax.tr...  6.92 us
    ppermute x1, waiting for transfers between devices, per_device(): far = lax.ppermute(sums[1], ('energy', 'space'), both)  1.65 us
    ppermute x1, waiting for transfers between devices, per_device(): other_a = lax.ppermute(own, 'energy', pairs_a)  1.6 us
    ppermute x1, starting transfers between devices, per_device(): other_a = lax.ppermute(own, 'energy', pairs_a)  1.3 us
    ppermute x1, waiting for transfers between devices, per_device(): other_b = lax.ppermute(own, 'energy', pairs_b)  1.3 us
    ppermute x1, starting transfers between devices, per_device(): lax.ppermute(sums[1], 'energy', [(e, e ^ 1) for e in range(energies)])  1.28 us
    ppermute x1, starting transfers between devices, per_device(): other_b = lax.ppermute(own, 'energy', pairs_b)  1.21 us
  transfers between devices with their start and end apart: 8, of which 4 were waited for; matrix products, arithmetic and copies ran while one was open for 0% of the time, Pallas kernels for 2%

profile of v1, /device:TPU:1, one launch (start us, length us, event | category | flops | bytes accessed | tf_op | source)
XLA Modules:
  0.0 28.4 jit_solution(11909835938410095937)
XLA Ops:
  0.0 0.0 copy-start.2
  0.0 1.0 %pad_maximum_fusion.2 = f32[4,128,128]{2,1,0:T(8,128)S(1)} fusion(f32[2,128,128]{2,1,0:T(8,128)} %bitcast.9, f32[2,128,128]{2,1,0:T(8,128)} %bitcast.6), kind=kLoop, calls=%fused_computation.2 | loop fusion | flops 65536 | bytes 524288 | tf_op jit(solution)/shard_map/concatenate | solution.py:182
  1.0 0.0 copy-start.3
  1.0 0.0 copy-start.4
  1.1 2.1 %collective-permute-start.6 = (f32[4,128,128]{2,1,0:T(8,128)S(1)}, f32[4,128,128]{2,1,0:T(8,128)S(1)}, u32[]{:S(2)}, u32[]{:S(2)}) collective-permute-start(f32[4,128,128]{2,1,0:T(8,128)S(1)} %pad_maximum_fusion.2), channel_id=1, source_target_pairs={{0,2},{1,3},{2,0},{3,1},{4,6},{5,7},{6,4},{7,5},{8,10},{9,11},{10,... | collective-permute-start | bytes 786440 | tf_op jit(solution)/shard_map/ppermute | solution.py:159
  3.2 0.0 copy-done.2
  3.2 0.0 copy-start
  3.2 0.0 copy-start.1
  3.2 1.3 %collective-permute-start = (f32[2,128,128]{2,1,0:T(8,128)S(1)}, f32[2,128,128]{2,1,0:T(8,128)S(1)}, u32[]{:S(2)}, u32[]{:S(2)}) collective-permute-start(f32[2,128,128]{2,1,0:T(8,128)S(1)} %bitcast.12), channel_id=1, source_target_pairs={{0,8},{4,12},{8,0},{12,4},{16,24},{20,28},{24,16},{28,20},{1,9},{5... | collective-permute-start | bytes 393224 | tf_op jit(solution)/shard_map/ppermute | solution.py:180
  4.5 1.2 %collective-permute-start.1 = (f32[2,128,128]{2,1,0:T(8,128)S(1)}, f32[2,128,128]{2,1,0:T(8,128)S(1)}, u32[]{:S(2)}, u32[]{:S(2)}) collective-permute-start(f32[2,128,128]{2,1,0:T(8,128)S(1)} %bitcast.13), channel_id=1, source_target_pairs={{0,4},{4,0},{8,16},{12,20},{16,8},{20,12},{24,28},{28,24},{1,5},{5... | collective-permute-start | bytes 393224 | tf_op jit(solution)/shard_map/ppermute | solution.py:181
  5.7 1.6 %collective-permute-done.other_a = f32[2,128,128]{2,1,0:T(8,128)S(1)} collective-permute-done((f32[2,128,128]{2,1,0:T(8,128)S(1)}, f32[2,128,128]{2,1,0:T(8,128)S(1)}, u32[]{:S(2)}, u32[]{:S(2)}) %collective-permute-start) | collective-permute-done | bytes 131104 | tf_op jit(solution)/shard_map/ppermute | solution.py:180
  7.3 1.3 %collective-permute-done.1.other_b = f32[2,128,128]{2,1,0:T(8,128)S(1)} collective-permute-done((f32[2,128,128]{2,1,0:T(8,128)S(1)}, f32[2,128,128]{2,1,0:T(8,128)S(1)}, u32[]{:S(2)}, u32[]{:S(2)}) %collective-permute-start.1) | collective-permute-done | bytes 131104 | tf_op jit(solution)/shard_map/ppermute | solution.py:181
  8.6 0.0 copy-done.3
  8.6 0.0 copy-done.4
  8.6 0.6 %shard_map.73 = (f32[2,128,128]{2,1,0:T(8,128)S(1)}, f32[2,128,128]{2,1,0:T(8,128)S(1)}) custom-call(s32[8]{0:T(128)S(1)} %copy-done.3, f32[8]{0:T(128)S(1)} %copy-done.4, f32[2,128,128]{2,1,0:T(8,128)S(1)} %bitcast.14, f32[2,128,128]{2,1,0:T(8,128)S(1)} %collective-permute-done.other_a, f32[2,128,128]{2,1,0:T(8,128)S(1)} %collective-permute-done.1.other_b), custom_call_target="tpu_custom_call" | custom-call | bytes 393280 | tf_op jit(solution)/shard_map/pallas_call | solution.py:144
  9.3 1.3 %collective-permute-start.2 = (f32[2,128,128]{2,1,0:T(8,128)S(1)}, f32[2,128,128]{2,1,0:T(8,128)S(1)}, u32[]{:S(2)}, u32[]{:S(2)}) collective-permute-start(f32[2,128,128]{2,1,0:T(8,128)S(1)} %get-tuple-element.10), channel_id=1, source_target_pairs={{0,4},{4,0},{8,12},{12,8},{16,20},{20,16},{24,28},{28,24},{1,5},{5... | collective-permute-start | bytes 393224 | tf_op jit(solution)/shard_map/ppermute | solution.py:195
  10.5 0.2 collective-permute-start.3
  10.8 1.2 %collective-permute-start.4 = (f32[2,128,128]{2,1,0:T(8,128)S(1)}, f32[2,128,128]{2,1,0:T(8,128)S(1)}, u32[]{:S(2)}, u32[]{:S(2)}) collective-permute-start(f32[2,128,128]{2,1,0:T(8,128)S(1)} %get-tuple-element.10), channel_id=1, source_target_pairs={{0,6},{1,7},{2,4},{3,5},{4,2},{5,3},{6,0},{7,1},{8,14},{9,15},{10,... | collective-permute-start | bytes 393224 | tf_op jit(solution)/shard_map/ppermute | solution.py:194
  12.0 0.0 collective-permute-done.6
  12.0 0.0 copy-done
  12.0 0.0 copy-done.1
  12.0 3.0 %collective-permute-start.7 = (f32[8,128,128]{2,1,0:T(8,128)S(1)}, f32[8,128,128]{2,1,0:T(8,128)S(1)}, u32[]{:S(2)}, u32[]{:S(2)}) collective-permute-start(f32[8,128,128]{2,1,0:T(8,128)S(1)} %pad_maximum_fusion), channel_id=1, source_target_pairs={{0,1},{1,0},{2,3},{3,2},{4,5},{5,4},{6,7},{7,6},{8,9},{9,8},{10,11... | collective-permute-start | bytes 1572872 | tf_op jit(solution)/shard_map/ppermute | solution.py:159
  15.0 0.0 collective-permute-done.2
  15.1 0.0 collective-permute-done.3
  15.1 1.6 %collective-permute-done.4 = f32[2,128,128]{2,1,0:T(8,128)S(1)} collective-permute-done((f32[2,128,128]{2,1,0:T(8,128)S(1)}, f32[2,128,128]{2,1,0:T(8,128)S(1)}, u32[]{:S(2)}, u32[]{:S(2)}) %collective-permute-start.4) | collective-permute-done | bytes 131104 | tf_op jit(solution)/shard_map/ppermute | solution.py:194
  16.8 3.1 %collective-permute-start.5 = (f32[4,128,128]{2,1,0:T(8,128)S(1)}, f32[4,128,128]{2,1,0:T(8,128)S(1)}, u32[]{:S(2)}, u32[]{:S(2)}) collective-permute-start(f32[4,128,128]{2,1,0:T(8,128)S(1)} %pad_maximum_fusion.1), channel_id=1, source_target_pairs={{0,1},{1,0},{2,3},{3,2},{4,5},{5,4},{6,7},{7,6},{8,9},{9,8},{10,11... | collective-permute-start | bytes 786440 | tf_op jit(solution)/shard_map/ppermute | solution.py:159
  19.9 1.1 %collective-permute-done.5 = f32[4,128,128]{2,1,0:T(8,128)S(1)} collective-permute-done((f32[4,128,128]{2,1,0:T(8,128)S(1)}, f32[4,128,128]{2,1,0:T(8,128)S(1)}, u32[]{:S(2)}, u32[]{:S(2)}) %collective-permute-start.5) | collective-permute-done | bytes 262176 | tf_op jit(solution)/shard_map/ppermute | solution.py:159
  21.1 0.0 copy-start.5
  21.1 0.0 collective-permute-done.7
  21.1 0.0 copy-start.6
  21.1 1.0 %copy-done.5 = f32[4,2,128,128]{3,2,1,0:T(8,128)S(1)} copy-done((f32[4,2,128,128]{3,2,1,0:T(8,128)S(1)}, f32[4,2,128,128]{3,2,1,0:T(8,128)}, u32[]{:S(2)}) %copy-start.5) | copy-done | bytes 524312
  22.1 0.0 copy-done.6
  22.1 2.5 %shard_map.74 = (bf16[4,384,256]{2,1,0:T(8,128)(2,1)S(1)}, bf16[4,384,256]{2,1,0:T(8,128)(2,1)S(1)}) custom-call(s32[4]{0:T(128)S(1)} %copy-done.6, f32[4,2,128,128]{3,2,1,0:T(8,128)S(1)} %copy-done.5, f32[2,128,128]{2,1,0:T(8,128)S(1)} %bitcast.8, f32[2,128,128]{2,1,0:T(8,128)S(1)} %get-tuple-element.16.refs_1_, ...), custom_call_target="tpu_custom_call" | custom-call | flops 1000000000 | bytes 1572880 | tf_op jit(solution)/shard_map/pallas_call | solution.py:144
  24.6 1.6 %shard_map.75.refs_4_ = f32[2,128,128]{2,1,0:T(8,128)S(1)} custom-call(f32[2,128,128]{2,1,0:T(8,128)S(1)} %add.6.refs_0_, f32[2,128,128]{2,1,0:T(8,128)S(1)} %add.7.refs_1_, bf16[4,384,256]{2,1,0:T(8,128)(2,1)S(1)} %get-tuple-element.11.refs_2_, bf16[4,384,256]{2,1,0:T(8,128)(2,1)S(1)} %get-tuple-element.12.refs_3_), custom_call_target="tpu_custom_call" | custom-call | flops 1000000000 | bytes 1835008 | tf_op jit(solution)/shard_map/pallas_call | solution.py:144
  26.2 2.2 %shard_map.76 = f32[2,128,128]{2,1,0:T(8,128)} custom-call(f32[2,128,128]{2,1,0:T(8,128)S(1)} %get-tuple-element.20.refs_0_, f32[2,128,128]{2,1,0:T(8,128)S(1)} %get-tuple-element.19.refs_1_, bf16[4,384,256]{2,1,0:T(8,128)(2,1)S(1)} %get-tuple-element.11.refs_2_, bf16[4,384,256]{2,1,0:T(8,128)(2,1)S(1)} %get-tuple-element.12.refs_3_, ...), custom_call_target="tpu_custom_call" | custom-call | flops 1000000000 | bytes 1966080 | tf_op jit(solution)/shard_map/pallas_call | solution.py:144
  (7 shorter events, 0.2 us)
Async XLA Ops:
  0.0 3.2 %copy-start.2 = (f32[2,1,1,128,128]{4,3,2,1,0:T(8,128)S(1)}, f32[2,1,1,128,128]{4,3,2,1,0:T(8,128)}, u32[]{:S(2)}) copy-start(f32[2,1,1,128,128]{4,3,2,1,0:T(8,128)} %param.7) | copy-start | bytes 393220
  1.0 7.6 %copy-start.3 = (s32[8]{0:T(128)S(1)}, s32[8]{0:T(128)}, u32[]{:S(2)}) copy-start(s32[8]{0:T(128)} %offsets.1) | copy-start | bytes 100
  1.0 7.6 %copy-start.4 = (f32[8]{0:T(128)S(1)}, f32[8]{0:T(128)}, u32[]{:S(2)}) copy-start(f32[8]{0:T(128)} %weights.1) | copy-start | bytes 100
  1.1 10.9 %collective-permute-start.6 = (f32[4,128,128]{2,1,0:T(8,128)S(1)}, f32[4,128,128]{2,1,0:T(8,128)S(1)}, u32[]{:S(2)}, u32[]{:S(2)}) collective-permute-start(f32[4,128,128]{2,1,0:T(8,128)S(1)} %pad_maximum_fusion.2), channel_id=1, source_target_pairs={{0,2},{1,3},{2,0},{3,1},{4,6},{5,7},{6,4},{7,5},{8,10},{9,11},{10,... | collective-permute-start | bytes 786440 | tf_op jit(solution)/shard_map/ppermute | solution.py:159
  3.2 8.8 %copy-start = (f32[2,1,1,128,128]{4,3,2,1,0:T(8,128)S(1)}, f32[2,1,1,128,128]{4,3,2,1,0:T(8,128)}, u32[]{:S(2)}) copy-start(f32[2,1,1,128,128]{4,3,2,1,0:T(8,128)} %param.8) | copy-start | bytes 393220
  3.2 8.8 %copy-start.1 = (f32[2,1,128,128]{3,2,1,0:T(8,128)S(1)}, f32[2,1,128,128]{3,2,1,0:T(8,128)}, u32[]{:S(2)}) copy-start(f32[2,1,128,128]{3,2,1,0:T(8,128)} %param.9) | copy-start | bytes 393220
  3.2 4.1 %collective-permute-start = (f32[2,128,128]{2,1,0:T(8,128)S(1)}, f32[2,128,128]{2,1,0:T(8,128)S(1)}, u32[]{:S(2)}, u32[]{:S(2)}) collective-permute-start(f32[2,128,128]{2,1,0:T(8,128)S(1)} %bitcast.12), channel_id=1, source_target_pairs={{0,8},{4,12},{8,0},{12,4},{16,24},{20,28},{24,16},{28,20},{1,9},{5... | collective-permute-start | bytes 393224 | tf_op jit(solution)/shard_map/ppermute | solution.py:180
  4.5 4.1 %collective-permute-start.1 = (f32[2,128,128]{2,1,0:T(8,128)S(1)}, f32[2,128,128]{2,1,0:T(8,128)S(1)}, u32[]{:S(2)}, u32[]{:S(2)}) collective-permute-start(f32[2,128,128]{2,1,0:T(8,128)S(1)} %bitcast.13), channel_id=1, source_target_pairs={{0,4},{4,0},{8,16},{12,20},{16,8},{20,12},{24,28},{28,24},{1,5},{5... | collective-permute-start | bytes 393224 | tf_op jit(solution)/shard_map/ppermute | solution.py:181
  9.3 5.8 %collective-permute-start.2 = (f32[2,128,128]{2,1,0:T(8,128)S(1)}, f32[2,128,128]{2,1,0:T(8,128)S(1)}, u32[]{:S(2)}, u32[]{:S(2)}) collective-permute-start(f32[2,128,128]{2,1,0:T(8,128)S(1)} %get-tuple-element.10), channel_id=1, source_target_pairs={{0,4},{4,0},{8,12},{12,8},{16,20},{20,16},{24,28},{28,24},{1,5},{5... | collective-permute-start | bytes 393224 | tf_op jit(solution)/shard_map/ppermute | solution.py:195
  10.5 4.5 %collective-permute-start.3 = (f32[2,128,128]{2,1,0:T(8,128)S(1)}, f32[2,128,128]{2,1,0:T(8,128)S(1)}, u32[]{:S(2)}, u32[]{:S(2)}) collective-permute-start(f32[2,128,128]{2,1,0:T(8,128)S(1)} %get-tuple-element.9), channel_id=1, source_target_pairs={{0,2},{1,3},{2,0},{3,1},{4,6},{5,7},{6,4},{7,5},{8,10},{9,11},{10,... | collective-permute-start | bytes 393224 | tf_op jit(solution)/shard_map/ppermute | solution.py:159
  10.8 6.0 %collective-permute-start.4 = (f32[2,128,128]{2,1,0:T(8,128)S(1)}, f32[2,128,128]{2,1,0:T(8,128)S(1)}, u32[]{:S(2)}, u32[]{:S(2)}) collective-permute-start(f32[2,128,128]{2,1,0:T(8,128)S(1)} %get-tuple-element.10), channel_id=1, source_target_pairs={{0,6},{1,7},{2,4},{3,5},{4,2},{5,3},{6,0},{7,1},{8,14},{9,15},{10,... | collective-permute-start | bytes 393224 | tf_op jit(solution)/shard_map/ppermute | solution.py:194
  12.0 9.0 %collective-permute-start.7 = (f32[8,128,128]{2,1,0:T(8,128)S(1)}, f32[8,128,128]{2,1,0:T(8,128)S(1)}, u32[]{:S(2)}, u32[]{:S(2)}) collective-permute-start(f32[8,128,128]{2,1,0:T(8,128)S(1)} %pad_maximum_fusion), channel_id=1, source_target_pairs={{0,1},{1,0},{2,3},{3,2},{4,5},{5,4},{6,7},{7,6},{8,9},{9,8},{10,11... | collective-permute-start | bytes 1572872 | tf_op jit(solution)/shard_map/ppermute | solution.py:159
  16.8 4.3 %collective-permute-start.5 = (f32[4,128,128]{2,1,0:T(8,128)S(1)}, f32[4,128,128]{2,1,0:T(8,128)S(1)}, u32[]{:S(2)}, u32[]{:S(2)}) collective-permute-start(f32[4,128,128]{2,1,0:T(8,128)S(1)} %pad_maximum_fusion.1), channel_id=1, source_target_pairs={{0,1},{1,0},{2,3},{3,2},{4,5},{5,4},{6,7},{7,6},{8,9},{9,8},{10,11... | collective-permute-start | bytes 786440 | tf_op jit(solution)/shard_map/ppermute | solution.py:159
  21.1 1.0 %copy-start.5 = (f32[4,2,128,128]{3,2,1,0:T(8,128)S(1)}, f32[4,2,128,128]{3,2,1,0:T(8,128)}, u32[]{:S(2)}) copy-start(f32[4,2,128,128]{3,2,1,0:T(8,128)} %table.1) | copy-start | bytes 1572868
  21.1 1.0 %copy-start.6 = (s32[4]{0:T(128)S(1)}, s32[4]{0:T(128)}, u32[]{:S(2)}) copy-start(s32[4]{0:T(128)} %material.1) | copy-start | bytes 52

commit v2 on v1

v2 whole, which is shorter than its diff:
```python
import functools

import jax
import jax.numpy as jnp
from jax import lax
from jax.experimental import pallas as pl
from jax.experimental.pallas import tpu as pltpu
from jax.sharding import PartitionSpec as P

F32 = jnp.float32
BF16 = jnp.bfloat16
VMEM = pl.BlockSpec(memory_space=pltpu.VMEM)
SMEM = pl.BlockSpec(memory_space=pltpu.SMEM)
NN = (((1,), (0,)), ((), ()))
NT = (((1,), (1,)), ((), ()))


def split(value):
    high = value.astype(BF16)
    return high, (value - high.astype(F32)).astype(BF16)


def rows(block):
    return jnp.concatenate([block[0], block[1]], axis=1)


def block_of(row):
    half = row.shape[1] // 2
    return jnp.stack([row[:, :half], row[:, half:]])


def full(row):
    half = row.shape[1] // 2
    turned = jnp.concatenate([-row[:, half:], row[:, :half]], axis=1)
    return jnp.concatenate([row, turned], axis=0)


def product(left, right, dims):
    def dot(a, b):
        return lax.dot_general(a, b, dims, preferred_element_type=F32)

    return dot(left[0], right[0]) + (dot(left[0], right[1]) + dot(left[1], right[0]))


def times(left, right_block):
    return product(left, [full(part) for part in split(rows(right_block))], NN)


def times_dagger(left, right_block):
    return product(left, [full(part) for part in split(rows(right_block))], NT)


def share_kernel(group, offsets, weights, out):
    count = lax.axis_size("energy")
    mine = lax.axis_index("energy")
    place, rank = mine // group, mine % group
    source_a, source_b, has_a, has_b = partners(place, count // group, mine, group)

    def coefficient(target, source, valid):
        total = jnp.float32(0)
        for mode in range(offsets.shape[0]):
            total += jnp.where(target + offsets[mode] == source, weights[mode], jnp.float32(0))
        return jnp.where(valid, total, jnp.float32(0))

    for step in range(group):
        target = place * group + (rank + step) % group
        for index, (source, valid) in enumerate(((mine, True), (source_a, has_a), (source_b, has_b))):
            out[step, index] = jnp.full(out.shape[2:], coefficient(target, source, valid), F32)


def smear_kernel(group, shares, own, other_a, other_b, *outs):
    shape = (-1,) + shares.shape[2:]
    parts = [part[...].reshape(shape) for part in (own, other_a, other_b)]
    for step in range(group):
        total = sum(shares[step, index][None] * part for index, part in enumerate(parts))
        outs[step][...] = total.reshape(outs[step].shape)


def partners(place, places, mine, group):
    even = place % 2 == 0
    side_a = jnp.where(even, 1, -1)
    has_a = (place + side_a < places) & (place + side_a >= 0)
    has_b = (place - side_a < places) & (place - side_a >= 0)
    return mine + side_a * group, mine - side_a * group, has_a, has_b


def matchings(places, group):
    result = []
    for first in (0, 1):
        pairs = []
        for place in range(places):
            other = place + 1 if place % 2 == first else place - 1
            for rank in range(group):
                mine = place * group + rank
                if 0 <= other < places:
                    pairs.append((mine, other * group + rank))
                elif group % 2 == 0:
                    pairs.append((mine, mine ^ 1))
        result.append(pairs)
    return result


def pair_kernel(own, other, out):
    odd = lax.axis_index("space") % 2 == 1
    mine, theirs = own[...], other[...]
    first, second = jnp.where(odd, theirs, mine), jnp.where(odd, mine, theirs)
    out[0:2] = block_of(times(split(times(split(rows(second[:2])), second[2:])), first[:2]))
    out[2:4] = second[:2]
    if out.shape[0] > 4:
        out[4:6] = first[2:]


def valid_terms(slab, mine, count):
    return slab <= mine, (slab >= 1) & (slab <= mine + 1), slab < mine


def factor_kernel(count, material, table, own, other, *refs):
    pairs = refs[: count // 2]
    outs, token, held, base = refs[count // 2 : count // 2 + 2], *refs[count // 2 + 2 :]
    mine = lax.axis_index("space")
    size = table.shape[-1]
    for slot in range(1, count // 2):
        held[slot - 1] = pairs[slot][...]
    token[...] = jnp.zeros_like(token)

    def store(slab, which, parts):
        valid = valid_terms(slab, mine, count)
        position = sum((v.astype(jnp.int32) for v in valid[:which]), jnp.int32(0))

        @pl.when(valid[which] & (slab >= 0) & (slab < count))
        def _():
            for out, part in zip(outs, parts):
                out[jnp.bitwise_xor(mine, slab), pl.ds(pl.multiple_of(position * size, size), size)] = part

    def spread(slabs, maps):
        made = []
        for slab, whole in zip(slabs, maps):
            parts = split(whole)
            right = times(parts, table[material[slab]])
            left = times_dagger(parts, table[material[jnp.maximum(slab - 1, 0)]])
            made.append((parts, split(right), split(left)))
        for slab, (same, right, left) in zip(slabs, made):
            store(slab, 0, same)
            store(slab + 1, 1, right)
            store(slab - 1, 2, left)

    odd = mine % 2 == 1

    @pl.when(odd)
    def _():
        spread([mine, mine - 1], [rows(own[:2]), rows(pairs[0][:2])])

    @pl.when(jnp.logical_not(odd))
    def _():
        spread([mine], [rows(own[:2])])

    @pl.when(mine >= 2)
    def _():
        start = split(jnp.where(odd, rows(pairs[0][:2]), rows(own[:2])))
        base[...] = times(start, jnp.where(odd, other[2:], own[2:]))

    def earlier(step, _):
        pair = mine // 2 - step
        block = held.at[jnp.bitwise_xor(mine // 2, pair) - 1]
        parts = split(base[...])
        near, far = times(parts, block[2:4]), times(parts, block[0:2])
        spread([2 * pair + 1, 2 * pair], [near, far])
        if held.shape[1] > 4:
            base[...] = times(split(far), block[4:6])
        return _

    lax.fori_loop(1, mine // 2 + 1, earlier, 0)


def add_kernel(left, right, after, out):
    out[...] = left[...] + right[...]


def field_kernel(count, slot, has_state, field, high, low, *rest):
    out = rest[-1]
    size = out.shape[-1]
    mine = lax.axis_index("space")
    valid = valid_terms(jnp.bitwise_xor(mine, slot), mine, count)
    present = sum(v.astype(jnp.int32) for v in valid)

    def run(terms):
        total = rows(rest[0]) if has_state else jnp.zeros((size, 2 * size), F32)
        if terms:
            factors = [part[slot, : terms * size] for part in (high, low)]
            left = split(times(factors, field))
            for term in range(terms):
                here = slice(term * size, (term + 1) * size)
                total = total + product([p[here] for p in left], [full(f[here]) for f in factors], NT)
        out[...] = block_of(total)

    for terms in range(4):
        pl.when(present == terms)(functools.partial(run, terms))


def call(kernel, shapes, specs, *args, scratch=()):
    return pl.pallas_call(
        kernel,
        out_shape=shapes,
        in_specs=specs,
        out_specs=jax.tree.map(lambda _: VMEM, shapes),
        scratch_shapes=scratch,
        compiler_params=pltpu.CompilerParams(vmem_limit_bytes=32 * 2**20),
        cost_estimate=pl.CostEstimate(
            flops=10**9, bytes_accessed=sum(a.size * a.dtype.itemsize for a in args), transcendentals=0
        ),
    )(*args)


def exchange(value, bit):
    count = lax.axis_size("space")
    return lax.ppermute(value, "space", [(i, i ^ bit) for i in range(count)])


def gather(slots, bits):
    for bit in bits:
        slots = slots | {key ^ bit: exchange(block, bit) for key, block in slots.items()}
    return slots


def per_device(lesser_prev, retarded, coupling, gradient_table, material, offsets, weights):
    size = lesser_prev.shape[-1]
    energies, slabs = lax.axis_size("energy"), lax.axis_size("space")
    group = max(energies // 4, 1)
    block = jax.ShapeDtypeStruct((2, size, size), F32)
    own = lesser_prev.reshape(2, size, size)
    chip_bits = [1 << b for b in range(1, slabs.bit_length() - 1)]

    pairs_a, pairs_b = matchings(energies // group, group)
    other_a = lax.ppermute(own, "energy", pairs_a)
    other_b = lax.ppermute(own, "energy", pairs_b)
    packed = jnp.concatenate([retarded.reshape(2, size, size), coupling.reshape(2, size, size)], axis=0)
    packed_other = exchange(packed, 1)
    kept = 4 if slabs <= 4 else 6
    pair = call(pair_kernel, jax.ShapeDtypeStruct((kept, size, size), F32), [VMEM] * 2, packed, packed_other)
    pairs = gather({0: pair}, chip_bits)
    factor_shape = jax.ShapeDtypeStruct((slabs, 3 * size, 2 * size), BF16)
    *factors, token = call(
        functools.partial(factor_kernel, slabs), [factor_shape] * 2 + [jax.ShapeDtypeStruct((8, 128), F32)],
        [SMEM] + [VMEM] * (3 + slabs // 2),
        material, gradient_table, packed, packed_other, *[pairs[2 * p] for p in range(slabs // 2)],
        scratch=[pltpu.VMEM((max(slabs // 2 - 1, 1), kept, size, size), F32), pltpu.VMEM((size, 2 * size), F32)],
    )

    shares = call(
        functools.partial(share_kernel, group), jax.ShapeDtypeStruct((group, 3, 8, 128), F32), [SMEM, SMEM],
        offsets, weights,
    )
    sums = call(functools.partial(smear_kernel, group), [block] * group, [VMEM] * 4, shares, own, other_a, other_b)

    def propagate(state, slot, field):
        kernel = functools.partial(field_kernel, slabs, slot, bool(state))
        return (call(kernel, block, [VMEM] * (3 + len(state)), field, *factors, *state),)

    if group == 2 and len(chip_bits) == 1:
        bit = chip_bits[0]
        both = [
            (e * slabs + s, (e ^ 1) * slabs + (s ^ bit)) for e in range(energies) for s in range(slabs)
        ]
        near = lax.ppermute(sums[1], "energy", [(e, e ^ 1) for e in range(energies)])
        across = exchange(sums[0], bit)
        far = lax.ppermute(sums[1], ("energy", "space"), both)
        fields = {0: call(add_kernel, block, [VMEM] * 3, sums[0], near, token)}
        fields[1] = exchange(fields[0], 1)
        state = propagate((), 0, fields[0])
        fields[bit] = call(add_kernel, block, [VMEM] * 3, across, far, state[0])
        fields[bit ^ 1] = exchange(fields[bit], 1)
        rest = [1, bit, bit ^ 1]
    else:
        field = sums[0]
        for step in range(1, group):
            pairs = [(e, e - e % group + (e + step) % group) for e in range(energies)]
            field = field + lax.ppermute(sums[step], "energy", pairs)
        fields = gather({0: field}, chip_bits + [1])
        state, rest = (), sorted(fields)
    for slot in rest:
        state = propagate(state, slot, fields[slot])
    return state[0].reshape(lesser_prev.shape)


def solution(mesh):
    placed = (
        P(None, "energy", "space", None, None),
        P(None, "energy", "space", None, None),
        P(None, "space", None, None),
        P(),
        P(),
        P(),
        P(),
    )
    return jax.shard_map(
        per_device,
        mesh=mesh,
        in_specs=placed,
        out_specs=P(None, "energy", "space", None, None),
        check_vma=False,
    )
```

time: 28.9 us -> 23 us (0.80)
  waiting for transfers between devices: 5.73 us -> 2.8 us
  Pallas kernels: 6.92 us -> 4.85 us
  local copies, waits for them, and re-layouts: 1.07 us -> 0.02 us
  starting transfers between devices: 13.4 us -> 13.9 us
    pallas_call x4 -> x10, Pallas kernels: 6.92 us -> 4.85 us  [call(): pl.pallas_call(kernel, out_shape=shapes, in_specs=specs, out_specs=jax.tr...]
    ppermute x1, waiting for transfers between devices: 1.65 us -> 0.01 us  [per_device(): far = lax.ppermute(sums[1], ('energy', 'space'), both)]
    ppermute x1, waiting for transfers between devices: 1.6 us -> 0.11 us  [per_device(): other_a = lax.ppermute(own, 'energy', pairs_a)]
    ppermute x1, starting transfers between devices: 1.3 us -> 2.77 us  [per_device(): other_a = lax.ppermute(own, 'energy', pairs_a)]
    ppermute x1, waiting for transfers between devices: 1.3 us -> 2.42 us  [per_device(): other_b = lax.ppermute(own, 'energy', pairs_b)]
    ppermute x1, starting transfers between devices: 1.21 us -> 0.2 us  [per_device(): far = lax.ppermute(sums[1], ('energy', 'space'), both)]
    unnamed x14 -> x10, local copies, waits for them, and re-layouts: 1 us -> 0.02 us
    ppermute x4 -> x5, waiting for transfers between devices: 1.18 us -> 0.26 us  [exchange(): return lax.ppermute(value, 'space', [(i, i ^ bit) for i in range(count)])]
  transfers between devices with their start and end apart: 8 -> 9, of which waited for: 4 -> 3; matrix products, arithmetic and copies ran while one was open for 0% -> 0% of each run, Pallas kernels for 2% -> 16%
where the time goes in v2:
time: 23 us; the launch traced here: 22.8 us
  starting transfers between devices  13.9 us (60%)
  Pallas kernels  4.85 us (21%)
  waiting for transfers between devices  2.8 us (12%)
  other arithmetic  1.02 us (4%)
    ppermute x5, starting transfers between devices, exchange(): return lax.ppermute(value, 'space', [(i, i ^ bit) for i in range(count)])  8.49 us
    pallas_call x10, Pallas kernels, call(): pl.pallas_call(kernel, out_shape=shapes, in_specs=specs, out_specs=jax.tr...  4.85 us
    ppermute x1, starting transfers between devices, per_device(): other_a = lax.ppermute(own, 'energy', pairs_a)  2.77 us
    ppermute x1, waiting for transfers between devices, per_device(): other_b = lax.ppermute(own, 'energy', pairs_b)  2.42 us
    ppermute x1, starting transfers between devices, per_device(): lax.ppermute(sums[1], 'energy', [(e, e ^ 1) for e in range(energies)])  1.28 us
    ppermute x1, starting transfers between devices, per_device(): other_b = lax.ppermute(own, 'energy', pairs_b)  1.21 us
    concatenate x1, other arithmetic, per_device(): jnp.concatenate([retarded.reshape(2, size, size), coupling.reshape(2, siz...  1.02 us
  transfers between devices with their start and end apart: 9, of which 3 were waited for; matrix products, arithmetic and copies ran while one was open for 0% of the time, Pallas kernels for 16%

profile of v2, /device:TPU:1, one launch (start us, length us, event | category | flops | bytes accessed | tf_op | source)
XLA Modules:
  0.0 22.8 jit_solution(10556823057004555222)
XLA Ops:
  0.0 0.0 copy-start.1
  0.0 1.0 %pad_maximum_fusion.own = f32[4,128,128]{2,1,0:T(8,128)S(1)} fusion(f32[2,128,128]{2,1,0:T(8,128)} %bitcast.9, f32[2,128,128]{2,1,0:T(8,128)} %bitcast.10), kind=kLoop, calls=%fused_computation | loop fusion | flops 65536 | bytes 524288 | tf_op jit(solution)/shard_map/concatenate | solution.py:236
  1.0 0.1 collective-permute-start.5
  1.2 0.0 copy-done.1
  1.2 0.0 copy-start.2
  1.2 0.0 copy-start.3
  1.2 2.8 %collective-permute-start = (f32[2,128,128]{2,1,0:T(8,128)S(1)}, f32[2,128,128]{2,1,0:T(8,128)S(1)}, u32[]{:S(2)}, u32[]{:S(2)}) collective-permute-start(f32[2,128,128]{2,1,0:T(8,128)S(1)} %bitcast.6), channel_id=1, source_target_pairs={{0,8},{4,12},{8,0},{12,4},{16,24},{20,28},{24,16},{28,20},{1,9},{5... | collective-permute-start | bytes 393224 | tf_op jit(solution)/shard_map/ppermute | solution.py:234
  3.9 0.0 collective-permute-done.5.other
  3.9 0.4 %shard_map.75.refs_0_ = f32[4,128,128]{2,1,0:T(8,128)S(1)} custom-call(f32[4,128,128]{2,1,0:T(8,128)S(1)} %pad_maximum_fusion.own, f32[4,128,128]{2,1,0:T(8,128)S(1)} %collective-permute-done.5.other), custom_call_target="tpu_custom_call" | custom-call | flops 1000000000 | bytes 524288 | tf_op jit(solution)/shard_map/pallas_call | solution.py:201
  4.4 1.3 %collective-permute-start.6 = (f32[4,128,128]{2,1,0:T(8,128)S(1)}, f32[4,128,128]{2,1,0:T(8,128)S(1)}, u32[]{:S(2)}, u32[]{:S(2)}) collective-permute-start(f32[4,128,128]{2,1,0:T(8,128)S(1)} %shard_map.75.refs_0_), channel_id=1, source_target_pairs={{0,2},{1,3},{2,0},{3,1},{4,6},{5,7},{6,4},{7,5},{8,10},{9,11},{10,... | collective-permute-start | bytes 786440 | tf_op jit(solution)/shard_map/ppermute | solution.py:216
  5.7 1.2 %collective-permute-start.1 = (f32[2,128,128]{2,1,0:T(8,128)S(1)}, f32[2,128,128]{2,1,0:T(8,128)S(1)}, u32[]{:S(2)}, u32[]{:S(2)}) collective-permute-start(f32[2,128,128]{2,1,0:T(8,128)S(1)} %bitcast.7), channel_id=1, source_target_pairs={{0,4},{4,0},{8,16},{12,20},{16,8},{20,12},{24,28},{28,24},{1,5},{5... | collective-permute-start | bytes 393224 | tf_op jit(solution)/shard_map/ppermute | solution.py:235
  6.9 0.0 copy-done.2
  6.9 0.0 copy-done.3
  6.9 0.6 %shard_map.73.shares = f32[2,3,8,128]{3,2,1,0:T(8,128)S(1)} custom-call(s32[8]{0:T(128)S(1)} %copy-done.2, f32[8]{0:T(128)S(1)} %copy-done.3), custom_call_target="tpu_custom_call" | custom-call | flops 1000000000 | bytes 64 | tf_op jit(solution)/shard_map/pallas_call | solution.py:201
  7.5 0.0 copy-start
  7.6 0.1 collective-permute-done.other_a
  7.7 2.4 %collective-permute-done.1.other_b = f32[2,128,128]{2,1,0:T(8,128)S(1)} collective-permute-done((f32[2,128,128]{2,1,0:T(8,128)S(1)}, f32[2,128,128]{2,1,0:T(8,128)S(1)}, u32[]{:S(2)}, u32[]{:S(2)}) %collective-permute-start.1) | collective-permute-done | bytes 131104 | tf_op jit(solution)/shard_map/ppermute | solution.py:235
  10.1 0.1 shard_map.74
  10.2 0.0 copy-start.4
  10.2 1.3 %collective-permute-start.4 = (f32[2,128,128]{2,1,0:T(8,128)S(1)}, f32[2,128,128]{2,1,0:T(8,128)S(1)}, u32[]{:S(2)}, u32[]{:S(2)}) collective-permute-start(f32[2,128,128]{2,1,0:T(8,128)S(1)} %get-tuple-element.11), channel_id=1, source_target_pairs={{0,4},{4,0},{8,12},{12,8},{16,20},{20,16},{24,28},{28,24},{1,5},{5... | collective-permute-start | bytes 393224 | tf_op jit(solution)/shard_map/ppermute | solution.py:264
  11.4 0.2 collective-permute-start.3
  11.6 1.2 %collective-permute-start.2 = (f32[2,128,128]{2,1,0:T(8,128)S(1)}, f32[2,128,128]{2,1,0:T(8,128)S(1)}, u32[]{:S(2)}, u32[]{:S(2)}) collective-permute-start(f32[2,128,128]{2,1,0:T(8,128)S(1)} %get-tuple-element.10.left), channel_id=1, source_target_pairs={{0,2},{1,3},{2,0},{3,1},{4,6},{5,7},{6,4},{7,5},{8,10},{9,11},{10,... | collective-permute-start | bytes 393224 | tf_op jit(solution)/shard_map/ppermute | solution.py:216
  12.9 0.0 collective-permute-done.6.refs_1_
  12.9 0.0 copy-done
  12.9 0.0 copy-done.4
  12.9 1.2 %shard_map.76 = (bf16[4,384,256]{2,1,0:T(8,128)(2,1)S(1)}, bf16[4,384,256]{2,1,0:T(8,128)(2,1)S(1)}, f32[8,128]{1,0:T(8,128)S(1)}) custom-call(s32[4]{0:T(128)S(1)} %copy-done.4, f32[4,2,128,128]{3,2,1,0:T(8,128)S(1)} %copy-done, f32[4,128,128]{2,1,0:T(8,128)S(1)} %pad_maximum_fusion.own, f32[4,128,128]{2,1,0:T(8,128)S(1)} %collective-permute-done.5.other, ...), custom_call_target="tpu_custom_call" | custom-call | flops 1000000000 | bytes 1572880 | tf_op jit(solution)/shard_map/pallas_call | solution.py:201
  14.1 0.0 collective-permute-done.4.right
  14.1 3.5 %collective-permute-start.8 = (f32[2,128,128]{2,1,0:T(8,128)S(1)}, f32[2,128,128]{2,1,0:T(8,128)S(1)}, u32[]{:S(2)}, u32[]{:S(2)}) collective-permute-start(f32[2,128,128]{2,1,0:T(8,128)S(1)} %shard_map.77.field), channel_id=1, source_target_pairs={{0,1},{1,0},{2,3},{3,2},{4,5},{5,4},{6,7},{7,6},{8,9},{9,8},{10,11... | collective-permute-start | bytes 393224 | tf_op jit(solution)/shard_map/ppermute | solution.py:216
  17.6 0.7 %shard_map.78.after.rest_0_ = f32[2,128,128]{2,1,0:T(8,128)S(1)} custom-call(f32[2,128,128]{2,1,0:T(8,128)S(1)} %shard_map.77.field, bf16[4,384,256]{2,1,0:T(8,128)(2,1)S(1)} %get-tuple-element.13.high, bf16[4,384,256]{2,1,0:T(8,128)(2,1)S(1)} %get-tuple-element.14.low), custom_call_target="tpu_custom_call" | custom-call | flops 1000000000 | bytes 1703936 | tf_op jit(solution)/shard_map/pallas_call | solution.py:201
  18.3 0.0 collective-permute-done.2.left
  18.3 0.0 collective-permute-done.3.right
  18.4 2.3 %collective-permute-start.7 = (f32[2,128,128]{2,1,0:T(8,128)S(1)}, f32[2,128,128]{2,1,0:T(8,128)S(1)}, u32[]{:S(2)}, u32[]{:S(2)}) collective-permute-start(f32[2,128,128]{2,1,0:T(8,128)S(1)} %shard_map.79.field), channel_id=1, source_target_pairs={{0,1},{1,0},{2,3},{3,2},{4,5},{5,4},{6,7},{7,6},{8,9},{9,8},{10,11... | collective-permute-start | bytes 393224 | tf_op jit(solution)/shard_map/ppermute | solution.py:216
  20.7 0.0 collective-permute-done.8.field
  20.7 0.7 %shard_map.80.rest_0_ = f32[2,128,128]{2,1,0:T(8,128)S(1)} custom-call(f32[2,128,128]{2,1,0:T(8,128)S(1)} %collective-permute-done.8.field, bf16[4,384,256]{2,1,0:T(8,128)(2,1)S(1)} %get-tuple-element.13.high, bf16[4,384,256]{2,1,0:T(8,128)(2,1)S(1)} %get-tuple-element.14.low, f32[2,128,128]{2,1,0:T(8,128)S(1)} %shard_map.78.after.rest_0_), custom_call_target="tpu_custom_call" | custom-call | flops 1000000000 | bytes 1835008 | tf_op jit(solution)/shard_map/pallas_call | solution.py:201
  21.4 0.3 %collective-permute-done.7.field = f32[2,128,128]{2,1,0:T(8,128)S(1)} collective-permute-done((f32[2,128,128]{2,1,0:T(8,128)S(1)}, f32[2,128,128]{2,1,0:T(8,128)S(1)}, u32[]{:S(2)}, u32[]{:S(2)}) %collective-permute-start.7) | collective-permute-done | bytes 131104 | tf_op jit(solution)/shard_map/ppermute | solution.py:216
  21.6 1.1 %shard_map.82 = f32[2,128,128]{2,1,0:T(8,128)} custom-call(f32[2,128,128]{2,1,0:T(8,128)S(1)} %collective-permute-done.7.field, bf16[4,384,256]{2,1,0:T(8,128)(2,1)S(1)} %get-tuple-element.13.high, bf16[4,384,256]{2,1,0:T(8,128)(2,1)S(1)} %get-tuple-element.14.low, f32[2,128,128]{2,1,0:T(8,128)S(1)} %shard_map.81.rest_0_), custom_call_target="tpu_custom_call" | custom-call | flops 1000000000 | bytes 1835008 | tf_op jit(solution)/shard_map/pallas_call | solution.py:201
  (3 shorter events, 0.1 us)
Async XLA Ops:
  0.0 1.2 %copy-start.1 = (f32[2,1,1,128,128]{4,3,2,1,0:T(8,128)S(1)}, f32[2,1,1,128,128]{4,3,2,1,0:T(8,128)}, u32[]{:S(2)}) copy-start(f32[2,1,1,128,128]{4,3,2,1,0:T(8,128)} %param.7) | copy-start | bytes 393220
  1.0 2.9 %collective-permute-start.5 = (f32[4,128,128]{2,1,0:T(8,128)S(1)}, f32[4,128,128]{2,1,0:T(8,128)S(1)}, u32[]{:S(2)}, u32[]{:S(2)}) collective-permute-start(f32[4,128,128]{2,1,0:T(8,128)S(1)} %pad_maximum_fusion.own), channel_id=1, source_target_pairs={{0,1},{1,0},{2,3},{3,2},{4,5},{5,4},{6,7},{7,6},{8,9},{9,8},{10,11... | collective-permute-start | bytes 786440 | tf_op jit(solution)/shard_map/ppermute | solution.py:216
  1.2 5.7 %copy-start.2 = (s32[8]{0:T(128)S(1)}, s32[8]{0:T(128)}, u32[]{:S(2)}) copy-start(s32[8]{0:T(128)} %offsets.1) | copy-start | bytes 100
  1.2 5.7 %copy-start.3 = (f32[8]{0:T(128)S(1)}, f32[8]{0:T(128)}, u32[]{:S(2)}) copy-start(f32[8]{0:T(128)} %weights.1) | copy-start | bytes 100
  1.2 6.5 %collective-permute-start = (f32[2,128,128]{2,1,0:T(8,128)S(1)}, f32[2,128,128]{2,1,0:T(8,128)S(1)}, u32[]{:S(2)}, u32[]{:S(2)}) collective-permute-start(f32[2,128,128]{2,1,0:T(8,128)S(1)} %bitcast.6), channel_id=1, source_target_pairs={{0,8},{4,12},{8,0},{12,4},{16,24},{20,28},{24,16},{28,20},{1,9},{5... | collective-permute-start | bytes 393224 | tf_op jit(solution)/shard_map/ppermute | solution.py:234
  4.4 8.5 %collective-permute-start.6 = (f32[4,128,128]{2,1,0:T(8,128)S(1)}, f32[4,128,128]{2,1,0:T(8,128)S(1)}, u32[]{:S(2)}, u32[]{:S(2)}) collective-permute-start(f32[4,128,128]{2,1,0:T(8,128)S(1)} %shard_map.75.refs_0_), channel_id=1, source_target_pairs={{0,2},{1,3},{2,0},{3,1},{4,6},{5,7},{6,4},{7,5},{8,10},{9,11},{10,... | collective-permute-start | bytes 786440 | tf_op jit(solution)/shard_map/ppermute | solution.py:216
  5.7 4.4 %collective-permute-start.1 = (f32[2,128,128]{2,1,0:T(8,128)S(1)}, f32[2,128,128]{2,1,0:T(8,128)S(1)}, u32[]{:S(2)}, u32[]{:S(2)}) collective-permute-start(f32[2,128,128]{2,1,0:T(8,128)S(1)} %bitcast.7), channel_id=1, source_target_pairs={{0,4},{4,0},{8,16},{12,20},{16,8},{20,12},{24,28},{28,24},{1,5},{5... | collective-permute-start | bytes 393224 | tf_op jit(solution)/shard_map/ppermute | solution.py:235
  7.5 5.3 %copy-start = (f32[4,2,128,128]{3,2,1,0:T(8,128)S(1)}, f32[4,2,128,128]{3,2,1,0:T(8,128)}, u32[]{:S(2)}) copy-start(f32[4,2,128,128]{3,2,1,0:T(8,128)} %table.1) | copy-start | bytes 1572868
  10.2 2.7 %copy-start.4 = (s32[4]{0:T(128)S(1)}, s32[4]{0:T(128)}, u32[]{:S(2)}) copy-start(s32[4]{0:T(128)} %material.1) | copy-start | bytes 52
  10.2 3.9 %collective-permute-start.4 = (f32[2,128,128]{2,1,0:T(8,128)S(1)}, f32[2,128,128]{2,1,0:T(8,128)S(1)}, u32[]{:S(2)}, u32[]{:S(2)}) collective-permute-start(f32[2,128,128]{2,1,0:T(8,128)S(1)} %get-tuple-element.11), channel_id=1, source_target_pairs={{0,4},{4,0},{8,12},{12,8},{16,20},{20,16},{24,28},{28,24},{1,5},{5... | collective-permute-start | bytes 393224 | tf_op jit(solution)/shard_map/ppermute | solution.py:264
  11.4 6.9 %collective-permute-start.3 = (f32[2,128,128]{2,1,0:T(8,128)S(1)}, f32[2,128,128]{2,1,0:T(8,128)S(1)}, u32[]{:S(2)}, u32[]{:S(2)}) collective-permute-start(f32[2,128,128]{2,1,0:T(8,128)S(1)} %get-tuple-element.11), channel_id=1, source_target_pairs={{0,6},{1,7},{2,4},{3,5},{4,2},{5,3},{6,0},{7,1},{8,14},{9,15},{10,... | collective-permute-start | bytes 393224 | tf_op jit(solution)/shard_map/ppermute | solution.py:266
  11.6 6.7 %collective-permute-start.2 = (f32[2,128,128]{2,1,0:T(8,128)S(1)}, f32[2,128,128]{2,1,0:T(8,128)S(1)}, u32[]{:S(2)}, u32[]{:S(2)}) collective-permute-start(f32[2,128,128]{2,1,0:T(8,128)S(1)} %get-tuple-element.10.left), channel_id=1, source_target_pairs={{0,2},{1,3},{2,0},{3,1},{4,6},{5,7},{6,4},{7,5},{8,10},{9,11},{10,... | collective-permute-start | bytes 393224 | tf_op jit(solution)/shard_map/ppermute | solution.py:216
  14.1 6.6 %collective-permute-start.8 = (f32[2,128,128]{2,1,0:T(8,128)S(1)}, f32[2,128,128]{2,1,0:T(8,128)S(1)}, u32[]{:S(2)}, u32[]{:S(2)}) collective-permute-start(f32[2,128,128]{2,1,0:T(8,128)S(1)} %shard_map.77.field), channel_id=1, source_target_pairs={{0,1},{1,0},{2,3},{3,2},{4,5},{5,4},{6,7},{7,6},{8,9},{9,8},{10,11... | collective-permute-start | bytes 393224 | tf_op jit(solution)/shard_map/ppermute | solution.py:216
  18.4 3.3 %collective-permute-start.7 = (f32[2,128,128]{2,1,0:T(8,128)S(1)}, f32[2,128,128]{2,1,0:T(8,128)S(1)}, u32[]{:S(2)}, u32[]{:S(2)}) collective-permute-start(f32[2,128,128]{2,1,0:T(8,128)S(1)} %shard_map.79.field), channel_id=1, source_target_pairs={{0,1},{1,0},{2,3},{3,2},{4,5},{5,4},{6,7},{7,6},{8,9},{9,8},{10,11... | collective-permute-start | bytes 393224 | tf_op jit(solution)/shard_map/ppermute | solution.py:216

commit v3 on v2

--- a/solution.py
+++ b/solution.py
@@ -100,28 +100,27 @@
     return result
 
 
-def pair_kernel(own, other, out):
+def pair_kernel(own_r, own_c, other_r, other_c, combined, second_r, first_c):
     odd = lax.axis_index("space") % 2 == 1
-    mine, theirs = own[...], other[...]
-    first, second = jnp.where(odd, theirs, mine), jnp.where(odd, mine, theirs)
-    out[0:2] = block_of(times(split(times(split(rows(second[:2])), second[2:])), first[:2]))
-    out[2:4] = second[:2]
-    if out.shape[0] > 4:
-        out[4:6] = first[2:]
+    first_r = jnp.where(odd, other_r[...], own_r[...])
+    second_c = jnp.where(odd, own_c[...], other_c[...])
+    second_r[...] = jnp.where(odd, own_r[...], other_r[...])
+    first_c[...] = jnp.where(odd, other_c[...], own_c[...])
+    combined[...] = block_of(times(split(times(split(rows(second_r)), second_c)), first_r))
 
 
 def valid_terms(slab, mine, count):
     return slab <= mine, (slab >= 1) & (slab <= mine + 1), slab < mine
 
 
-def factor_kernel(count, material, table, own, other, *refs):
-    pairs = refs[: count // 2]
-    outs, token, held, base = refs[count // 2 : count // 2 + 2], *refs[count // 2 + 2 :]
+def factor_kernel(count, material, table, own_r, *refs):
+    combined, second_r, first_c = (refs[n * count // 2 : (n + 1) * count // 2] for n in range(3))
+    *outs, held, base = refs[3 * count // 2 :]
     mine = lax.axis_index("space")
     size = table.shape[-1]
     for slot in range(1, count // 2):
-        held[slot - 1] = pairs[slot][...]
-    token[...] = jnp.zeros_like(token)
+        for index, blocks in enumerate((combined, second_r, first_c)):
+            held[slot - 1, index] = blocks[slot][...]
 
     def store(slab, which, parts):
         valid = valid_terms(slab, mine, count)
@@ -148,44 +147,45 @@
 
     @pl.when(odd)
     def _():
-        spread([mine, mine - 1], [rows(own[:2]), rows(pairs[0][:2])])
+        spread([mine, mine - 1], [rows(own_r), rows(combined[0])])
 
     @pl.when(jnp.logical_not(odd))
     def _():
-        spread([mine], [rows(own[:2])])
+        spread([mine], [rows(own_r)])
 
     @pl.when(mine >= 2)
     def _():
-        start = split(jnp.where(odd, rows(pairs[0][:2]), rows(own[:2])))
-        base[...] = times(start, jnp.where(odd, other[2:], own[2:]))
+        start = split(jnp.where(odd, rows(combined[0]), rows(own_r)))
+        base[...] = times(start, first_c[0])
 
     def earlier(step, _):
         pair = mine // 2 - step
         block = held.at[jnp.bitwise_xor(mine // 2, pair) - 1]
         parts = split(base[...])
-        near, far = times(parts, block[2:4]), times(parts, block[0:2])
+        near, far = times(parts, block[1]), times(parts, block[0])
         spread([2 * pair + 1, 2 * pair], [near, far])
-        if held.shape[1] > 4:
-            base[...] = times(split(far), block[4:6])
+        if count > 4:
+            base[...] = times(split(far), block[2])
         return _
 
     lax.fori_loop(1, mine // 2 + 1, earlier, 0)
 
 
-def add_kernel(left, right, after, out):
-    out[...] = left[...] + right[...]
-
-
-def field_kernel(count, slot, has_state, field, high, low, *rest):
+def pass_kernel(value, after, out):
+    out[...] = value[...]
+
+
+def field_kernel(count, slots, has_state, *refs):
+    fields, (high, low), rest = refs[: len(slots)], refs[len(slots) : len(slots) + 2], refs[len(slots) + 2 :]
     out = rest[-1]
     size = out.shape[-1]
     mine = lax.axis_index("space")
-    valid = valid_terms(jnp.bitwise_xor(mine, slot), mine, count)
-    present = sum(v.astype(jnp.int32) for v in valid)
-
-    def run(terms):
+
+    def run(present):
         total = rows(rest[0]) if has_state else jnp.zeros((size, 2 * size), F32)
-        if terms:
+        for slot, field, terms in zip(slots, fields, present):
+            if not terms:
+                continue
             factors = [part[slot, : terms * size] for part in (high, low)]
             left = split(times(factors, field))
             for term in range(terms):
@@ -193,8 +193,14 @@
                 total = total + product([p[here] for p in left], [full(f[here]) for f in factors], NT)
         out[...] = block_of(total)
 
-    for terms in range(4):
-        pl.when(present == terms)(functools.partial(run, terms))
+    cases = {}
+    for device in range(count):
+        present = tuple(sum(map(bool, valid_terms(device ^ slot, device, count))) for slot in slots)
+        cases.setdefault(present, []).append(device)
+    for present, devices in cases.items():
+        pl.when(functools.reduce(jnp.logical_or, [mine == device for device in devices]))(
+            functools.partial(run, present)
+        )
 
 
 def call(kernel, shapes, specs, *args, scratch=()):
@@ -233,53 +239,48 @@
     pairs_a, pairs_b = matchings(energies // group, group)
     other_a = lax.ppermute(own, "energy", pairs_a)
     other_b = lax.ppermute(own, "energy", pairs_b)
-    packed = jnp.concatenate([retarded.reshape(2, size, size), coupling.reshape(2, size, size)], axis=0)
-    packed_other = exchange(packed, 1)
-    kept = 4 if slabs <= 4 else 6
-    pair = call(pair_kernel, jax.ShapeDtypeStruct((kept, size, size), F32), [VMEM] * 2, packed, packed_other)
-    pairs = gather({0: pair}, chip_bits)
+    retarded = retarded.reshape(2, size, size)
+    coupling = coupling.reshape(2, size, size)
+    shares = call(
+        functools.partial(share_kernel, group), jax.ShapeDtypeStruct((group, 3, 8, 128), F32), [SMEM] * 2,
+        offsets, weights,
+    )
+    pair = call(
+        pair_kernel, [block] * 3, [VMEM] * 4, retarded, coupling, exchange(retarded, 1), exchange(coupling, 1)
+    )
+    combined, second_r = (gather({0: part}, chip_bits) for part in pair[:2])
+    first_c = gather({0: pair[2]}, chip_bits) if slabs > 4 else {2 * p: pair[2] for p in range(slabs // 2)}
     factor_shape = jax.ShapeDtypeStruct((slabs, 3 * size, 2 * size), BF16)
-    *factors, token = call(
-        functools.partial(factor_kernel, slabs), [factor_shape] * 2 + [jax.ShapeDtypeStruct((8, 128), F32)],
-        [SMEM] + [VMEM] * (3 + slabs // 2),
-        material, gradient_table, packed, packed_other, *[pairs[2 * p] for p in range(slabs // 2)],
-        scratch=[pltpu.VMEM((max(slabs // 2 - 1, 1), kept, size, size), F32), pltpu.VMEM((size, 2 * size), F32)],
-    )
-
-    shares = call(
-        functools.partial(share_kernel, group), jax.ShapeDtypeStruct((group, 3, 8, 128), F32), [SMEM, SMEM],
-        offsets, weights,
-    )
+    earlier = [part[2 * p] for part in (combined, second_r, first_c) for p in range(slabs // 2)]
+    factors = call(
+        functools.partial(factor_kernel, slabs), [factor_shape] * 2,
+        [SMEM] + [VMEM] * (2 + len(earlier)), material, gradient_table, retarded, *earlier,
+        scratch=[pltpu.VMEM((max(slabs // 2 - 1, 1), 3, 2, size, size), F32), pltpu.VMEM((size, 2 * size), F32)],
+    )
+
     sums = call(functools.partial(smear_kernel, group), [block] * group, [VMEM] * 4, shares, own, other_a, other_b)
 
-    def propagate(state, slot, field):
-        kernel = functools.partial(field_kernel, slabs, slot, bool(state))
-        return (call(kernel, block, [VMEM] * (3 + len(state)), field, *factors, *state),)
-
-    if group == 2 and len(chip_bits) == 1:
-        bit = chip_bits[0]
-        both = [
-            (e * slabs + s, (e ^ 1) * slabs + (s ^ bit)) for e in range(energies) for s in range(slabs)
-        ]
-        near = lax.ppermute(sums[1], "energy", [(e, e ^ 1) for e in range(energies)])
-        across = exchange(sums[0], bit)
-        far = lax.ppermute(sums[1], ("energy", "space"), both)
-        fields = {0: call(add_kernel, block, [VMEM] * 3, sums[0], near, token)}
-        fields[1] = exchange(fields[0], 1)
-        state = propagate((), 0, fields[0])
-        fields[bit] = call(add_kernel, block, [VMEM] * 3, across, far, state[0])
-        fields[bit ^ 1] = exchange(fields[bit], 1)
-        rest = [1, bit, bit ^ 1]
-    else:
-        field = sums[0]
-        for step in range(1, group):
-            pairs = [(e, e - e % group + (e + step) % group) for e in range(energies)]
-            field = field + lax.ppermute(sums[step], "energy", pairs)
-        fields = gather({0: field}, chip_bits + [1])
-        state, rest = (), sorted(fields)
-    for slot in rest:
-        state = propagate(state, slot, fields[slot])
-    return state[0].reshape(lesser_prev.shape)
+    field = sums[0]
+    for step in range(1, group):
+        pairs = [(e, e - e % group + (e + step) % group) for e in range(energies)]
+        arrived = lax.ppermute(sums[step], "energy", pairs)
+        field = field + arrived
+
+    def propagate(slots, fields, *state):
+        kernel = functools.partial(field_kernel, slabs, slots, bool(state))
+        operands = *[fields[slot] for slot in slots], *factors, *state
+        return call(kernel, block, [VMEM] * len(operands), *operands)
+
+    fields = gather({0: field}, [1])
+    state = propagate([0, 1], fields)
+    for bit in chip_bits:
+        keys = sorted(key for key in fields if key % 2 == 0)
+        for key in keys:
+            arrived = call(pass_kernel, block, [VMEM] * 2, exchange(fields[key], bit), state)
+            fields |= {key ^ bit: arrived, key ^ bit ^ 1: exchange(arrived, 1)}
+        state = propagate([key ^ bit for key in keys], fields, state)
+        state = propagate([key ^ bit ^ 1 for key in keys], fields, state)
+    return state.reshape(lesser_prev.shape)
 
 
 def solution(mesh):

time: 23 us -> 22.5 us (0.978)
  the two profiles are of different devices: /device:TPU:1 before, /device:TPU:13 now
where the time goes in v3:
time: 22.5 us; the launch traced here: 22.4 us
  starting transfers between devices  11.7 us (52%)
  Pallas kernels  7.22 us (32%)
  waiting for transfers between devices  3.32 us (15%)
    ppermute x7, starting transfers between devices, exchange(): return lax.ppermute(value, 'space', [(i, i ^ bit) for i in range(count)])  7.81 us
    pallas_call x8, Pallas kernels, call(): pl.pallas_call(kernel, out_shape=shapes, in_specs=specs, out_specs=jax.tr...  7.22 us
    ppermute x1, starting transfers between devices, per_device(): other_b = lax.ppermute(own, 'energy', pairs_b)  2.42 us
    ppermute x7, waiting for transfers between devices, exchange(): return lax.ppermute(value, 'space', [(i, i ^ bit) for i in range(count)])  1.58 us
    ppermute x1, starting transfers between devices, per_device(): arrived = lax.ppermute(sums[step], 'energy', pairs)  1.28 us
    ppermute x1, waiting for transfers between devices, per_device(): other_b = lax.ppermute(own, 'energy', pairs_b)  1.15 us
    ppermute x1, waiting for transfers between devices, per_device(): arrived = lax.ppermute(sums[step], 'energy', pairs)  0.59 us
  transfers between devices with their start and end apart: 10, of which 4 were waited for; matrix products, arithmetic and copies ran while one was open for 0% of the time, Pallas kernels for 26%

profile of v3, /device:TPU:13, one launch (start us, length us, event | category | flops | bytes accessed | tf_op | source)
XLA Modules:
  0.0 22.4 jit_solution(2818666931423396007)
XLA Ops:
  0.0 0.2 collective-permute-start
  0.2 2.4 %collective-permute-start.1 = (f32[2,128,128]{2,1,0:T(8,128)}, f32[2,128,128]{2,1,0:T(8,128)S(1)}, u32[]{:S(2)}, u32[]{:S(2)}) collective-permute-start(f32[2,128,128]{2,1,0:T(8,128)} %bitcast.7), channel_id=1, source_target_pairs={{0,4},{4,0},{8,16},{12,20},{16,8},{20,12},{24,28},{28,24},{1,5},{5... | collective-permute-start | bytes 393224 | tf_op jit(solution)/shard_map/ppermute | solution.py:241
  2.6 0.0 copy-start.4
  2.6 0.0 copy-start.5
  2.6 1.2 %collective-permute-start.5 = (f32[2,128,128]{2,1,0:T(8,128)}, f32[2,128,128]{2,1,0:T(8,128)S(1)}, u32[]{:S(2)}, u32[]{:S(2)}) collective-permute-start(f32[2,128,128]{2,1,0:T(8,128)} %bitcast.11), channel_id=1, source_target_pairs={{0,1},{1,0},{2,3},{3,2},{4,5},{5,4},{6,7},{7,6},{8,9},{9,8},{10,11... | collective-permute-start | bytes 393224 | tf_op jit(solution)/shard_map/ppermute | solution.py:222
  3.8 0.0 copy-start.1
  3.8 0.1 collective-permute-start.6
  3.9 0.0 copy-done.4
  3.9 0.0 copy-done.5
  3.9 0.6 %shard_map.73.shares = f32[2,3,8,128]{3,2,1,0:T(8,128)S(1)} custom-call(s32[8]{0:T(128)S(1)} %copy-done.4, f32[8]{0:T(128)S(1)} %copy-done.5), custom_call_target="tpu_custom_call" | custom-call | flops 1000000000 | bytes 64 | tf_op jit(solution)/shard_map/pallas_call | solution.py:207
  4.6 0.0 copy-start.2
  4.6 0.0 copy-start.3
  4.6 0.0 collective-permute-done.other_a
  4.6 1.2 %collective-permute-done.1.other_b = f32[2,128,128]{2,1,0:T(8,128)S(1)} collective-permute-done((f32[2,128,128]{2,1,0:T(8,128)}, f32[2,128,128]{2,1,0:T(8,128)S(1)}, u32[]{:S(2)}, u32[]{:S(2)}) %collective-permute-start.1) | collective-permute-done | bytes 131104 | tf_op jit(solution)/shard_map/ppermute | solution.py:241
  5.7 0.0 copy-done.1
  5.7 0.1 shard_map.74
  5.8 0.0 copy-start
  5.8 1.3 %collective-permute-start.2 = (f32[2,128,128]{2,1,0:T(8,128)S(1)}, f32[2,128,128]{2,1,0:T(8,128)S(1)}, u32[]{:S(2)}, u32[]{:S(2)}) collective-permute-start(f32[2,128,128]{2,1,0:T(8,128)S(1)} %get-tuple-element.13), channel_id=1, source_target_pairs={{0,4},{4,0},{8,12},{12,8},{16,20},{20,16},{24,28},{28,24},{1,5},{5... | collective-permute-start | bytes 393224 | tf_op jit(solution)/shard_map/ppermute | solution.py:266
  7.1 0.0 collective-permute-done.5.other_r
  7.1 0.0 collective-permute-done.6.other_c
  7.1 0.0 copy-done.2
  7.1 0.0 copy-done.3
  7.1 0.5 %shard_map.75 = (f32[2,128,128]{2,1,0:T(8,128)S(1)}, f32[2,128,128]{2,1,0:T(8,128)S(1)}, f32[2,128,128]{2,1,0:T(8,128)S(1)}) custom-call(f32[2,128,128]{2,1,0:T(8,128)S(1)} %bitcast.12, f32[2,128,128]{2,1,0:T(8,128)S(1)} %bitcast.10, f32[2,128,128]{2,1,0:T(8,128)S(1)} %collective-permute-done.5.other_r, f32[2,128,128]{2,1,0:T(8,128)S(1)} %collective-permute-done.6.other_c), custom_call_target="tpu_custom_call" | custom-call | flops 1000000000 | bytes 524288 | tf_op jit(solution)/shard_map/pallas_call | solution.py:207
  7.6 0.3 %collective-permute-start.7 = (f32[2,128,128]{2,1,0:T(8,128)S(1)}, f32[2,128,128]{2,1,0:T(8,128)S(1)}, u32[]{:S(2)}, u32[]{:S(2)}) collective-permute-start(f32[2,128,128]{2,1,0:T(8,128)S(1)} %get-tuple-element.14.refs_0_), channel_id=1, source_target_pairs={{0,2},{1,3},{2,0},{3,1},{4,6},{5,7},{6,4},{7,5},{8,10},{9,11},{10,... | collective-permute-start | bytes 393224 | tf_op jit(solution)/shard_map/ppermute | solution.py:222
  7.9 1.2 %collective-permute-start.8 = (f32[2,128,128]{2,1,0:T(8,128)S(1)}, f32[2,128,128]{2,1,0:T(8,128)S(1)}, u32[]{:S(2)}, u32[]{:S(2)}) collective-permute-start(f32[2,128,128]{2,1,0:T(8,128)S(1)} %get-tuple-element.15.refs_2_), channel_id=1, source_target_pairs={{0,2},{1,3},{2,0},{3,1},{4,6},{5,7},{6,4},{7,5},{8,10},{9,11},{10,... | collective-permute-start | bytes 393224 | tf_op jit(solution)/shard_map/ppermute | solution.py:222
  9.1 0.6 %collective-permute-done.2 = f32[2,128,128]{2,1,0:T(8,128)S(1)} collective-permute-done((f32[2,128,128]{2,1,0:T(8,128)S(1)}, f32[2,128,128]{2,1,0:T(8,128)S(1)}, u32[]{:S(2)}, u32[]{:S(2)}) %collective-permute-start.2) | collective-permute-done | bytes 131104 | tf_op jit(solution)/shard_map/ppermute | solution.py:266
  9.7 0.0 copy-start.6
  9.7 2.8 %collective-permute-start.4 = (f32[2,128,128]{2,1,0:T(8,128)S(1)}, f32[2,128,128]{2,1,0:T(8,128)S(1)}, u32[]{:S(2)}, u32[]{:S(2)}) collective-permute-start(f32[2,128,128]{2,1,0:T(8,128)S(1)} %add.3.refs_0_), channel_id=1, source_target_pairs={{0,1},{1,0},{2,3},{3,2},{4,5},{5,4},{6,7},{7,6},{8,9},{9,8},{10,11... | collective-permute-start | bytes 393224 | tf_op jit(solution)/shard_map/ppermute | solution.py:222
  12.5 0.2 %collective-permute-start.3 = (f32[2,128,128]{2,1,0:T(8,128)S(1)}, f32[2,128,128]{2,1,0:T(8,128)S(1)}, u32[]{:S(2)}, u32[]{:S(2)}) collective-permute-start(f32[2,128,128]{2,1,0:T(8,128)S(1)} %add.3.refs_0_), channel_id=1, source_target_pairs={{0,2},{1,3},{2,0},{3,1},{4,6},{5,7},{6,4},{7,5},{8,10},{9,11},{10,... | collective-permute-start | bytes 393224 | tf_op jit(solution)/shard_map/ppermute | solution.py:222
  12.7 0.0 collective-permute-done.7.refs_1_
  12.7 0.9 %collective-permute-done.8.refs_3_ = f32[2,128,128]{2,1,0:T(8,128)S(1)} collective-permute-done((f32[2,128,128]{2,1,0:T(8,128)S(1)}, f32[2,128,128]{2,1,0:T(8,128)S(1)}, u32[]{:S(2)}, u32[]{:S(2)}) %collective-permute-start.8) | collective-permute-done | bytes 131104 | tf_op jit(solution)/shard_map/ppermute | solution.py:222
  13.6 0.0 copy-done
  13.6 0.0 copy-done.6
  13.6 2.2 %shard_map.76 = (bf16[4,384,256]{2,1,0:T(8,128)(2,1)S(1)}, bf16[4,384,256]{2,1,0:T(8,128)(2,1)S(1)}) custom-call(s32[4]{0:T(128)S(1)} %copy-done.6, f32[4,2,128,128]{3,2,1,0:T(8,128)S(1)} %copy-done, f32[2,128,128]{2,1,0:T(8,128)S(1)} %bitcast.13, f32[2,128,128]{2,1,0:T(8,128)S(1)} %get-tuple-element.14.refs_0_, ...), custom_call_target="tpu_custom_call" | custom-call | flops 1000000000 | bytes 1441808 | tf_op jit(solution)/shard_map/pallas_call | solution.py:207
  15.8 0.0 collective-permute-done.4.refs_1_
  15.8 1.6 %shard_map.77.after.refs_3_ = f32[2,128,128]{2,1,0:T(8,128)S(1)} custom-call(f32[2,128,128]{2,1,0:T(8,128)S(1)} %add.3.refs_0_, f32[2,128,128]{2,1,0:T(8,128)S(1)} %collective-permute-done.4.refs_1_, bf16[4,384,256]{2,1,0:T(8,128)(2,1)S(1)} %get-tuple-element.17.refs_2_.refs_1_, bf16[4,384,256]{2,1,0:T(8,128)(2,1)S(1)} %get-tuple-element.18.refs_3_.refs_2_), custom_call_target="tpu_custom_call" | custom-call | flops 1000000000 | bytes 1835008 | tf_op jit(solution)/shard_map/pallas_call | solution.py:207
  17.4 0.6 %collective-permute-done.3.value = f32[2,128,128]{2,1,0:T(8,128)S(1)} collective-permute-done((f32[2,128,128]{2,1,0:T(8,128)S(1)}, f32[2,128,128]{2,1,0:T(8,128)S(1)}, u32[]{:S(2)}, u32[]{:S(2)}) %collective-permute-start.3) | collective-permute-done | bytes 131104 | tf_op jit(solution)/shard_map/ppermute | solution.py:222
  18.1 2.0 %collective-permute-start.9 = (f32[2,128,128]{2,1,0:T(8,128)S(1)}, f32[2,128,128]{2,1,0:T(8,128)S(1)}, u32[]{:S(2)}, u32[]{:S(2)}) collective-permute-start(f32[2,128,128]{2,1,0:T(8,128)S(1)} %shard_map.78.refs_0_), channel_id=1, source_target_pairs={{0,1},{1,0},{2,3},{3,2},{4,5},{5,4},{6,7},{7,6},{8,9},{9,8},{10,11... | collective-permute-start | bytes 393224 | tf_op jit(solution)/shard_map/ppermute | solution.py:222
  20.1 0.9 %shard_map.79.refs_3_ = f32[2,128,128]{2,1,0:T(8,128)S(1)} custom-call(f32[2,128,128]{2,1,0:T(8,128)S(1)} %shard_map.78.refs_0_, bf16[4,384,256]{2,1,0:T(8,128)(2,1)S(1)} %get-tuple-element.17.refs_2_.refs_1_, bf16[4,384,256]{2,1,0:T(8,128)(2,1)S(1)} %get-tuple-element.18.refs_3_.refs_2_, f32[2,128,128]{2,1,0:T(8,128)S(1)} %shard_map.77.after.refs_3_), custom_call_target="tpu_custom_call" | custom-call | flops 1000000000 | bytes 1835008 | tf_op jit(solution)/shard_map/pallas_call | solution.py:207
  21.0 0.0 collective-permute-done.9.refs_0_
  21.1 1.3 %shard_map.80 = f32[2,128,128]{2,1,0:T(8,128)} custom-call(f32[2,128,128]{2,1,0:T(8,128)S(1)} %collective-permute-done.9.refs_0_, bf16[4,384,256]{2,1,0:T(8,128)(2,1)S(1)} %get-tuple-element.17.refs_2_.refs_1_, bf16[4,384,256]{2,1,0:T(8,128)(2,1)S(1)} %get-tuple-element.18.refs_3_.refs_2_, f32[2,128,128]{2,1,0:T(8,128)S(1)} %shard_map.79.refs_3_), custom_call_target="tpu_custom_call" | custom-call | flops 1000000000 | bytes 1835008 | tf_op jit(solution)/shard_map/pallas_call | solution.py:207
  (2 shorter events, 0.0 us)
Async XLA Ops:
  0.0 4.6 %collective-permute-start = (f32[2,128,128]{2,1,0:T(8,128)}, f32[2,128,128]{2,1,0:T(8,128)S(1)}, u32[]{:S(2)}, u32[]{:S(2)}) collective-permute-start(f32[2,128,128]{2,1,0:T(8,128)} %bitcast.6), channel_id=1, source_target_pairs={{0,8},{4,12},{8,0},{12,4},{16,24},{20,28},{24,16},{28,20},{1,9},{5... | collective-permute-start | bytes 393224 | tf_op jit(solution)/shard_map/ppermute | solution.py:240
  0.2 5.6 %collective-permute-start.1 = (f32[2,128,128]{2,1,0:T(8,128)}, f32[2,128,128]{2,1,0:T(8,128)S(1)}, u32[]{:S(2)}, u32[]{:S(2)}) collective-permute-start(f32[2,128,128]{2,1,0:T(8,128)} %bitcast.7), channel_id=1, source_target_pairs={{0,4},{4,0},{8,16},{12,20},{16,8},{20,12},{24,28},{28,24},{1,5},{5... | collective-permute-start | bytes 393224 | tf_op jit(solution)/shard_map/ppermute | solution.py:241
  2.6 1.3 %copy-start.4 = (s32[8]{0:T(128)S(1)}, s32[8]{0:T(128)}, u32[]{:S(2)}) copy-start(s32[8]{0:T(128)} %offsets.1) | copy-start | bytes 100
  2.6 1.3 %copy-start.5 = (f32[8]{0:T(128)S(1)}, f32[8]{0:T(128)}, u32[]{:S(2)}) copy-start(f32[8]{0:T(128)} %weights.1) | copy-start | bytes 100
  2.6 4.5 %collective-permute-start.5 = (f32[2,128,128]{2,1,0:T(8,128)}, f32[2,128,128]{2,1,0:T(8,128)S(1)}, u32[]{:S(2)}, u32[]{:S(2)}) collective-permute-start(f32[2,128,128]{2,1,0:T(8,128)} %bitcast.11), channel_id=1, source_target_pairs={{0,1},{1,0},{2,3},{3,2},{4,5},{5,4},{6,7},{7,6},{8,9},{9,8},{10,11... | collective-permute-start | bytes 393224 | tf_op jit(solution)/shard_map/ppermute | solution.py:222
  3.8 1.9 %copy-start.1 = (f32[2,1,1,128,128]{4,3,2,1,0:T(8,128)S(1)}, f32[2,1,1,128,128]{4,3,2,1,0:T(8,128)}, u32[]{:S(2)}) copy-start(f32[2,1,1,128,128]{4,3,2,1,0:T(8,128)} %param.7) | copy-start | bytes 393220
  3.8 3.3 %collective-permute-start.6 = (f32[2,128,128]{2,1,0:T(8,128)}, f32[2,128,128]{2,1,0:T(8,128)S(1)}, u32[]{:S(2)}, u32[]{:S(2)}) collective-permute-start(f32[2,128,128]{2,1,0:T(8,128)} %bitcast.9), channel_id=1, source_target_pairs={{0,1},{1,0},{2,3},{3,2},{4,5},{5,4},{6,7},{7,6},{8,9},{9,8},{10,11... | collective-permute-start | bytes 393224 | tf_op jit(solution)/shard_map/ppermute | solution.py:222
  4.6 2.5 %copy-start.2 = (f32[2,1,128,128]{3,2,1,0:T(8,128)S(1)}, f32[2,1,128,128]{3,2,1,0:T(8,128)}, u32[]{:S(2)}) copy-start(f32[2,1,128,128]{3,2,1,0:T(8,128)} %param.9) | copy-start | bytes 393220
  4.6 2.5 %copy-start.3 = (f32[2,1,1,128,128]{4,3,2,1,0:T(8,128)S(1)}, f32[2,1,1,128,128]{4,3,2,1,0:T(8,128)}, u32[]{:S(2)}) copy-start(f32[2,1,1,128,128]{4,3,2,1,0:T(8,128)} %param.8) | copy-start | bytes 393220
  5.8 7.8 %copy-start = (f32[4,2,128,128]{3,2,1,0:T(8,128)S(1)}, f32[4,2,128,128]{3,2,1,0:T(8,128)}, u32[]{:S(2)}) copy-start(f32[4,2,128,128]{3,2,1,0:T(8,128)} %table.1) | copy-start | bytes 1572868
  5.8 3.9 %collective-permute-start.2 = (f32[2,128,128]{2,1,0:T(8,128)S(1)}, f32[2,128,128]{2,1,0:T(8,128)S(1)}, u32[]{:S(2)}, u32[]{:S(2)}) collective-permute-start(f32[2,128,128]{2,1,0:T(8,128)S(1)} %get-tuple-element.13), channel_id=1, source_target_pairs={{0,4},{4,0},{8,12},{12,8},{16,20},{20,16},{24,28},{28,24},{1,5},{5... | collective-permute-start | bytes 393224 | tf_op jit(solution)/shard_map/ppermute | solution.py:266
  7.6 5.2 %collective-permute-start.7 = (f32[2,128,128]{2,1,0:T(8,128)S(1)}, f32[2,128,128]{2,1,0:T(8,128)S(1)}, u32[]{:S(2)}, u32[]{:S(2)}) collective-permute-start(f32[2,128,128]{2,1,0:T(8,128)S(1)} %get-tuple-element.14.refs_0_), channel_id=1, source_target_pairs={{0,2},{1,3},{2,0},{3,1},{4,6},{5,7},{6,4},{7,5},{8,10},{9,11},{10,... | collective-permute-start | bytes 393224 | tf_op jit(solution)/shard_map/ppermute | solution.py:222
  7.9 5.7 %collective-permute-start.8 = (f32[2,128,128]{2,1,0:T(8,128)S(1)}, f32[2,128,128]{2,1,0:T(8,128)S(1)}, u32[]{:S(2)}, u32[]{:S(2)}) collective-permute-start(f32[2,128,128]{2,1,0:T(8,128)S(1)} %get-tuple-element.15.refs_2_), channel_id=1, source_target_pairs={{0,2},{1,3},{2,0},{3,1},{4,6},{5,7},{6,4},{7,5},{8,10},{9,11},{10,... | collective-permute-start | bytes 393224 | tf_op jit(solution)/shard_map/ppermute | solution.py:222
  9.7 3.9 %copy-start.6 = (s32[4]{0:T(128)S(1)}, s32[4]{0:T(128)}, u32[]{:S(2)}) copy-start(s32[4]{0:T(128)} %material.1) | copy-start | bytes 52
  9.7 6.1 %collective-permute-start.4 = (f32[2,128,128]{2,1,0:T(8,128)S(1)}, f32[2,128,128]{2,1,0:T(8,128)S(1)}, u32[]{:S(2)}, u32[]{:S(2)}) collective-permute-start(f32[2,128,128]{2,1,0:T(8,128)S(1)} %add.3.refs_0_), channel_id=1, source_target_pairs={{0,1},{1,0},{2,3},{3,2},{4,5},{5,4},{6,7},{7,6},{8,9},{9,8},{10,11... | collective-permute-start | bytes 393224 | tf_op jit(solution)/shard_map/ppermute | solution.py:222
  12.5 5.6 %collective-permute-start.3 = (f32[2,128,128]{2,1,0:T(8,128)S(1)}, f32[2,128,128]{2,1,0:T(8,128)S(1)}, u32[]{:S(2)}, u32[]{:S(2)}) collective-permute-start(f32[2,128,128]{2,1,0:T(8,128)S(1)} %add.3.refs_0_), channel_id=1, source_target_pairs={{0,2},{1,3},{2,0},{3,1},{4,6},{5,7},{6,4},{7,5},{8,10},{9,11},{10,... | collective-permute-start | bytes 393224 | tf_op jit(solution)/shard_map/ppermute | solution.py:222
  18.1 3.0 %collective-permute-start.9 = (f32[2,128,128]{2,1,0:T(8,128)S(1)}, f32[2,128,128]{2,1,0:T(8,128)S(1)}, u32[]{:S(2)}, u32[]{:S(2)}) collective-permute-start(f32[2,128,128]{2,1,0:T(8,128)S(1)} %shard_map.78.refs_0_), channel_id=1, source_target_pairs={{0,1},{1,0},{2,3},{3,2},{4,5},{5,4},{6,7},{7,6},{8,9},{9,8},{10,11... | collective-permute-start | bytes 393224 | tf_op jit(solution)/shard_map/ppermute | solution.py:222

commit v4 on v3

--- a/solution.py
+++ b/solution.py
@@ -50,7 +50,7 @@
     return product(left, [full(part) for part in split(rows(right_block))], NT)
 
 
-def share_kernel(group, offsets, weights, out):
+def share_kernel(group, offsets, weights, material, out, kinds):
     count = lax.axis_size("energy")
     mine = lax.axis_index("energy")
     place, rank = mine // group, mine % group
@@ -66,6 +66,8 @@
         target = place * group + (rank + step) % group
         for index, (source, valid) in enumerate(((mine, True), (source_a, has_a), (source_b, has_b))):
             out[step, index] = jnp.full(out.shape[2:], coefficient(target, source, valid), F32)
+    for slab in range(material.shape[0]):
+        kinds[slab] = jnp.full(kinds.shape[1:], material[slab], jnp.int32)
 
 
 def smear_kernel(group, shares, own, other_a, other_b, *outs):
@@ -100,27 +102,33 @@
     return result
 
 
-def pair_kernel(own_r, own_c, other_r, other_c, combined, second_r, first_c):
+def pair_kernel(own_r, own_c, other_r, other_c, after, combined, sent, first_c):
     odd = lax.axis_index("space") % 2 == 1
     first_r = jnp.where(odd, other_r[...], own_r[...])
+    second_r = jnp.where(odd, own_r[...], other_r[...])
     second_c = jnp.where(odd, own_c[...], other_c[...])
-    second_r[...] = jnp.where(odd, own_r[...], other_r[...])
     first_c[...] = jnp.where(odd, other_c[...], own_c[...])
-    combined[...] = block_of(times(split(times(split(rows(second_r)), second_c)), first_r))
+    made = block_of(times(split(times(split(rows(second_r)), second_c)), first_r))
+    combined[...] = made
+    sent[...] = jnp.where(odd, own_r[...], made)
 
 
 def valid_terms(slab, mine, count):
     return slab <= mine, (slab >= 1) & (slab <= mine + 1), slab < mine
 
 
-def factor_kernel(count, material, table, own_r, *refs):
-    combined, second_r, first_c = (refs[n * count // 2 : (n + 1) * count // 2] for n in range(3))
-    *outs, held, base = refs[3 * count // 2 :]
+def factor_kernel(count, kinds, table, own_r, combined, own_first_c, *refs):
+    pairs = count // 2
+    sent, crossed, first_c = (refs[n * (pairs - 1) : (n + 1) * (pairs - 1)] for n in range(3))
+    *outs, held, base = refs[3 * (pairs - 1) :]
     mine = lax.axis_index("space")
+    odd = mine % 2 == 1
     size = table.shape[-1]
-    for slot in range(1, count // 2):
-        for index, blocks in enumerate((combined, second_r, first_c)):
-            held[slot - 1, index] = blocks[slot][...]
+    for slot in range(pairs - 1):
+        here, there = sent[slot][...], crossed[slot][...]
+        held[slot, 0] = jnp.where(odd, there, here)
+        held[slot, 1] = jnp.where(odd, here, there)
+        held[slot, 2] = first_c[slot][...]
 
     def store(slab, which, parts):
         valid = valid_terms(slab, mine, count)
@@ -135,19 +143,17 @@
         made = []
         for slab, whole in zip(slabs, maps):
             parts = split(whole)
-            right = times(parts, table[material[slab]])
-            left = times_dagger(parts, table[material[jnp.maximum(slab - 1, 0)]])
+            right = times(parts, table[kinds[slab, 0, 0]])
+            left = times_dagger(parts, table[kinds[jnp.maximum(slab - 1, 0), 0, 0]])
             made.append((parts, split(right), split(left)))
         for slab, (same, right, left) in zip(slabs, made):
             store(slab, 0, same)
             store(slab + 1, 1, right)
             store(slab - 1, 2, left)
 
-    odd = mine % 2 == 1
-
     @pl.when(odd)
     def _():
-        spread([mine, mine - 1], [rows(own_r), rows(combined[0])])
+        spread([mine, mine - 1], [rows(own_r), rows(combined)])
 
     @pl.when(jnp.logical_not(odd))
     def _():
@@ -155,8 +161,8 @@
 
     @pl.when(mine >= 2)
     def _():
-        start = split(jnp.where(odd, rows(combined[0]), rows(own_r)))
-        base[...] = times(start, first_c[0])
+        start = split(jnp.where(odd, rows(combined), rows(own_r)))
+        base[...] = times(start, own_first_c)
 
     def earlier(step, _):
         pair = mine // 2 - step
@@ -241,23 +247,22 @@
     other_b = lax.ppermute(own, "energy", pairs_b)
     retarded = retarded.reshape(2, size, size)
     coupling = coupling.reshape(2, size, size)
-    shares = call(
-        functools.partial(share_kernel, group), jax.ShapeDtypeStruct((group, 3, 8, 128), F32), [SMEM] * 2,
-        offsets, weights,
-    )
-    pair = call(
-        pair_kernel, [block] * 3, [VMEM] * 4, retarded, coupling, exchange(retarded, 1), exchange(coupling, 1)
-    )
-    combined, second_r = (gather({0: part}, chip_bits) for part in pair[:2])
-    first_c = gather({0: pair[2]}, chip_bits) if slabs > 4 else {2 * p: pair[2] for p in range(slabs // 2)}
-    factor_shape = jax.ShapeDtypeStruct((slabs, 3 * size, 2 * size), BF16)
-    earlier = [part[2 * p] for part in (combined, second_r, first_c) for p in range(slabs // 2)]
-    factors = call(
-        functools.partial(factor_kernel, slabs), [factor_shape] * 2,
-        [SMEM] + [VMEM] * (2 + len(earlier)), material, gradient_table, retarded, *earlier,
-        scratch=[pltpu.VMEM((max(slabs // 2 - 1, 1), 3, 2, size, size), F32), pltpu.VMEM((size, 2 * size), F32)],
-    )
-
+    shares, kinds = call(
+        functools.partial(share_kernel, group),
+        [jax.ShapeDtypeStruct((group, 3, 8, 128), F32), jax.ShapeDtypeStruct((slabs, 8, 128), jnp.int32)], [SMEM] * 3,
+        offsets, weights, material,
+    )
+    combined, sent, first_c = call(
+        pair_kernel, [block] * 3, [VMEM] * 5, retarded, coupling, exchange(retarded, 1), exchange(coupling, 1), shares,
+    )
+    sent = gather({0: sent}, chip_bits)
+    all_c = gather({0: first_c}, chip_bits) if slabs > 4 else {slot: first_c for slot in sent}
+    others = [slot for slot in sorted(sent) if slot]
+    earlier = (
+        [sent[slot] for slot in others]
+        + [exchange(sent[slot], 1) for slot in others]
+        + [all_c[slot] for slot in others]
+    )
     sums = call(functools.partial(smear_kernel, group), [block] * group, [VMEM] * 4, shares, own, other_a, other_b)
 
     field = sums[0]
@@ -266,20 +271,29 @@
         arrived = lax.ppermute(sums[step], "energy", pairs)
         field = field + arrived
 
+    factor_shape = jax.ShapeDtypeStruct((slabs, 3 * size, 2 * size), BF16)
+    factors = call(
+        functools.partial(factor_kernel, slabs), [factor_shape] * 2,
+        [VMEM] * (5 + len(earlier)), kinds, gradient_table, retarded, combined, first_c, *earlier,
+        scratch=[pltpu.VMEM((max(slabs // 2 - 1, 1), 3, 2, size, size), F32), pltpu.VMEM((size, 2 * size), F32)],
+    )
+
     def propagate(slots, fields, *state):
         kernel = functools.partial(field_kernel, slabs, slots, bool(state))
         operands = *[fields[slot] for slot in slots], *factors, *state
         return call(kernel, block, [VMEM] * len(operands), *operands)
 
-    fields = gather({0: field}, [1])
-    state = propagate([0, 1], fields)
+    fields = {0: field}
+    state = propagate([0], fields)
+    own = call(pass_kernel, block, [VMEM] * 2, field, state)
+    fields[1] = exchange(own, 1)
     for bit in chip_bits:
-        keys = sorted(key for key in fields if key % 2 == 0)
-        for key in keys:
-            arrived = call(pass_kernel, block, [VMEM] * 2, exchange(fields[key], bit), state)
-            fields |= {key ^ bit: arrived, key ^ bit ^ 1: exchange(arrived, 1)}
-        state = propagate([key ^ bit for key in keys], fields, state)
-        state = propagate([key ^ bit ^ 1 for key in keys], fields, state)
+        for key in [key for key in fields if key % 2 == 0]:
+            fields[key ^ bit] = call(pass_kernel, block, [VMEM] * 2, exchange(fields[key], bit), own)
+    others = [key for key in sorted(fields) if key % 2 == 0 and key]
+    fields |= gather({key: fields[key] for key in others}, [1])
+    state = propagate([1] + others, fields, state)
+    state = propagate([key ^ 1 for key in others], fields, state)
     return state.reshape(lesser_prev.shape)
 
 

time: 22.5 us -> 21.5 us (0.956)
  the two profiles are of different devices: /device:TPU:13 before, /device:TPU:1 now
where the time goes in v4:
time: 21.5 us; the launch traced here: 21.4 us
  starting transfers between devices  15.2 us (71%)
  Pallas kernels  4.34 us (20%)
  waiting for transfers between devices  1.63 us (8%)
    ppermute x7, starting transfers between devices, exchange(): return lax.ppermute(value, 'space', [(i, i ^ bit) for i in range(count)])  10.3 us
    pallas_call x9, Pallas kernels, call(): pl.pallas_call(kernel, out_shape=shapes, in_specs=specs, out_specs=jax.tr...  4.34 us
    ppermute x1, starting transfers between devices, per_device(): other_a = lax.ppermute(own, 'energy', pairs_a)  2.38 us
    ppermute x1, starting transfers between devices, per_device(): arrived = lax.ppermute(sums[step], 'energy', pairs)  1.28 us
    ppermute x1, starting transfers between devices, per_device(): other_b = lax.ppermute(own, 'energy', pairs_b)  1.21 us
    ppermute x1, waiting for transfers between devices, per_device(): other_b = lax.ppermute(own, 'energy', pairs_b)  0.81 us
    ppermute x7, waiting for transfers between devices, exchange(): return lax.ppermute(value, 'space', [(i, i ^ bit) for i in range(count)])  0.71 us
  transfers between devices with their start and end apart: 10, of which 4 were waited for; matrix products, arithmetic and copies ran while one was open for 0% of the time, Pallas kernels for 15%

profile of v4, /device:TPU:1, one launch (start us, length us, event | category | flops | bytes accessed | tf_op | source)
XLA Modules:
  0.0 21.4 jit_solution(1033509797202930082)
XLA Ops:
  0.0 0.1 collective-permute-start.4
  0.1 0.0 copy-start.4
  0.1 0.0 copy-start.5
  0.1 0.0 copy-start.6
  0.1 0.5 %collective-permute-start.5 = (f32[2,128,128]{2,1,0:T(8,128)}, f32[2,128,128]{2,1,0:T(8,128)S(1)}, u32[]{:S(2)}, u32[]{:S(2)}) collective-permute-start(f32[2,128,128]{2,1,0:T(8,128)} %bitcast.6), channel_id=1, source_target_pairs={{0,1},{1,0},{2,3},{3,2},{4,5},{5,4},{6,7},{7,6},{8,9},{9,8},{10,11... | collective-permute-start | bytes 393224 | tf_op jit(solution)/shard_map/ppermute | solution.py:228
  0.5 0.0 copy-start.1
  0.5 0.0 copy-start.3
  0.5 2.4 %collective-permute-start = (f32[2,128,128]{2,1,0:T(8,128)}, f32[2,128,128]{2,1,0:T(8,128)S(1)}, u32[]{:S(2)}, u32[]{:S(2)}) collective-permute-start(f32[2,128,128]{2,1,0:T(8,128)} %bitcast.8), channel_id=1, source_target_pairs={{0,8},{4,12},{8,0},{12,4},{16,24},{20,28},{24,16},{28,20},{1,9},{5... | collective-permute-start | bytes 393224 | tf_op jit(solution)/shard_map/ppermute | solution.py:246
  2.9 1.2 %collective-permute-start.1 = (f32[2,128,128]{2,1,0:T(8,128)}, f32[2,128,128]{2,1,0:T(8,128)S(1)}, u32[]{:S(2)}, u32[]{:S(2)}) collective-permute-start(f32[2,128,128]{2,1,0:T(8,128)} %bitcast.9), channel_id=1, source_target_pairs={{0,4},{4,0},{8,16},{12,20},{16,8},{20,12},{24,28},{28,24},{1,5},{5... | collective-permute-start | bytes 393224 | tf_op jit(solution)/shard_map/ppermute | solution.py:247
  4.1 0.0 copy-done.4
  4.1 0.0 copy-done.5
  4.1 0.0 copy-done.6
  4.1 0.6 %shard_map.73 = (f32[2,3,8,128]{3,2,1,0:T(8,128)S(1)}, s32[4,8,128]{2,1,0:T(8,128)S(1)}) custom-call(s32[8]{0:T(128)S(1)} %copy-done.4, f32[8]{0:T(128)S(1)} %copy-done.5, s32[4]{0:T(128)S(1)} %copy-done.6), custom_call_target="tpu_custom_call" | custom-call | flops 1000000000 | bytes 80 | tf_op jit(solution)/shard_map/pallas_call | solution.py:213
  4.8 0.0 collective-permute-done.4.other_r
  4.8 0.0 collective-permute-done.5.other_c
  4.8 0.0 copy-done.1
  4.8 0.0 copy-done.3
  4.8 0.0 copy-start.2
  4.8 0.5 %shard_map.75 = (f32[2,128,128]{2,1,0:T(8,128)S(1)}, f32[2,128,128]{2,1,0:T(8,128)S(1)}, f32[2,128,128]{2,1,0:T(8,128)S(1)}) custom-call(f32[2,128,128]{2,1,0:T(8,128)S(1)} %bitcast.12, f32[2,128,128]{2,1,0:T(8,128)S(1)} %bitcast.7, f32[2,128,128]{2,1,0:T(8,128)S(1)} %collective-permute-done.4.other_r, f32[2,128,128]{2,1,0:T(8,128)S(1)} %collective-permute-done.5.other_c, ...), custom_call_target="tpu_custom_call" | custom-call | flops 1000000000 | bytes 548864 | tf_op jit(solution)/shard_map/pallas_call | solution.py:213
  5.3 0.0 copy-start
  5.3 1.3 %collective-permute-start.6 = (f32[2,128,128]{2,1,0:T(8,128)S(1)}, f32[2,128,128]{2,1,0:T(8,128)S(1)}, u32[]{:S(2)}, u32[]{:S(2)}) collective-permute-start(f32[2,128,128]{2,1,0:T(8,128)S(1)} %get-tuple-element.20), channel_id=1, source_target_pairs={{0,2},{1,3},{2,0},{3,1},{4,6},{5,7},{6,4},{7,5},{8,10},{9,11},{10,... | collective-permute-start | bytes 393224 | tf_op jit(solution)/shard_map/ppermute | solution.py:228
  6.6 0.0 collective-permute-done.other_a
  6.6 0.8 %collective-permute-done.1.other_b = f32[2,128,128]{2,1,0:T(8,128)S(1)} collective-permute-done((f32[2,128,128]{2,1,0:T(8,128)}, f32[2,128,128]{2,1,0:T(8,128)S(1)}, u32[]{:S(2)}, u32[]{:S(2)}) %collective-permute-start.1) | collective-permute-done | bytes 131104 | tf_op jit(solution)/shard_map/ppermute | solution.py:247
  7.4 0.0 copy-done.2
  7.4 0.1 shard_map.74
  7.5 1.3 %collective-permute-start.2 = (f32[2,128,128]{2,1,0:T(8,128)S(1)}, f32[2,128,128]{2,1,0:T(8,128)S(1)}, u32[]{:S(2)}, u32[]{:S(2)}) collective-permute-start(f32[2,128,128]{2,1,0:T(8,128)S(1)} %get-tuple-element.16), channel_id=1, source_target_pairs={{0,4},{4,0},{8,12},{12,8},{16,20},{20,16},{24,28},{28,24},{1,5},{5... | collective-permute-start | bytes 393224 | tf_op jit(solution)/shard_map/ppermute | solution.py:271
  8.8 0.4 %collective-permute-done.6.refs_0_ = f32[2,128,128]{2,1,0:T(8,128)S(1)} collective-permute-done((f32[2,128,128]{2,1,0:T(8,128)S(1)}, f32[2,128,128]{2,1,0:T(8,128)S(1)}, u32[]{:S(2)}, u32[]{:S(2)}) %collective-permute-start.6) | collective-permute-done | bytes 131104 | tf_op jit(solution)/shard_map/ppermute | solution.py:228
  9.2 2.1 %collective-permute-start.7 = (f32[2,128,128]{2,1,0:T(8,128)S(1)}, f32[2,128,128]{2,1,0:T(8,128)S(1)}, u32[]{:S(2)}, u32[]{:S(2)}) collective-permute-start(f32[2,128,128]{2,1,0:T(8,128)S(1)} %collective-permute-done.6.refs_0_), channel_id=1, source_target_pairs={{0,1},{1,0},{2,3},{3,2},{4,5},{5,4},{6,7},{7,6},{8,9},{9,8},{10,11... | collective-permute-start | bytes 393224 | tf_op jit(solution)/shard_map/ppermute | solution.py:228
  11.3 0.1 collective-permute-done.2
  11.4 1.3 %collective-permute-start.3 = (f32[2,128,128]{2,1,0:T(8,128)S(1)}, f32[2,128,128]{2,1,0:T(8,128)S(1)}, u32[]{:S(2)}, u32[]{:S(2)}) collective-permute-start(f32[2,128,128]{2,1,0:T(8,128)S(1)} %add.3.refs_0_.value), channel_id=1, source_target_pairs={{0,2},{1,3},{2,0},{3,1},{4,6},{5,7},{6,4},{7,5},{8,10},{9,11},{10,... | collective-permute-start | bytes 393224 | tf_op jit(solution)/shard_map/ppermute | solution.py:228
  12.7 0.0 collective-permute-done.7.refs_1_
  12.7 0.0 copy-done
  12.7 0.7 %shard_map.76 = (bf16[4,384,256]{2,1,0:T(8,128)(2,1)S(1)}, bf16[4,384,256]{2,1,0:T(8,128)(2,1)S(1)}) custom-call(s32[4,8,128]{2,1,0:T(8,128)S(1)} %get-tuple-element.17.kinds, f32[4,2,128,128]{3,2,1,0:T(8,128)S(1)} %copy-done, f32[2,128,128]{2,1,0:T(8,128)S(1)} %bitcast.13, f32[2,128,128]{2,1,0:T(8,128)S(1)} %get-tuple-element.18.combined, ...), custom_call_target="tpu_custom_call" | custom-call | flops 1000000000 | bytes 1327104 | tf_op jit(solution)/shard_map/pallas_call | solution.py:213
  13.4 0.7 %shard_map.77.after.refs_4_ = f32[2,128,128]{2,1,0:T(8,128)S(1)} custom-call(f32[2,128,128]{2,1,0:T(8,128)S(1)} %add.3.refs_0_.value, bf16[4,384,256]{2,1,0:T(8,128)(2,1)S(1)} %get-tuple-element.21.refs_1_.refs_2_, bf16[4,384,256]{2,1,0:T(8,128)(2,1)S(1)} %get-tuple-element.22.refs_2_.refs_3_), custom_call_target="tpu_custom_call" | custom-call | flops 1000000000 | bytes 1703936 | tf_op jit(solution)/shard_map/pallas_call | solution.py:213
  14.1 2.6 %collective-permute-start.9 = (f32[2,128,128]{2,1,0:T(8,128)S(1)}, f32[2,128,128]{2,1,0:T(8,128)S(1)}, u32[]{:S(2)}, u32[]{:S(2)}) collective-permute-start(f32[2,128,128]{2,1,0:T(8,128)S(1)} %shard_map.78.after), channel_id=1, source_target_pairs={{0,1},{1,0},{2,3},{3,2},{4,5},{5,4},{6,7},{7,6},{8,9},{9,8},{10,11... | collective-permute-start | bytes 393224 | tf_op jit(solution)/shard_map/ppermute | solution.py:228
  16.8 0.0 collective-permute-done.3.value
  16.8 2.5 %collective-permute-start.8 = (f32[2,128,128]{2,1,0:T(8,128)S(1)}, f32[2,128,128]{2,1,0:T(8,128)S(1)}, u32[]{:S(2)}, u32[]{:S(2)}) collective-permute-start(f32[2,128,128]{2,1,0:T(8,128)S(1)} %shard_map.79.refs_1_), channel_id=1, source_target_pairs={{0,1},{1,0},{2,3},{3,2},{4,5},{5,4},{6,7},{7,6},{8,9},{9,8},{10,11... | collective-permute-start | bytes 393224 | tf_op jit(solution)/shard_map/ppermute | solution.py:228
  19.3 0.0 collective-permute-done.9.refs_0_
  19.3 0.7 %shard_map.80.refs_3_ = f32[2,128,128]{2,1,0:T(8,128)S(1)} custom-call(f32[2,128,128]{2,1,0:T(8,128)S(1)} %collective-permute-done.9.refs_0_, f32[2,128,128]{2,1,0:T(8,128)S(1)} %shard_map.79.refs_1_, bf16[4,384,256]{2,1,0:T(8,128)(2,1)S(1)} %get-tuple-element.21.refs_1_.refs_2_, bf16[4,384,256]{2,1,0:T(8,128)(2,1)S(1)} %get-tuple-element.22.refs_2_.refs_3_, ...), custom_call_target="tpu_custom_call" | custom-call | flops 1000000000 | bytes 1966080 | tf_op jit(solution)/shard_map/pallas_call | solution.py:213
  19.9 0.3 %collective-permute-done.8.refs_0_ = f32[2,128,128]{2,1,0:T(8,128)S(1)} collective-permute-done((f32[2,128,128]{2,1,0:T(8,128)S(1)}, f32[2,128,128]{2,1,0:T(8,128)S(1)}, u32[]{:S(2)}, u32[]{:S(2)}) %collective-permute-start.8) | collective-permute-done | bytes 131104 | tf_op jit(solution)/shard_map/ppermute | solution.py:228
  20.2 1.1 %shard_map.81 = f32[2,128,128]{2,1,0:T(8,128)} custom-call(f32[2,128,128]{2,1,0:T(8,128)S(1)} %collective-permute-done.8.refs_0_, bf16[4,384,256]{2,1,0:T(8,128)(2,1)S(1)} %get-tuple-element.21.refs_1_.refs_2_, bf16[4,384,256]{2,1,0:T(8,128)(2,1)S(1)} %get-tuple-element.22.refs_2_.refs_3_, f32[2,128,128]{2,1,0:T(8,128)S(1)} %shard_map.80.refs_3_), custom_call_target="tpu_custom_call" | custom-call | flops 1000000000 | bytes 1835008 | tf_op jit(solution)/shard_map/pallas_call | solution.py:213
  (3 shorter events, 0.0 us)
Async XLA Ops:
  0.0 4.8 %collective-permute-start.4 = (f32[2,128,128]{2,1,0:T(8,128)}, f32[2,128,128]{2,1,0:T(8,128)S(1)}, u32[]{:S(2)}, u32[]{:S(2)}) collective-permute-start(f32[2,128,128]{2,1,0:T(8,128)} %bitcast.11), channel_id=1, source_target_pairs={{0,1},{1,0},{2,3},{3,2},{4,5},{5,4},{6,7},{7,6},{8,9},{9,8},{10,11... | collective-permute-start | bytes 393224 | tf_op jit(solution)/shard_map/ppermute | solution.py:228
  0.1 4.1 %copy-start.4 = (s32[8]{0:T(128)S(1)}, s32[8]{0:T(128)}, u32[]{:S(2)}) copy-start(s32[8]{0:T(128)} %offsets.1) | copy-start | bytes 100
  0.1 4.1 %copy-start.5 = (f32[8]{0:T(128)S(1)}, f32[8]{0:T(128)}, u32[]{:S(2)}) copy-start(f32[8]{0:T(128)} %weights.1) | copy-start | bytes 100
  0.1 4.1 %copy-start.6 = (s32[4]{0:T(128)S(1)}, s32[4]{0:T(128)}, u32[]{:S(2)}) copy-start(s32[4]{0:T(128)} %material.1) | copy-start | bytes 52
  0.1 4.7 %collective-permute-start.5 = (f32[2,128,128]{2,1,0:T(8,128)}, f32[2,128,128]{2,1,0:T(8,128)S(1)}, u32[]{:S(2)}, u32[]{:S(2)}) collective-permute-start(f32[2,128,128]{2,1,0:T(8,128)} %bitcast.6), channel_id=1, source_target_pairs={{0,1},{1,0},{2,3},{3,2},{4,5},{5,4},{6,7},{7,6},{8,9},{9,8},{10,11... | collective-permute-start | bytes 393224 | tf_op jit(solution)/shard_map/ppermute | solution.py:228
  0.5 4.3 %copy-start.1 = (f32[2,1,128,128]{3,2,1,0:T(8,128)S(1)}, f32[2,1,128,128]{3,2,1,0:T(8,128)}, u32[]{:S(2)}) copy-start(f32[2,1,128,128]{3,2,1,0:T(8,128)} %param.9) | copy-start | bytes 393220
  0.5 4.3 %copy-start.3 = (f32[2,1,1,128,128]{4,3,2,1,0:T(8,128)S(1)}, f32[2,1,1,128,128]{4,3,2,1,0:T(8,128)}, u32[]{:S(2)}) copy-start(f32[2,1,1,128,128]{4,3,2,1,0:T(8,128)} %param.8) | copy-start | bytes 393220
  0.5 6.1 %collective-permute-start = (f32[2,128,128]{2,1,0:T(8,128)}, f32[2,128,128]{2,1,0:T(8,128)S(1)}, u32[]{:S(2)}, u32[]{:S(2)}) collective-permute-start(f32[2,128,128]{2,1,0:T(8,128)} %bitcast.8), channel_id=1, source_target_pairs={{0,8},{4,12},{8,0},{12,4},{16,24},{20,28},{24,16},{28,20},{1,9},{5... | collective-permute-start | bytes 393224 | tf_op jit(solution)/shard_map/ppermute | solution.py:246
  2.9 4.5 %collective-permute-start.1 = (f32[2,128,128]{2,1,0:T(8,128)}, f32[2,128,128]{2,1,0:T(8,128)S(1)}, u32[]{:S(2)}, u32[]{:S(2)}) collective-permute-start(f32[2,128,128]{2,1,0:T(8,128)} %bitcast.9), channel_id=1, source_target_pairs={{0,4},{4,0},{8,16},{12,20},{16,8},{20,12},{24,28},{28,24},{1,5},{5... | collective-permute-start | bytes 393224 | tf_op jit(solution)/shard_map/ppermute | solution.py:247
  4.8 2.6 %copy-start.2 = (f32[2,1,1,128,128]{4,3,2,1,0:T(8,128)S(1)}, f32[2,1,1,128,128]{4,3,2,1,0:T(8,128)}, u32[]{:S(2)}) copy-start(f32[2,1,1,128,128]{4,3,2,1,0:T(8,128)} %param.7) | copy-start | bytes 393220
  5.3 7.4 %copy-start = (f32[4,2,128,128]{3,2,1,0:T(8,128)S(1)}, f32[4,2,128,128]{3,2,1,0:T(8,128)}, u32[]{:S(2)}) copy-start(f32[4,2,128,128]{3,2,1,0:T(8,128)} %table.1) | copy-start | bytes 1572868
  5.3 3.9 %collective-permute-start.6 = (f32[2,128,128]{2,1,0:T(8,128)S(1)}, f32[2,128,128]{2,1,0:T(8,128)S(1)}, u32[]{:S(2)}, u32[]{:S(2)}) collective-permute-start(f32[2,128,128]{2,1,0:T(8,128)S(1)} %get-tuple-element.20), channel_id=1, source_target_pairs={{0,2},{1,3},{2,0},{3,1},{4,6},{5,7},{6,4},{7,5},{8,10},{9,11},{10,... | collective-permute-start | bytes 393224 | tf_op jit(solution)/shard_map/ppermute | solution.py:228
  7.5 3.9 %collective-permute-start.2 = (f32[2,128,128]{2,1,0:T(8,128)S(1)}, f32[2,128,128]{2,1,0:T(8,128)S(1)}, u32[]{:S(2)}, u32[]{:S(2)}) collective-permute-start(f32[2,128,128]{2,1,0:T(8,128)S(1)} %get-tuple-element.16), channel_id=1, source_target_pairs={{0,4},{4,0},{8,12},{12,8},{16,20},{20,16},{24,28},{28,24},{1,5},{5... | collective-permute-start | bytes 393224 | tf_op jit(solution)/shard_map/ppermute | solution.py:271
  9.2 3.5 %collective-permute-start.7 = (f32[2,128,128]{2,1,0:T(8,128)S(1)}, f32[2,128,128]{2,1,0:T(8,128)S(1)}, u32[]{:S(2)}, u32[]{:S(2)}) collective-permute-start(f32[2,128,128]{2,1,0:T(8,128)S(1)} %collective-permute-done.6.refs_0_), channel_id=1, source_target_pairs={{0,1},{1,0},{2,3},{3,2},{4,5},{5,4},{6,7},{7,6},{8,9},{9,8},{10,11... | collective-permute-start | bytes 393224 | tf_op jit(solution)/shard_map/ppermute | solution.py:228
  11.4 5.3 %collective-permute-start.3 = (f32[2,128,128]{2,1,0:T(8,128)S(1)}, f32[2,128,128]{2,1,0:T(8,128)S(1)}, u32[]{:S(2)}, u32[]{:S(2)}) collective-permute-start(f32[2,128,128]{2,1,0:T(8,128)S(1)} %add.3.refs_0_.value), channel_id=1, source_target_pairs={{0,2},{1,3},{2,0},{3,1},{4,6},{5,7},{6,4},{7,5},{8,10},{9,11},{10,... | collective-permute-start | bytes 393224 | tf_op jit(solution)/shard_map/ppermute | solution.py:228
  14.1 5.1 %collective-permute-start.9 = (f32[2,128,128]{2,1,0:T(8,128)S(1)}, f32[2,128,128]{2,1,0:T(8,128)S(1)}, u32[]{:S(2)}, u32[]{:S(2)}) collective-permute-start(f32[2,128,128]{2,1,0:T(8,128)S(1)} %shard_map.78.after), channel_id=1, source_target_pairs={{0,1},{1,0},{2,3},{3,2},{4,5},{5,4},{6,7},{7,6},{8,9},{9,8},{10,11... | collective-permute-start | bytes 393224 | tf_op jit(solution)/shard_map/ppermute | solution.py:228
  16.8 3.5 %collective-permute-start.8 = (f32[2,128,128]{2,1,0:T(8,128)S(1)}, f32[2,128,128]{2,1,0:T(8,128)S(1)}, u32[]{:S(2)}, u32[]{:S(2)}) collective-permute-start(f32[2,128,128]{2,1,0:T(8,128)S(1)} %shard_map.79.refs_1_), channel_id=1, source_target_pairs={{0,1},{1,0},{2,3},{3,2},{4,5},{5,4},{6,7},{7,6},{8,9},{9,8},{10,11... | collective-permute-start | bytes 393224 | tf_op jit(solution)/shard_map/ppermute | solution.py:228

commit v5 on v4

--- a/solution.py
+++ b/solution.py
@@ -86,18 +86,17 @@
     return mine + side_a * group, mine - side_a * group, has_a, has_b
 
 
-def matchings(places, group):
+def matchings(places, group, slabs):
     result = []
     for first in (0, 1):
         pairs = []
         for place in range(places):
             other = place + 1 if place % 2 == first else place - 1
             for rank in range(group):
-                mine = place * group + rank
-                if 0 <= other < places:
-                    pairs.append((mine, other * group + rank))
-                elif group % 2 == 0:
-                    pairs.append((mine, mine ^ 1))
+                for slab in range(slabs):
+                    mine = (place * group + rank) * slabs + slab
+                    inside = 0 <= other < places
+                    pairs.append((mine, (other * group + rank) * slabs + slab if inside else mine ^ 1))
         result.append(pairs)
     return result
 
@@ -120,7 +119,7 @@
 def factor_kernel(count, kinds, table, own_r, combined, own_first_c, *refs):
     pairs = count // 2
     sent, crossed, first_c = (refs[n * (pairs - 1) : (n + 1) * (pairs - 1)] for n in range(3))
-    *outs, held, base = refs[3 * (pairs - 1) :]
+    field, *outs, state, field_out, held, base = refs[3 * (pairs - 1) :]
     mine = lax.axis_index("space")
     odd = mine % 2 == 1
     size = table.shape[-1]
@@ -175,38 +174,42 @@
         return _
 
     lax.fori_loop(1, mine // 2 + 1, earlier, 0)
-
-
-def pass_kernel(value, after, out):
-    out[...] = value[...]
-
-
-def field_kernel(count, slots, has_state, *refs):
-    fields, (high, low), rest = refs[: len(slots)], refs[len(slots) : len(slots) + 2], refs[len(slots) + 2 :]
-    out = rest[-1]
+    field_out[...] = field[...]
+    add_fields(count, {0: field}, outs, None, state)
+
+
+def add_fields(count, fields, factors, before, out, wanted=lambda slot, device: True):
     size = out.shape[-1]
     mine = lax.axis_index("space")
 
     def run(present):
-        total = rows(rest[0]) if has_state else jnp.zeros((size, 2 * size), F32)
-        for slot, field, terms in zip(slots, fields, present):
-            if not terms:
-                continue
-            factors = [part[slot, : terms * size] for part in (high, low)]
-            left = split(times(factors, field))
+        total = jnp.zeros((size, 2 * size), F32) if before is None else rows(before)
+        for slot, terms in present:
+            maps = [part[slot, : terms * size] for part in factors]
+            left = split(times(maps, fields[slot]))
             for term in range(terms):
                 here = slice(term * size, (term + 1) * size)
-                total = total + product([p[here] for p in left], [full(f[here]) for f in factors], NT)
+                total = total + product([p[here] for p in left], [full(m[here]) for m in maps], NT)
         out[...] = block_of(total)
 
     cases = {}
     for device in range(count):
-        present = tuple(sum(map(bool, valid_terms(device ^ slot, device, count))) for slot in slots)
+        terms = {slot: sum(map(bool, valid_terms(device ^ slot, device, count))) for slot in fields}
+        present = tuple((slot, number) for slot, number in terms.items() if number and wanted(slot, device))
         cases.setdefault(present, []).append(device)
     for present, devices in cases.items():
-        pl.when(functools.reduce(jnp.logical_or, [mine == device for device in devices]))(
-            functools.partial(run, present)
-        )
+        here = functools.reduce(jnp.logical_or, [mine == device for device in devices])
+        pl.when(here)(functools.partial(run, present))
+
+
+def first_kernel(count, arrived, other, high, low, before, arrived_out, out):
+    arrived_out[...] = arrived[...]
+    add_fields(count, {1: other}, (high, low), before, out, lambda slot, device: device % 2 == 1)
+
+
+def field_kernel(count, slots, high, low, before, *refs):
+    fields = dict(zip(slots, refs))
+    add_fields(count, fields, (high, low), before, refs[-1], lambda slot, device: slot != 1 or device % 2 == 0)
 
 
 def call(kernel, shapes, specs, *args, scratch=()):
@@ -242,9 +245,9 @@
     own = lesser_prev.reshape(2, size, size)
     chip_bits = [1 << b for b in range(1, slabs.bit_length() - 1)]
 
-    pairs_a, pairs_b = matchings(energies // group, group)
-    other_a = lax.ppermute(own, "energy", pairs_a)
-    other_b = lax.ppermute(own, "energy", pairs_b)
+    pairs_a, pairs_b = matchings(energies // group, group, slabs)
+    other_a = lax.ppermute(own, ("energy", "space"), pairs_a)
+    other_b = lax.ppermute(own, ("energy", "space"), pairs_b)
     retarded = retarded.reshape(2, size, size)
     coupling = coupling.reshape(2, size, size)
     shares, kinds = call(
@@ -272,28 +275,29 @@
         field = field + arrived
 
     factor_shape = jax.ShapeDtypeStruct((slabs, 3 * size, 2 * size), BF16)
-    factors = call(
-        functools.partial(factor_kernel, slabs), [factor_shape] * 2,
-        [VMEM] * (5 + len(earlier)), kinds, gradient_table, retarded, combined, first_c, *earlier,
+    *factors, state, own = call(
+        functools.partial(factor_kernel, slabs), [factor_shape] * 2 + [block] * 2,
+        [VMEM] * (6 + len(earlier)), kinds, gradient_table, retarded, combined, first_c, *earlier, field,
         scratch=[pltpu.VMEM((max(slabs // 2 - 1, 1), 3, 2, size, size), F32), pltpu.VMEM((size, 2 * size), F32)],
     )
 
-    def propagate(slots, fields, *state):
-        kernel = functools.partial(field_kernel, slabs, slots, bool(state))
-        operands = *[fields[slot] for slot in slots], *factors, *state
-        return call(kernel, block, [VMEM] * len(operands), *operands)
-
-    fields = {0: field}
-    state = propagate([0], fields)
-    own = call(pass_kernel, block, [VMEM] * 2, field, state)
-    fields[1] = exchange(own, 1)
+    def propagate(slots):
+        operands = *factors, state, *[fields[slot] for slot in slots]
+        return call(functools.partial(field_kernel, slabs, slots), block, [VMEM] * len(operands), *operands)
+
+    fields = {0: field, 1: exchange(own, 1)}
     for bit in chip_bits:
         for key in [key for key in fields if key % 2 == 0]:
-            fields[key ^ bit] = call(pass_kernel, block, [VMEM] * 2, exchange(fields[key], bit), own)
+            fields[key ^ bit] = exchange(fields[key], bit)
+            if bit == chip_bits[0]:
+                fields[bit], state = call(
+                    functools.partial(first_kernel, slabs), [block] * 2, [VMEM] * 5,
+                    fields[bit], fields[1], *factors, state,
+                )
     others = [key for key in sorted(fields) if key % 2 == 0 and key]
     fields |= gather({key: fields[key] for key in others}, [1])
-    state = propagate([1] + others, fields, state)
-    state = propagate([key ^ 1 for key in others], fields, state)
+    state = propagate([1] + others)
+    state = propagate([key ^ 1 for key in others])
     return state.reshape(lesser_prev.shape)
 
 

time: 21.5 us -> 21 us (0.977)
  the two profiles are of different devices: /device:TPU:1 before, /device:TPU:21 now
where the time goes in v5:
time: 21 us; the launch traced here: 20.8 us
  starting transfers between devices  9 us (43%)
  Pallas kernels  6.77 us (32%)
  waiting for transfers between devices  4.89 us (23%)
    pallas_call x7, Pallas kernels, call(): pl.pallas_call(kernel, out_shape=shapes, in_specs=specs, out_specs=jax.tr...  6.77 us
    ppermute x7, starting transfers between devices, exchange(): return lax.ppermute(value, 'space', [(i, i ^ bit) for i in range(count)])  6.41 us
    ppermute x1, waiting for transfers between devices, per_device(): other_a = lax.ppermute(own, ('energy', 'space'), pairs_a)  2.07 us
    ppermute x1, starting transfers between devices, per_device(): other_a = lax.ppermute(own, ('energy', 'space'), pairs_a)  1.31 us
    ppermute x1, starting transfers between devices, per_device(): arrived = lax.ppermute(sums[step], 'energy', pairs)  1.28 us
    ppermute x7, waiting for transfers between devices, exchange(): return lax.ppermute(value, 'space', [(i, i ^ bit) for i in range(count)])  1.1 us
    ppermute x1, waiting for transfers between devices, per_device(): other_b = lax.ppermute(own, ('energy', 'space'), pairs_b)  0.98 us
    ppermute x1, waiting for transfers between devices, per_device(): arrived = lax.ppermute(sums[step], 'energy', pairs)  0.74 us
  transfers between devices with their start and end apart: 10, of which 5 were waited for; matrix products, arithmetic and copies ran while one was open for 0% of the time, Pallas kernels for 22%

profile of v5, /device:TPU:21, one launch (start us, length us, event | category | flops | bytes accessed | tf_op | source)
XLA Modules:
  0.0 20.8 jit_solution(5665663953654190045)
XLA Ops:
  0.0 0.7 %collective-permute-start = (f32[2,128,128]{2,1,0:T(8,128)}, f32[2,128,128]{2,1,0:T(8,128)S(1)}, u32[]{:S(2)}, u32[]{:S(2)}) collective-permute-start(f32[2,128,128]{2,1,0:T(8,128)} %bitcast.11), channel_id=1, source_target_pairs={{0,1},{1,0},{2,3},{3,2},{4,5},{5,4},{6,7},{7,6},{8,9},{9,8},{10,11... | collective-permute-start | bytes 393224 | tf_op jit(solution)/shard_map/ppermute | solution.py:231
  0.7 0.0 copy-start.4
  0.7 0.0 copy-start.5
  0.7 0.0 copy-start.6
  0.7 0.1 collective-permute-start.1
  0.8 0.0 copy-start.1
  0.8 0.0 copy-start.3
  0.8 1.3 %collective-permute-start.4 = (f32[2,128,128]{2,1,0:T(8,128)}, f32[2,128,128]{2,1,0:T(8,128)S(1)}, u32[]{:S(2)}, u32[]{:S(2)}) collective-permute-start(f32[2,128,128]{2,1,0:T(8,128)} %bitcast.8), channel_id=1, source_target_pairs={{0,8},{1,9},{2,10},{3,11},{4,12},{5,13},{6,14},{7,15},{8,0},{9,1},... | collective-permute-start | bytes 393224 | tf_op jit(solution)/shard_map/ppermute | solution.py:249
  2.1 0.0 collective-permute-start.5
  2.1 0.0 copy-done.4
  2.1 0.0 copy-done.5
  2.1 0.0 copy-done.6
  2.1 0.6 %shard_map.73 = (f32[2,3,8,128]{3,2,1,0:T(8,128)S(1)}, s32[4,8,128]{2,1,0:T(8,128)S(1)}) custom-call(s32[8]{0:T(128)S(1)} %copy-done.4, f32[8]{0:T(128)S(1)} %copy-done.5, s32[4]{0:T(128)S(1)} %copy-done.6), custom_call_target="tpu_custom_call" | custom-call | flops 1000000000 | bytes 80 | tf_op jit(solution)/shard_map/pallas_call | solution.py:216
  2.7 0.0 collective-permute-done.other_r
  2.8 0.0 collective-permute-done.1.other_c
  2.8 0.0 copy-done.1
  2.8 0.0 copy-done.3
  2.8 0.0 copy-start.2
  2.8 0.5 %shard_map.74 = (f32[2,128,128]{2,1,0:T(8,128)S(1)}, f32[2,128,128]{2,1,0:T(8,128)S(1)}, f32[2,128,128]{2,1,0:T(8,128)S(1)}) custom-call(f32[2,128,128]{2,1,0:T(8,128)S(1)} %bitcast.12, f32[2,128,128]{2,1,0:T(8,128)S(1)} %bitcast.7, f32[2,128,128]{2,1,0:T(8,128)S(1)} %collective-permute-done.other_r, f32[2,128,128]{2,1,0:T(8,128)S(1)} %collective-permute-done.1.other_c, ...), custom_call_target="tpu_custom_call" | custom-call | flops 1000000000 | bytes 548864 | tf_op jit(solution)/shard_map/pallas_call | solution.py:216
  3.3 0.0 copy-start
  3.3 0.3 %collective-permute-start.2 = (f32[2,128,128]{2,1,0:T(8,128)S(1)}, f32[2,128,128]{2,1,0:T(8,128)S(1)}, u32[]{:S(2)}, u32[]{:S(2)}) collective-permute-start(f32[2,128,128]{2,1,0:T(8,128)S(1)} %get-tuple-element.22), channel_id=1, source_target_pairs={{0,2},{1,3},{2,0},{3,1},{4,6},{5,7},{6,4},{7,5},{8,10},{9,11},{10,... | collective-permute-start | bytes 393224 | tf_op jit(solution)/shard_map/ppermute | solution.py:231
  3.6 2.1 %collective-permute-done.4.other_a = f32[2,128,128]{2,1,0:T(8,128)S(1)} collective-permute-done((f32[2,128,128]{2,1,0:T(8,128)}, f32[2,128,128]{2,1,0:T(8,128)S(1)}, u32[]{:S(2)}, u32[]{:S(2)}) %collective-permute-start.4) | collective-permute-done | bytes 131104 | tf_op jit(solution)/shard_map/ppermute | solution.py:249
  5.6 1.0 %collective-permute-done.5.other_b = f32[2,128,128]{2,1,0:T(8,128)S(1)} collective-permute-done((f32[2,128,128]{2,1,0:T(8,128)}, f32[2,128,128]{2,1,0:T(8,128)S(1)}, u32[]{:S(2)}, u32[]{:S(2)}) %collective-permute-start.5) | collective-permute-done | bytes 131104 | tf_op jit(solution)/shard_map/ppermute | solution.py:250
  6.6 0.0 copy-done.2
  6.6 0.1 shard_map.75
  6.7 1.3 %collective-permute-start.6 = (f32[2,128,128]{2,1,0:T(8,128)S(1)}, f32[2,128,128]{2,1,0:T(8,128)S(1)}, u32[]{:S(2)}, u32[]{:S(2)}) collective-permute-start(f32[2,128,128]{2,1,0:T(8,128)S(1)} %get-tuple-element.24), channel_id=1, source_target_pairs={{0,4},{4,0},{8,12},{12,8},{16,20},{20,16},{24,28},{28,24},{1,5},{5... | collective-permute-start | bytes 393224 | tf_op jit(solution)/shard_map/ppermute | solution.py:274
  8.0 0.0 collective-permute-done.2.refs_0_
  8.0 1.9 %collective-permute-start.3 = (f32[2,128,128]{2,1,0:T(8,128)S(1)}, f32[2,128,128]{2,1,0:T(8,128)S(1)}, u32[]{:S(2)}, u32[]{:S(2)}) collective-permute-start(f32[2,128,128]{2,1,0:T(8,128)S(1)} %collective-permute-done.2.refs_0_), channel_id=1, source_target_pairs={{0,1},{1,0},{2,3},{3,2},{4,5},{5,4},{6,7},{7,6},{8,9},{9,8},{10,11... | collective-permute-start | bytes 393224 | tf_op jit(solution)/shard_map/ppermute | solution.py:231
  9.8 0.7 %collective-permute-done.6 = f32[2,128,128]{2,1,0:T(8,128)S(1)} collective-permute-done((f32[2,128,128]{2,1,0:T(8,128)S(1)}, f32[2,128,128]{2,1,0:T(8,128)S(1)}, u32[]{:S(2)}, u32[]{:S(2)}) %collective-permute-start.6) | collective-permute-done | bytes 131104 | tf_op jit(solution)/shard_map/ppermute | solution.py:274
  10.6 0.3 %collective-permute-start.7 = (f32[2,128,128]{2,1,0:T(8,128)S(1)}, f32[2,128,128]{2,1,0:T(8,128)S(1)}, u32[]{:S(2)}, u32[]{:S(2)}) collective-permute-start(f32[2,128,128]{2,1,0:T(8,128)S(1)} %add.3.refs_3_), channel_id=1, source_target_pairs={{0,2},{1,3},{2,0},{3,1},{4,6},{5,7},{6,4},{7,5},{8,10},{9,11},{10,... | collective-permute-start | bytes 393224 | tf_op jit(solution)/shard_map/ppermute | solution.py:231
  10.9 0.0 collective-permute-done.3.refs_1_
  10.9 0.0 copy-done
  10.9 2.4 %shard_map.76 = (bf16[4,384,256]{2,1,0:T(8,128)(2,1)S(1)}, bf16[4,384,256]{2,1,0:T(8,128)(2,1)S(1)}, f32[2,128,128]{2,1,0:T(8,128)S(1)}, f32[2,128,128]{2,1,0:T(8,128)S(1)}) custom-call(s32[4,8,128]{2,1,0:T(8,128)S(1)} %get-tuple-element.18.kinds, f32[4,2,128,128]{3,2,1,0:T(8,128)S(1)} %copy-done, f32[2,128,128]{2,1,0:T(8,128)S(1)} %bitcast.13, ...), custom_call_target="tpu_custom_call" | custom-call | flops 1000000000 | bytes 1458176 | tf_op jit(solution)/shard_map/pallas_call | solution.py:216
  13.3 2.8 %collective-permute-start.8 = (f32[2,128,128]{2,1,0:T(8,128)S(1)}, f32[2,128,128]{2,1,0:T(8,128)S(1)}, u32[]{:S(2)}, u32[]{:S(2)}) collective-permute-start(f32[2,128,128]{2,1,0:T(8,128)S(1)} %get-tuple-element.27), channel_id=1, source_target_pairs={{0,1},{1,0},{2,3},{3,2},{4,5},{5,4},{6,7},{7,6},{8,9},{9,8},{10,11... | collective-permute-start | bytes 393224 | tf_op jit(solution)/shard_map/ppermute | solution.py:231
  16.1 0.0 collective-permute-done.7.arrived
  16.1 1.0 %collective-permute-done.8.other.refs_0_ = f32[2,128,128]{2,1,0:T(8,128)S(1)} collective-permute-done((f32[2,128,128]{2,1,0:T(8,128)S(1)}, f32[2,128,128]{2,1,0:T(8,128)S(1)}, u32[]{:S(2)}, u32[]{:S(2)}) %collective-permute-start.8) | collective-permute-done | bytes 131104 | tf_op jit(solution)/shard_map/ppermute | solution.py:231
  17.1 0.9 %shard_map.77 = (f32[2,128,128]{2,1,0:T(8,128)S(1)}, f32[2,128,128]{2,1,0:T(8,128)S(1)}) custom-call(f32[2,128,128]{2,1,0:T(8,128)S(1)} %collective-permute-done.7.arrived, f32[2,128,128]{2,1,0:T(8,128)S(1)} %collective-permute-done.8.other.refs_0_, bf16[4,384,256]{2,1,0:T(8,128)(2,1)S(1)} %get-tuple-element.25.high, ...), custom_call_target="tpu_custom_call" | custom-call | flops 1000000000 | bytes 1966080 | tf_op jit(solution)/shard_map/pallas_call | solution.py:216
  18.1 0.4 %collective-permute-start.9 = (f32[2,128,128]{2,1,0:T(8,128)S(1)}, f32[2,128,128]{2,1,0:T(8,128)S(1)}, u32[]{:S(2)}, u32[]{:S(2)}) collective-permute-start(f32[2,128,128]{2,1,0:T(8,128)S(1)} %get-tuple-element.30.refs_1_), channel_id=1, source_target_pairs={{0,1},{1,0},{2,3},{3,2},{4,5},{5,4},{6,7},{7,6},{8,9},{9,8},{10,11... | collective-permute-start | bytes 393224 | tf_op jit(solution)/shard_map/ppermute | solution.py:231
  18.4 0.9 %shard_map.78.before = f32[2,128,128]{2,1,0:T(8,128)S(1)} custom-call(bf16[4,384,256]{2,1,0:T(8,128)(2,1)S(1)} %get-tuple-element.25.high, bf16[4,384,256]{2,1,0:T(8,128)(2,1)S(1)} %get-tuple-element.26.low, f32[2,128,128]{2,1,0:T(8,128)S(1)} %get-tuple-element.29.before, f32[2,128,128]{2,1,0:T(8,128)S(1)} %collective-permute-done.8.other.refs_0_, ...), custom_call_target="tpu_custom_call" | custom-call | flops 1000000000 | bytes 1966080 | tf_op jit(solution)/shard_map/pallas_call | solution.py:216
  19.4 0.1 collective-permute-done.9.refs_0_
  19.5 1.3 %shard_map.79 = f32[2,128,128]{2,1,0:T(8,128)} custom-call(bf16[4,384,256]{2,1,0:T(8,128)(2,1)S(1)} %get-tuple-element.25.high, bf16[4,384,256]{2,1,0:T(8,128)(2,1)S(1)} %get-tuple-element.26.low, f32[2,128,128]{2,1,0:T(8,128)S(1)} %shard_map.78.before, f32[2,128,128]{2,1,0:T(8,128)S(1)} %collective-permute-done.9.refs_0_), custom_call_target="tpu_custom_call" | custom-call | flops 1000000000 | bytes 1835008 | tf_op jit(solution)/shard_map/pallas_call | solution.py:216
  (1 shorter events, 0.0 us)
Async XLA Ops:
  0.0 2.7 %collective-permute-start = (f32[2,128,128]{2,1,0:T(8,128)}, f32[2,128,128]{2,1,0:T(8,128)S(1)}, u32[]{:S(2)}, u32[]{:S(2)}) collective-permute-start(f32[2,128,128]{2,1,0:T(8,128)} %bitcast.11), channel_id=1, source_target_pairs={{0,1},{1,0},{2,3},{3,2},{4,5},{5,4},{6,7},{7,6},{8,9},{9,8},{10,11... | collective-permute-start | bytes 393224 | tf_op jit(solution)/shard_map/ppermute | solution.py:231
  0.7 1.4 %copy-start.4 = (s32[8]{0:T(128)S(1)}, s32[8]{0:T(128)}, u32[]{:S(2)}) copy-start(s32[8]{0:T(128)} %offsets.1) | copy-start | bytes 100
  0.7 1.4 %copy-start.5 = (f32[8]{0:T(128)S(1)}, f32[8]{0:T(128)}, u32[]{:S(2)}) copy-start(f32[8]{0:T(128)} %weights.1) | copy-start | bytes 100
  0.7 1.4 %copy-start.6 = (s32[4]{0:T(128)S(1)}, s32[4]{0:T(128)}, u32[]{:S(2)}) copy-start(s32[4]{0:T(128)} %material.1) | copy-start | bytes 52
  0.7 2.1 %collective-permute-start.1 = (f32[2,128,128]{2,1,0:T(8,128)}, f32[2,128,128]{2,1,0:T(8,128)S(1)}, u32[]{:S(2)}, u32[]{:S(2)}) collective-permute-start(f32[2,128,128]{2,1,0:T(8,128)} %bitcast.6), channel_id=1, source_target_pairs={{0,1},{1,0},{2,3},{3,2},{4,5},{5,4},{6,7},{7,6},{8,9},{9,8},{10,11... | collective-permute-start | bytes 393224 | tf_op jit(solution)/shard_map/ppermute | solution.py:231
  0.8 2.0 %copy-start.1 = (f32[2,1,128,128]{3,2,1,0:T(8,128)S(1)}, f32[2,1,128,128]{3,2,1,0:T(8,128)}, u32[]{:S(2)}) copy-start(f32[2,1,128,128]{3,2,1,0:T(8,128)} %param.9) | copy-start | bytes 393220
  0.8 2.0 %copy-start.3 = (f32[2,1,1,128,128]{4,3,2,1,0:T(8,128)S(1)}, f32[2,1,1,128,128]{4,3,2,1,0:T(8,128)}, u32[]{:S(2)}) copy-start(f32[2,1,1,128,128]{4,3,2,1,0:T(8,128)} %param.8) | copy-start | bytes 393220
  0.8 4.9 %collective-permute-start.4 = (f32[2,128,128]{2,1,0:T(8,128)}, f32[2,128,128]{2,1,0:T(8,128)S(1)}, u32[]{:S(2)}, u32[]{:S(2)}) collective-permute-start(f32[2,128,128]{2,1,0:T(8,128)} %bitcast.8), channel_id=1, source_target_pairs={{0,8},{1,9},{2,10},{3,11},{4,12},{5,13},{6,14},{7,15},{8,0},{9,1},... | collective-permute-start | bytes 393224 | tf_op jit(solution)/shard_map/ppermute | solution.py:249
  2.1 4.5 %collective-permute-start.5 = (f32[2,128,128]{2,1,0:T(8,128)}, f32[2,128,128]{2,1,0:T(8,128)S(1)}, u32[]{:S(2)}, u32[]{:S(2)}) collective-permute-start(f32[2,128,128]{2,1,0:T(8,128)} %bitcast.9), channel_id=1, source_target_pairs={{0,1},{1,0},{2,3},{3,2},{4,5},{5,4},{6,7},{7,6},{8,16},{9,17},{10,... | collective-permute-start | bytes 393224 | tf_op jit(solution)/shard_map/ppermute | solution.py:250
  2.8 3.8 %copy-start.2 = (f32[2,1,1,128,128]{4,3,2,1,0:T(8,128)S(1)}, f32[2,1,1,128,128]{4,3,2,1,0:T(8,128)}, u32[]{:S(2)}) copy-start(f32[2,1,1,128,128]{4,3,2,1,0:T(8,128)} %param.7) | copy-start | bytes 393220
  3.3 7.6 %copy-start = (f32[4,2,128,128]{3,2,1,0:T(8,128)S(1)}, f32[4,2,128,128]{3,2,1,0:T(8,128)}, u32[]{:S(2)}) copy-start(f32[4,2,128,128]{3,2,1,0:T(8,128)} %table.1) | copy-start | bytes 1572868
  3.3 4.7 %collective-permute-start.2 = (f32[2,128,128]{2,1,0:T(8,128)S(1)}, f32[2,128,128]{2,1,0:T(8,128)S(1)}, u32[]{:S(2)}, u32[]{:S(2)}) collective-permute-start(f32[2,128,128]{2,1,0:T(8,128)S(1)} %get-tuple-element.22), channel_id=1, source_target_pairs={{0,2},{1,3},{2,0},{3,1},{4,6},{5,7},{6,4},{7,5},{8,10},{9,11},{10,... | collective-permute-start | bytes 393224 | tf_op jit(solution)/shard_map/ppermute | solution.py:231
  6.7 3.9 %collective-permute-start.6 = (f32[2,128,128]{2,1,0:T(8,128)S(1)}, f32[2,128,128]{2,1,0:T(8,128)S(1)}, u32[]{:S(2)}, u32[]{:S(2)}) collective-permute-start(f32[2,128,128]{2,1,0:T(8,128)S(1)} %get-tuple-element.24), channel_id=1, source_target_pairs={{0,4},{4,0},{8,12},{12,8},{16,20},{20,16},{24,28},{28,24},{1,5},{5... | collective-permute-start | bytes 393224 | tf_op jit(solution)/shard_map/ppermute | solution.py:274
  8.0 2.9 %collective-permute-start.3 = (f32[2,128,128]{2,1,0:T(8,128)S(1)}, f32[2,128,128]{2,1,0:T(8,128)S(1)}, u32[]{:S(2)}, u32[]{:S(2)}) collective-permute-start(f32[2,128,128]{2,1,0:T(8,128)S(1)} %collective-permute-done.2.refs_0_), channel_id=1, source_target_pairs={{0,1},{1,0},{2,3},{3,2},{4,5},{5,4},{6,7},{7,6},{8,9},{9,8},{10,11... | collective-permute-start | bytes 393224 | tf_op jit(solution)/shard_map/ppermute | solution.py:231
  10.6 5.6 %collective-permute-start.7 = (f32[2,128,128]{2,1,0:T(8,128)S(1)}, f32[2,128,128]{2,1,0:T(8,128)S(1)}, u32[]{:S(2)}, u32[]{:S(2)}) collective-permute-start(f32[2,128,128]{2,1,0:T(8,128)S(1)} %add.3.refs_3_), channel_id=1, source_target_pairs={{0,2},{1,3},{2,0},{3,1},{4,6},{5,7},{6,4},{7,5},{8,10},{9,11},{10,... | collective-permute-start | bytes 393224 | tf_op jit(solution)/shard_map/ppermute | solution.py:231
  13.3 3.8 %collective-permute-start.8 = (f32[2,128,128]{2,1,0:T(8,128)S(1)}, f32[2,128,128]{2,1,0:T(8,128)S(1)}, u32[]{:S(2)}, u32[]{:S(2)}) collective-permute-start(f32[2,128,128]{2,1,0:T(8,128)S(1)} %get-tuple-element.27), channel_id=1, source_target_pairs={{0,1},{1,0},{2,3},{3,2},{4,5},{5,4},{6,7},{7,6},{8,9},{9,8},{10,11... | collective-permute-start | bytes 393224 | tf_op jit(solution)/shard_map/ppermute | solution.py:231
  18.1 1.4 %collective-permute-start.9 = (f32[2,128,128]{2,1,0:T(8,128)S(1)}, f32[2,128,128]{2,1,0:T(8,128)S(1)}, u32[]{:S(2)}, u32[]{:S(2)}) collective-permute-start(f32[2,128,128]{2,1,0:T(8,128)S(1)} %get-tuple-element.30.refs_1_), channel_id=1, source_target_pairs={{0,1},{1,0},{2,3},{3,2},{4,5},{5,4},{6,7},{7,6},{8,9},{9,8},{10,11... | collective-permute-start | bytes 393224 | tf_op jit(solution)/shard_map/ppermute | solution.py:231

commit v6 on v5

--- a/solution.py
+++ b/solution.py
@@ -54,7 +54,10 @@
     count = lax.axis_size("energy")
     mine = lax.axis_index("energy")
     place, rank = mine // group, mine % group
-    source_a, source_b, has_a, has_b = partners(place, count // group, mine, group)
+    sources = [(mine, True)]
+    for lower in range(count // group - 1):
+        step = jnp.where(place == lower, group, -group)
+        sources.append((mine + step, (place == lower) | (place == lower + 1)))
 
     def coefficient(target, source, valid):
         total = jnp.float32(0)
@@ -64,59 +67,51 @@
 
     for step in range(group):
         target = place * group + (rank + step) % group
-        for index, (source, valid) in enumerate(((mine, True), (source_a, has_a), (source_b, has_b))):
+        for index, (source, valid) in enumerate(sources):
             out[step, index] = jnp.full(out.shape[2:], coefficient(target, source, valid), F32)
     for slab in range(material.shape[0]):
         kinds[slab] = jnp.full(kinds.shape[1:], material[slab], jnp.int32)
 
 
-def smear_kernel(group, shares, own, other_a, other_b, *outs):
-    shape = (-1,) + shares.shape[2:]
-    parts = [part[...].reshape(shape) for part in (own, other_a, other_b)]
+def smear_kernel(group, shares, *refs):
+    held, outs = refs[:-group], refs[-group:]
+    parts = [part[...].reshape((-1,) + shares.shape[2:]) for part in held]
     for step in range(group):
         total = sum(shares[step, index][None] * part for index, part in enumerate(parts))
         outs[step][...] = total.reshape(outs[step].shape)
 
 
-def partners(place, places, mine, group):
-    even = place % 2 == 0
-    side_a = jnp.where(even, 1, -1)
-    has_a = (place + side_a < places) & (place + side_a >= 0)
-    has_b = (place - side_a < places) & (place - side_a >= 0)
-    return mine + side_a * group, mine - side_a * group, has_a, has_b
-
-
 def matchings(places, group, slabs):
     result = []
-    for first in (0, 1):
+    for lower in range(places - 1):
         pairs = []
         for place in range(places):
-            other = place + 1 if place % 2 == first else place - 1
+            other = {lower: lower + 1, lower + 1: lower}.get(place)
             for rank in range(group):
                 for slab in range(slabs):
                     mine = (place * group + rank) * slabs + slab
-                    inside = 0 <= other < places
-                    pairs.append((mine, (other * group + rank) * slabs + slab if inside else mine ^ 1))
+                    pairs.append((mine, mine ^ 1 if other is None else (other * group + rank) * slabs + slab))
         result.append(pairs)
     return result
 
 
-def pair_kernel(own_r, own_c, other_r, other_c, after, combined, sent, first_c):
+def pair_kernel(own_r, own_c, other_r, after, sent):
     odd = lax.axis_index("space") % 2 == 1
-    first_r = jnp.where(odd, other_r[...], own_r[...])
-    second_r = jnp.where(odd, own_r[...], other_r[...])
-    second_c = jnp.where(odd, own_c[...], other_c[...])
-    first_c[...] = jnp.where(odd, other_c[...], own_c[...])
-    made = block_of(times(split(times(split(rows(second_r)), second_c)), first_r))
-    combined[...] = made
-    sent[...] = jnp.where(odd, own_r[...], made)
+
+    @pl.when(odd)
+    def _():
+        sent[...] = block_of(times(split(times(split(rows(own_r)), own_c)), other_r))
+
+    @pl.when(jnp.logical_not(odd))
+    def _():
+        sent[...] = other_r[...]
 
 
 def valid_terms(slab, mine, count):
     return slab <= mine, (slab >= 1) & (slab <= mine + 1), slab < mine
 
 
-def factor_kernel(count, kinds, table, own_r, combined, own_first_c, *refs):
+def factor_kernel(count, kinds, table, own_r, own_c, other_c, combined, *refs):
     pairs = count // 2
     sent, crossed, first_c = (refs[n * (pairs - 1) : (n + 1) * (pairs - 1)] for n in range(3))
     field, *outs, state, field_out, held, base = refs[3 * (pairs - 1) :]
@@ -125,8 +120,8 @@
     size = table.shape[-1]
     for slot in range(pairs - 1):
         here, there = sent[slot][...], crossed[slot][...]
-        held[slot, 0] = jnp.where(odd, there, here)
-        held[slot, 1] = jnp.where(odd, here, there)
+        held[slot, 0] = jnp.where(odd, here, there)
+        held[slot, 1] = jnp.where(odd, there, here)
         held[slot, 2] = first_c[slot][...]
 
     def store(slab, which, parts):
@@ -161,7 +156,7 @@
     @pl.when(mine >= 2)
     def _():
         start = split(jnp.where(odd, rows(combined), rows(own_r)))
-        base[...] = times(start, own_first_c)
+        base[...] = times(start, jnp.where(odd, other_c[...], own_c[...]))
 
     def earlier(step, _):
         pair = mine // 2 - step
@@ -245,20 +240,22 @@
     own = lesser_prev.reshape(2, size, size)
     chip_bits = [1 << b for b in range(1, slabs.bit_length() - 1)]
 
-    pairs_a, pairs_b = matchings(energies // group, group, slabs)
-    other_a = lax.ppermute(own, ("energy", "space"), pairs_a)
-    other_b = lax.ppermute(own, ("energy", "space"), pairs_b)
+    held = [own]
+    for pairs in matchings(energies // group, group, slabs):
+        held.append(lax.ppermute(own, ("energy", "space"), pairs))
     retarded = retarded.reshape(2, size, size)
     coupling = coupling.reshape(2, size, size)
     shares, kinds = call(
         functools.partial(share_kernel, group),
-        [jax.ShapeDtypeStruct((group, 3, 8, 128), F32), jax.ShapeDtypeStruct((slabs, 8, 128), jnp.int32)], [SMEM] * 3,
+        [jax.ShapeDtypeStruct((group, len(held), 8, 128), F32), jax.ShapeDtypeStruct((slabs, 8, 128), jnp.int32)], [SMEM] * 3,
         offsets, weights, material,
     )
-    combined, sent, first_c = call(
-        pair_kernel, [block] * 3, [VMEM] * 5, retarded, coupling, exchange(retarded, 1), exchange(coupling, 1), shares,
-    )
-    sent = gather({0: sent}, chip_bits)
+    other_c = exchange(coupling, 1)
+    combined = call(pair_kernel, block, [VMEM] * 4, retarded, coupling, exchange(retarded, 1), shares)
+    sent = gather({0: combined}, chip_bits)
+    first_c = coupling
+    if slabs > 4:
+        first_c = jnp.where(lax.axis_index("space") % 2 == 1, other_c, coupling)
     all_c = gather({0: first_c}, chip_bits) if slabs > 4 else {slot: first_c for slot in sent}
     others = [slot for slot in sorted(sent) if slot]
     earlier = (
@@ -266,7 +263,7 @@
         + [exchange(sent[slot], 1) for slot in others]
         + [all_c[slot] for slot in others]
     )
-    sums = call(functools.partial(smear_kernel, group), [block] * group, [VMEM] * 4, shares, own, other_a, other_b)
+    sums = call(functools.partial(smear_kernel, group), [block] * group, [VMEM] * (1 + len(held)), shares, *held)
 
     field = sums[0]
     for step in range(1, group):
@@ -277,7 +274,8 @@
     factor_shape = jax.ShapeDtypeStruct((slabs, 3 * size, 2 * size), BF16)
     *factors, state, own = call(
         functools.partial(factor_kernel, slabs), [factor_shape] * 2 + [block] * 2,
-        [VMEM] * (6 + len(earlier)), kinds, gradient_table, retarded, combined, first_c, *earlier, field,
+        [VMEM] * (7 + len(earlier)),
+        kinds, gradient_table, retarded, coupling, other_c, combined, *earlier, field,
         scratch=[pltpu.VMEM((max(slabs // 2 - 1, 1), 3, 2, size, size), F32), pltpu.VMEM((size, 2 * size), F32)],
     )
 

time: 21 us -> 20.3 us (0.967)
  the two profiles are of different devices: /device:TPU:21 before, /device:TPU:1 now
where the time goes in v6:
time: 20.3 us; the launch traced here: 20.2 us
  starting transfers between devices  11.4 us (56%)
  Pallas kernels  4.37 us (22%)
  waiting for transfers between devices  4.24 us (21%)
    ppermute x7, starting transfers between devices, exchange(): return lax.ppermute(value, 'space', [(i, i ^ bit) for i in range(count)])  6.84 us
    pallas_call x7, Pallas kernels, call(): pl.pallas_call(kernel, out_shape=shapes, in_specs=specs, out_specs=jax.tr...  4.37 us
    ppermute x3, starting transfers between devices, per_device(): held.append(lax.ppermute(own, ('energy', 'space'), pairs))  3.3 us
    ppermute x7, waiting for transfers between devices, exchange(): return lax.ppermute(value, 'space', [(i, i ^ bit) for i in range(count)])  2.46 us
    ppermute x1, starting transfers between devices, per_device(): arrived = lax.ppermute(sums[step], 'energy', pairs)  1.26 us
    ppermute x3, waiting for transfers between devices, per_device(): held.append(lax.ppermute(own, ('energy', 'space'), pairs))  0.97 us
    ppermute x1, waiting for transfers between devices, per_device(): arrived = lax.ppermute(sums[step], 'energy', pairs)  0.82 us
  transfers between devices with their start and end apart: 11, of which 5 were waited for; matrix products, arithmetic and copies ran while one was open for 0% of the time, Pallas kernels for 13%

profile of v6, /device:TPU:1, one launch (start us, length us, event | category | flops | bytes accessed | tf_op | source)
XLA Modules:
  0.0 20.2 jit_solution(5347623281291881086)
XLA Ops:
  0.0 0.0 copy-start.4
  0.0 0.0 copy-start.5
  0.0 0.0 copy-start.6
  0.0 0.1 collective-permute-start.1
  0.1 0.0 copy-start.2
  0.1 0.0 copy-start.3
  0.1 2.8 %collective-permute-start.4 = (f32[2,128,128]{2,1,0:T(8,128)}, f32[2,128,128]{2,1,0:T(8,128)S(1)}, u32[]{:S(2)}, u32[]{:S(2)}) collective-permute-start(f32[2,128,128]{2,1,0:T(8,128)} %bitcast.6), channel_id=1, source_target_pairs={{0,8},{1,9},{2,10},{3,11},{4,12},{5,13},{6,14},{7,15},{8,0},{9,1},... | collective-permute-start | bytes 393224 | tf_op jit(solution)/shard_map/ppermute | solution.py:245
  2.9 0.4 %collective-permute-start.5 = (f32[2,128,128]{2,1,0:T(8,128)}, f32[2,128,128]{2,1,0:T(8,128)S(1)}, u32[]{:S(2)}, u32[]{:S(2)}) collective-permute-start(f32[2,128,128]{2,1,0:T(8,128)} %bitcast.7), channel_id=1, source_target_pairs={{0,1},{1,0},{2,3},{3,2},{4,5},{5,4},{6,7},{7,6},{8,16},{9,17},{10,... | collective-permute-start | bytes 393224 | tf_op jit(solution)/shard_map/ppermute | solution.py:245
  3.3 0.2 collective-permute-start.6
  3.4 0.0 copy-done.4
  3.4 0.0 copy-done.5
  3.4 0.0 copy-done.6
  3.4 0.7 %shard_map.73 = (f32[2,4,8,128]{3,2,1,0:T(8,128)S(1)}, s32[4,8,128]{2,1,0:T(8,128)S(1)}) custom-call(s32[8]{0:T(128)S(1)} %copy-done.4, f32[8]{0:T(128)S(1)} %copy-done.5, s32[4]{0:T(128)S(1)} %copy-done.6), custom_call_target="tpu_custom_call" | custom-call | flops 1000000000 | bytes 80 | tf_op jit(solution)/shard_map/pallas_call | solution.py:211
  4.1 0.0 collective-permute-done.1.other_r
  4.1 0.0 copy-done.2
  4.1 0.0 copy-done.3
  4.1 0.0 copy-start.1
  4.1 0.5 %shard_map.74.combined = f32[2,128,128]{2,1,0:T(8,128)S(1)} custom-call(f32[2,128,128]{2,1,0:T(8,128)S(1)} %bitcast.11, f32[2,128,128]{2,1,0:T(8,128)S(1)} %bitcast.13, f32[2,128,128]{2,1,0:T(8,128)S(1)} %collective-permute-done.1.other_r, f32[2,4,8,128]{3,2,1,0:T(8,128)S(1)} %get-tuple-element.16.after.shares), custom_call_target="tpu_custom_call" | custom-call | flops 1000000000 | bytes 425984 | tf_op jit(solution)/shard_map/pallas_call | solution.py:211
  4.6 0.0 copy-start
  4.6 1.3 %collective-permute-start.2 = (f32[2,128,128]{2,1,0:T(8,128)S(1)}, f32[2,128,128]{2,1,0:T(8,128)S(1)}, u32[]{:S(2)}, u32[]{:S(2)}) collective-permute-start(f32[2,128,128]{2,1,0:T(8,128)S(1)} %shard_map.74.combined), channel_id=1, source_target_pairs={{0,2},{1,3},{2,0},{3,1},{4,6},{5,7},{6,4},{7,5},{8,10},{9,11},{10,... | collective-permute-start | bytes 393224 | tf_op jit(solution)/shard_map/ppermute | solution.py:226
  5.9 1.0 %collective-permute-done.4.refs_1_ = f32[2,128,128]{2,1,0:T(8,128)S(1)} collective-permute-done((f32[2,128,128]{2,1,0:T(8,128)}, f32[2,128,128]{2,1,0:T(8,128)S(1)}, u32[]{:S(2)}, u32[]{:S(2)}) %collective-permute-start.4) | collective-permute-done | bytes 131104 | tf_op jit(solution)/shard_map/ppermute | solution.py:245
  6.9 0.0 collective-permute-done.5.refs_2_
  6.9 0.0 collective-permute-done.6.refs_3_
  6.9 0.0 copy-done.1
  6.9 0.1 shard_map.75
  7.0 1.3 %collective-permute-start.7 = (f32[2,128,128]{2,1,0:T(8,128)S(1)}, f32[2,128,128]{2,1,0:T(8,128)S(1)}, u32[]{:S(2)}, u32[]{:S(2)}) collective-permute-start(f32[2,128,128]{2,1,0:T(8,128)S(1)} %get-tuple-element.18), channel_id=1, source_target_pairs={{0,4},{4,0},{8,12},{12,8},{16,20},{20,16},{24,28},{28,24},{1,5},{5... | collective-permute-start | bytes 393224 | tf_op jit(solution)/shard_map/ppermute | solution.py:271
  8.2 1.2 %collective-permute-start = (f32[2,128,128]{2,1,0:T(8,128)S(1)}, f32[2,128,128]{2,1,0:T(8,128)S(1)}, u32[]{:S(2)}, u32[]{:S(2)}) collective-permute-start(f32[2,128,128]{2,1,0:T(8,128)S(1)} %bitcast.14), channel_id=1, source_target_pairs={{0,1},{1,0},{2,3},{3,2},{4,5},{5,4},{6,7},{7,6},{8,9},{9,8},{10,11... | collective-permute-start | bytes 393224 | tf_op jit(solution)/shard_map/ppermute | solution.py:226
  9.4 0.5 %collective-permute-done.2.refs_0_ = f32[2,128,128]{2,1,0:T(8,128)S(1)} collective-permute-done((f32[2,128,128]{2,1,0:T(8,128)S(1)}, f32[2,128,128]{2,1,0:T(8,128)S(1)}, u32[]{:S(2)}, u32[]{:S(2)}) %collective-permute-start.2) | collective-permute-done | bytes 131104 | tf_op jit(solution)/shard_map/ppermute | solution.py:226
  9.9 0.7 %collective-permute-start.3 = (f32[2,128,128]{2,1,0:T(8,128)S(1)}, f32[2,128,128]{2,1,0:T(8,128)S(1)}, u32[]{:S(2)}, u32[]{:S(2)}) collective-permute-start(f32[2,128,128]{2,1,0:T(8,128)S(1)} %collective-permute-done.2.refs_0_), channel_id=1, source_target_pairs={{0,1},{1,0},{2,3},{3,2},{4,5},{5,4},{6,7},{7,6},{8,9},{9,8},{10,11... | collective-permute-start | bytes 393224 | tf_op jit(solution)/shard_map/ppermute | solution.py:226
  10.6 0.8 %collective-permute-done.7 = f32[2,128,128]{2,1,0:T(8,128)S(1)} collective-permute-done((f32[2,128,128]{2,1,0:T(8,128)S(1)}, f32[2,128,128]{2,1,0:T(8,128)S(1)}, u32[]{:S(2)}, u32[]{:S(2)}) %collective-permute-start.7) | collective-permute-done | bytes 131104 | tf_op jit(solution)/shard_map/ppermute | solution.py:271
  11.4 1.1 %collective-permute-start.8 = (f32[2,128,128]{2,1,0:T(8,128)S(1)}, f32[2,128,128]{2,1,0:T(8,128)S(1)}, u32[]{:S(2)}, u32[]{:S(2)}) collective-permute-start(f32[2,128,128]{2,1,0:T(8,128)S(1)} %add.3.refs_3_), channel_id=1, source_target_pairs={{0,2},{1,3},{2,0},{3,1},{4,6},{5,7},{6,4},{7,5},{8,10},{9,11},{10,... | collective-permute-start | bytes 393224 | tf_op jit(solution)/shard_map/ppermute | solution.py:226
  12.5 0.0 collective-permute-done.other_c
  12.5 0.0 collective-permute-done.3.refs_1_
  12.5 0.0 copy-done
  12.5 1.4 %shard_map.76 = (bf16[4,384,256]{2,1,0:T(8,128)(2,1)S(1)}, bf16[4,384,256]{2,1,0:T(8,128)(2,1)S(1)}, f32[2,128,128]{2,1,0:T(8,128)S(1)}, f32[2,128,128]{2,1,0:T(8,128)S(1)}) custom-call(s32[4,8,128]{2,1,0:T(8,128)S(1)} %get-tuple-element.15.kinds, f32[4,2,128,128]{3,2,1,0:T(8,128)S(1)} %copy-done, f32[2,128,128]{2,1,0:T(8,128)S(1)} %bitcast.12, ...), custom_call_target="tpu_custom_call" | custom-call | flops 1000000000 | bytes 1589248 | tf_op jit(solution)/shard_map/pallas_call | solution.py:211
  13.9 1.7 %collective-permute-start.9 = (f32[2,128,128]{2,1,0:T(8,128)S(1)}, f32[2,128,128]{2,1,0:T(8,128)S(1)}, u32[]{:S(2)}, u32[]{:S(2)}) collective-permute-start(f32[2,128,128]{2,1,0:T(8,128)S(1)} %get-tuple-element.21), channel_id=1, source_target_pairs={{0,1},{1,0},{2,3},{3,2},{4,5},{5,4},{6,7},{7,6},{8,9},{9,8},{10,11... | collective-permute-start | bytes 393224 | tf_op jit(solution)/shard_map/ppermute | solution.py:226
  15.5 0.0 collective-permute-done.8.arrived
  15.5 1.0 %collective-permute-done.9.other.refs_0_ = f32[2,128,128]{2,1,0:T(8,128)S(1)} collective-permute-done((f32[2,128,128]{2,1,0:T(8,128)S(1)}, f32[2,128,128]{2,1,0:T(8,128)S(1)}, u32[]{:S(2)}, u32[]{:S(2)}) %collective-permute-start.9) | collective-permute-done | bytes 131104 | tf_op jit(solution)/shard_map/ppermute | solution.py:226
  16.5 0.7 %shard_map.77 = (f32[2,128,128]{2,1,0:T(8,128)S(1)}, f32[2,128,128]{2,1,0:T(8,128)S(1)}) custom-call(f32[2,128,128]{2,1,0:T(8,128)S(1)} %collective-permute-done.8.arrived, f32[2,128,128]{2,1,0:T(8,128)S(1)} %collective-permute-done.9.other.refs_0_, bf16[4,384,256]{2,1,0:T(8,128)(2,1)S(1)} %get-tuple-element.19.high, ...), custom_call_target="tpu_custom_call" | custom-call | flops 1000000000 | bytes 1966080 | tf_op jit(solution)/shard_map/pallas_call | solution.py:211
  17.2 0.9 %collective-permute-start.10 = (f32[2,128,128]{2,1,0:T(8,128)S(1)}, f32[2,128,128]{2,1,0:T(8,128)S(1)}, u32[]{:S(2)}, u32[]{:S(2)}) collective-permute-start(f32[2,128,128]{2,1,0:T(8,128)S(1)} %get-tuple-element.24.refs_1_), channel_id=1, source_target_pairs={{0,1},{1,0},{2,3},{3,2},{4,5},{5,4},{6,7},{7,6},{8,9},{9,8},{10,11... | collective-permute-start | bytes 393224 | tf_op jit(solution)/shard_map/ppermute | solution.py:226
  18.1 1.0 %collective-permute-done.10.refs_0_ = f32[2,128,128]{2,1,0:T(8,128)S(1)} collective-permute-done((f32[2,128,128]{2,1,0:T(8,128)S(1)}, f32[2,128,128]{2,1,0:T(8,128)S(1)}, u32[]{:S(2)}, u32[]{:S(2)}) %collective-permute-start.10) | collective-permute-done | bytes 131104 | tf_op jit(solution)/shard_map/ppermute | solution.py:226
  19.1 1.1 %shard_map.79 = f32[2,128,128]{2,1,0:T(8,128)} custom-call(bf16[4,384,256]{2,1,0:T(8,128)(2,1)S(1)} %get-tuple-element.19.high, bf16[4,384,256]{2,1,0:T(8,128)(2,1)S(1)} %get-tuple-element.20.low, f32[2,128,128]{2,1,0:T(8,128)S(1)} %shard_map.78.before, f32[2,128,128]{2,1,0:T(8,128)S(1)} %collective-permute-done.10.refs_0_), custom_call_target="tpu_custom_call" | custom-call | flops 1000000000 | bytes 1835008 | tf_op jit(solution)/shard_map/pallas_call | solution.py:211
  (2 shorter events, 0.0 us)
Async XLA Ops:
  0.0 3.4 %copy-start.4 = (s32[8]{0:T(128)S(1)}, s32[8]{0:T(128)}, u32[]{:S(2)}) copy-start(s32[8]{0:T(128)} %offsets.1) | copy-start | bytes 100
  0.0 3.4 %copy-start.5 = (f32[8]{0:T(128)S(1)}, f32[8]{0:T(128)}, u32[]{:S(2)}) copy-start(f32[8]{0:T(128)} %weights.1) | copy-start | bytes 100
  0.0 3.4 %copy-start.6 = (s32[4]{0:T(128)S(1)}, s32[4]{0:T(128)}, u32[]{:S(2)}) copy-start(s32[4]{0:T(128)} %material.1) | copy-start | bytes 52
  0.0 4.1 %collective-permute-start.1 = (f32[2,128,128]{2,1,0:T(8,128)}, f32[2,128,128]{2,1,0:T(8,128)S(1)}, u32[]{:S(2)}, u32[]{:S(2)}) collective-permute-start(f32[2,128,128]{2,1,0:T(8,128)} %bitcast.10), channel_id=1, source_target_pairs={{0,1},{1,0},{2,3},{3,2},{4,5},{5,4},{6,7},{7,6},{8,9},{9,8},{10,11... | collective-permute-start | bytes 393224 | tf_op jit(solution)/shard_map/ppermute | solution.py:226
  0.1 4.0 %copy-start.2 = (f32[2,1,1,128,128]{4,3,2,1,0:T(8,128)S(1)}, f32[2,1,1,128,128]{4,3,2,1,0:T(8,128)}, u32[]{:S(2)}) copy-start(f32[2,1,1,128,128]{4,3,2,1,0:T(8,128)} %param.8) | copy-start | bytes 393220
  0.1 4.0 %copy-start.3 = (f32[2,1,128,128]{3,2,1,0:T(8,128)S(1)}, f32[2,1,128,128]{3,2,1,0:T(8,128)}, u32[]{:S(2)}) copy-start(f32[2,1,128,128]{3,2,1,0:T(8,128)} %param.9) | copy-start | bytes 393220
  0.1 6.8 %collective-permute-start.4 = (f32[2,128,128]{2,1,0:T(8,128)}, f32[2,128,128]{2,1,0:T(8,128)S(1)}, u32[]{:S(2)}, u32[]{:S(2)}) collective-permute-start(f32[2,128,128]{2,1,0:T(8,128)} %bitcast.6), channel_id=1, source_target_pairs={{0,8},{1,9},{2,10},{3,11},{4,12},{5,13},{6,14},{7,15},{8,0},{9,1},... | collective-permute-start | bytes 393224 | tf_op jit(solution)/shard_map/ppermute | solution.py:245
  2.9 4.0 %collective-permute-start.5 = (f32[2,128,128]{2,1,0:T(8,128)}, f32[2,128,128]{2,1,0:T(8,128)S(1)}, u32[]{:S(2)}, u32[]{:S(2)}) collective-permute-start(f32[2,128,128]{2,1,0:T(8,128)} %bitcast.7), channel_id=1, source_target_pairs={{0,1},{1,0},{2,3},{3,2},{4,5},{5,4},{6,7},{7,6},{8,16},{9,17},{10,... | collective-permute-start | bytes 393224 | tf_op jit(solution)/shard_map/ppermute | solution.py:245
  3.3 3.6 %collective-permute-start.6 = (f32[2,128,128]{2,1,0:T(8,128)}, f32[2,128,128]{2,1,0:T(8,128)S(1)}, u32[]{:S(2)}, u32[]{:S(2)}) collective-permute-start(f32[2,128,128]{2,1,0:T(8,128)} %bitcast.8), channel_id=1, source_target_pairs={{0,1},{1,0},{2,3},{3,2},{4,5},{5,4},{6,7},{7,6},{8,9},{9,8},{10,11... | collective-permute-start | bytes 393224 | tf_op jit(solution)/shard_map/ppermute | solution.py:245
  4.1 2.8 %copy-start.1 = (f32[2,1,1,128,128]{4,3,2,1,0:T(8,128)S(1)}, f32[2,1,1,128,128]{4,3,2,1,0:T(8,128)}, u32[]{:S(2)}) copy-start(f32[2,1,1,128,128]{4,3,2,1,0:T(8,128)} %param.7) | copy-start | bytes 393220
  4.6 7.9 %copy-start = (f32[4,2,128,128]{3,2,1,0:T(8,128)S(1)}, f32[4,2,128,128]{3,2,1,0:T(8,128)}, u32[]{:S(2)}) copy-start(f32[4,2,128,128]{3,2,1,0:T(8,128)} %table.1) | copy-start | bytes 1572868
  4.6 5.3 %collective-permute-start.2 = (f32[2,128,128]{2,1,0:T(8,128)S(1)}, f32[2,128,128]{2,1,0:T(8,128)S(1)}, u32[]{:S(2)}, u32[]{:S(2)}) collective-permute-start(f32[2,128,128]{2,1,0:T(8,128)S(1)} %shard_map.74.combined), channel_id=1, source_target_pairs={{0,2},{1,3},{2,0},{3,1},{4,6},{5,7},{6,4},{7,5},{8,10},{9,11},{10,... | collective-permute-start | bytes 393224 | tf_op jit(solution)/shard_map/ppermute | solution.py:226
  7.0 4.4 %collective-permute-start.7 = (f32[2,128,128]{2,1,0:T(8,128)S(1)}, f32[2,128,128]{2,1,0:T(8,128)S(1)}, u32[]{:S(2)}, u32[]{:S(2)}) collective-permute-start(f32[2,128,128]{2,1,0:T(8,128)S(1)} %get-tuple-element.18), channel_id=1, source_target_pairs={{0,4},{4,0},{8,12},{12,8},{16,20},{20,16},{24,28},{28,24},{1,5},{5... | collective-permute-start | bytes 393224 | tf_op jit(solution)/shard_map/ppermute | solution.py:271
  8.2 4.3 %collective-permute-start = (f32[2,128,128]{2,1,0:T(8,128)S(1)}, f32[2,128,128]{2,1,0:T(8,128)S(1)}, u32[]{:S(2)}, u32[]{:S(2)}) collective-permute-start(f32[2,128,128]{2,1,0:T(8,128)S(1)} %bitcast.14), channel_id=1, source_target_pairs={{0,1},{1,0},{2,3},{3,2},{4,5},{5,4},{6,7},{7,6},{8,9},{9,8},{10,11... | collective-permute-start | bytes 393224 | tf_op jit(solution)/shard_map/ppermute | solution.py:226
  9.9 2.6 %collective-permute-start.3 = (f32[2,128,128]{2,1,0:T(8,128)S(1)}, f32[2,128,128]{2,1,0:T(8,128)S(1)}, u32[]{:S(2)}, u32[]{:S(2)}) collective-permute-start(f32[2,128,128]{2,1,0:T(8,128)S(1)} %collective-permute-done.2.refs_0_), channel_id=1, source_target_pairs={{0,1},{1,0},{2,3},{3,2},{4,5},{5,4},{6,7},{7,6},{8,9},{9,8},{10,11... | collective-permute-start | bytes 393224 | tf_op jit(solution)/shard_map/ppermute | solution.py:226
  11.4 4.1 %collective-permute-start.8 = (f32[2,128,128]{2,1,0:T(8,128)S(1)}, f32[2,128,128]{2,1,0:T(8,128)S(1)}, u32[]{:S(2)}, u32[]{:S(2)}) collective-permute-start(f32[2,128,128]{2,1,0:T(8,128)S(1)} %add.3.refs_3_), channel_id=1, source_target_pairs={{0,2},{1,3},{2,0},{3,1},{4,6},{5,7},{6,4},{7,5},{8,10},{9,11},{10,... | collective-permute-start | bytes 393224 | tf_op jit(solution)/shard_map/ppermute | solution.py:226
  13.9 2.7 %collective-permute-start.9 = (f32[2,128,128]{2,1,0:T(8,128)S(1)}, f32[2,128,128]{2,1,0:T(8,128)S(1)}, u32[]{:S(2)}, u32[]{:S(2)}) collective-permute-start(f32[2,128,128]{2,1,0:T(8,128)S(1)} %get-tuple-element.21), channel_id=1, source_target_pairs={{0,1},{1,0},{2,3},{3,2},{4,5},{5,4},{6,7},{7,6},{8,9},{9,8},{10,11... | collective-permute-start | bytes 393224 | tf_op jit(solution)/shard_map/ppermute | solution.py:226
  17.2 1.9 %collective-permute-start.10 = (f32[2,128,128]{2,1,0:T(8,128)S(1)}, f32[2,128,128]{2,1,0:T(8,128)S(1)}, u32[]{:S(2)}, u32[]{:S(2)}) collective-permute-start(f32[2,128,128]{2,1,0:T(8,128)S(1)} %get-tuple-element.24.refs_1_), channel_id=1, source_target_pairs={{0,1},{1,0},{2,3},{3,2},{4,5},{5,4},{6,7},{7,6},{8,9},{9,8},{10,11... | collective-permute-start | bytes 393224 | tf_op jit(solution)/shard_map/ppermute | solution.py:226

commit v7 on v6

--- a/solution.py
+++ b/solution.py
@@ -44,6 +44,10 @@
 
 def times(left, right_block):
     return product(left, [full(part) for part in split(rows(right_block))], NN)
+
+
+def times_row(left, right_row):
+    return product(left, [full(part) for part in split(right_row)], NN)
 
 
 def times_dagger(left, right_block):
@@ -95,80 +99,70 @@
     return result
 
 
-def pair_kernel(own_r, own_c, other_r, after, sent):
-    odd = lax.axis_index("space") % 2 == 1
-
-    @pl.when(odd)
-    def _():
-        sent[...] = block_of(times(split(times(split(rows(own_r)), own_c)), other_r))
-
-    @pl.when(jnp.logical_not(odd))
-    def _():
-        sent[...] = other_r[...]
-
-
 def valid_terms(slab, mine, count):
     return slab <= mine, (slab >= 1) & (slab <= mine + 1), slab < mine
 
 
-def factor_kernel(count, kinds, table, own_r, own_c, other_c, combined, *refs):
-    pairs = count // 2
-    sent, crossed, first_c = (refs[n * (pairs - 1) : (n + 1) * (pairs - 1)] for n in range(3))
-    field, *outs, state, field_out, held, base = refs[3 * (pairs - 1) :]
+def factor_kernel(count, kinds, table, field, *refs):
+    retarded, coupling, outs = refs[:count], refs[count : 2 * count], refs[2 * count : 2 * count + 2]
+    state, field_out, held_r, held_c, chain = refs[2 * count + 2 :]
     mine = lax.axis_index("space")
-    odd = mine % 2 == 1
     size = table.shape[-1]
-    for slot in range(pairs - 1):
-        here, there = sent[slot][...], crossed[slot][...]
-        held[slot, 0] = jnp.where(odd, here, there)
-        held[slot, 1] = jnp.where(odd, there, here)
-        held[slot, 2] = first_c[slot][...]
-
-    def store(slab, which, parts):
-        valid = valid_terms(slab, mine, count)
-        position = sum((v.astype(jnp.int32) for v in valid[:which]), jnp.int32(0))
-
-        @pl.when(valid[which] & (slab >= 0) & (slab < count))
-        def _():
-            for out, part in zip(outs, parts):
-                out[jnp.bitwise_xor(mine, slab), pl.ds(pl.multiple_of(position * size, size), size)] = part
-
-    def spread(slabs, maps):
-        made = []
-        for slab, whole in zip(slabs, maps):
-            parts = split(whole)
-            right = times(parts, table[kinds[slab, 0, 0]])
-            left = times_dagger(parts, table[kinds[jnp.maximum(slab - 1, 0), 0, 0]])
-            made.append((parts, split(right), split(left)))
-        for slab, (same, right, left) in zip(slabs, made):
+
+    def build(device):
+        steps = {
+            slab: times(split(rows(coupling[device ^ slab])), retarded[device ^ (slab - 1)])
+            for slab in range(1, device + 1)
+        }
+        whole = rows(retarded[0])
+        for slab in range(device, -1, -1):
+            same = split(whole)
+            made = [(slab, 0, same)]
+            if slab + 1 < count:
+                made.append((slab + 1, 1, split(times(same, table[kinds[slab, 0, 0]]))))
+            if slab:
+                made.append((slab - 1, 2, split(times_dagger(same, table[kinds[slab - 1, 0, 0]]))))
+                whole = times_row(same, steps[slab])
+            for target, which, parts in made:
+                position = sum(map(int, valid_terms(target, device, count)[:which]))
+                for out, part in zip(outs, parts):
+                    out[device ^ target, position * size : (position + 1) * size] = part
+
+    def build_any():
+        for slot in range(count):
+            held_r[slot] = retarded[slot][...]
+            held_c[slot] = coupling[slot][...]
+        chain[...] = rows(retarded[0])
+
+        def store(slab, which, parts):
+            valid = valid_terms(slab, mine, count)
+            position = sum((v.astype(jnp.int32) for v in valid[:which]), jnp.int32(0))
+
+            @pl.when(valid[which] & (slab >= 0) & (slab < count))
+            def _():
+                for out, part in zip(outs, parts):
+                    out[jnp.bitwise_xor(mine, slab), pl.ds(pl.multiple_of(position * size, size), size)] = part
+
+        def step(index, carry):
+            slab = mine - index
+            before = jnp.maximum(slab - 1, 0)
+            same = split(chain[...])
+            right = split(times(same, table[kinds[slab, 0, 0]]))
+            left = split(times_dagger(same, table[kinds[before, 0, 0]]))
+            carried = times(same, held_c[jnp.bitwise_xor(mine, slab)])
+            chain[...] = times(split(carried), held_r[jnp.bitwise_xor(mine, before)])
             store(slab, 0, same)
             store(slab + 1, 1, right)
             store(slab - 1, 2, left)
-
-    @pl.when(odd)
-    def _():
-        spread([mine, mine - 1], [rows(own_r), rows(combined)])
-
-    @pl.when(jnp.logical_not(odd))
-    def _():
-        spread([mine], [rows(own_r)])
-
-    @pl.when(mine >= 2)
-    def _():
-        start = split(jnp.where(odd, rows(combined), rows(own_r)))
-        base[...] = times(start, jnp.where(odd, other_c[...], own_c[...]))
-
-    def earlier(step, _):
-        pair = mine // 2 - step
-        block = held.at[jnp.bitwise_xor(mine // 2, pair) - 1]
-        parts = split(base[...])
-        near, far = times(parts, block[1]), times(parts, block[0])
-        spread([2 * pair + 1, 2 * pair], [near, far])
-        if count > 4:
-            base[...] = times(split(far), block[2])
-        return _
-
-    lax.fori_loop(1, mine // 2 + 1, earlier, 0)
+            return carry
+
+        lax.fori_loop(0, mine + 1, step, 0)
+
+    if count <= 4:
+        for device in range(count):
+            pl.when(mine == device)(functools.partial(build, device))
+    else:
+        build_any()
     field_out[...] = field[...]
     add_fields(count, {0: field}, outs, None, state)
 
@@ -200,6 +194,19 @@
 def first_kernel(count, arrived, other, high, low, before, arrived_out, out):
     arrived_out[...] = arrived[...]
     add_fields(count, {1: other}, (high, low), before, out, lambda slot, device: device % 2 == 1)
+
+
+def add_kernel(left, right, out):
+    out[...] = left[...] + right[...]
+
+
+def same_kernel(value, out):
+    out[...] = value[...]
+
+
+def mix_kernel(own, arrived, out):
+    odd = lax.axis_index("space") % 2 == 1
+    out[...] = jnp.where(odd, arrived[...], own[...])
 
 
 def field_kernel(count, slots, high, low, before, *refs):
@@ -250,19 +257,14 @@
         [jax.ShapeDtypeStruct((group, len(held), 8, 128), F32), jax.ShapeDtypeStruct((slabs, 8, 128), jnp.int32)], [SMEM] * 3,
         offsets, weights, material,
     )
-    other_c = exchange(coupling, 1)
-    combined = call(pair_kernel, block, [VMEM] * 4, retarded, coupling, exchange(retarded, 1), shares)
-    sent = gather({0: combined}, chip_bits)
-    first_c = coupling
-    if slabs > 4:
-        first_c = jnp.where(lax.axis_index("space") % 2 == 1, other_c, coupling)
-    all_c = gather({0: first_c}, chip_bits) if slabs > 4 else {slot: first_c for slot in sent}
-    others = [slot for slot in sorted(sent) if slot]
-    earlier = (
-        [sent[slot] for slot in others]
-        + [exchange(sent[slot], 1) for slot in others]
-        + [all_c[slot] for slot in others]
-    )
+    all_r = gather({0: retarded}, chip_bits + [1])
+    if len(chip_bits) == 1:
+        bit = chip_bits[0]
+        arrived = exchange(coupling, bit)
+        mixed = exchange(call(mix_kernel, block, [VMEM] * 2, coupling, arrived), 1)
+        all_c = {0: coupling, 1: mixed, bit: arrived, bit ^ 1: mixed}
+    else:
+        all_c = gather({0: coupling}, chip_bits + [1])
     sums = call(functools.partial(smear_kernel, group), [block] * group, [VMEM] * (1 + len(held)), shares, *held)
 
     field = sums[0]
@@ -273,10 +275,9 @@
 
     factor_shape = jax.ShapeDtypeStruct((slabs, 3 * size, 2 * size), BF16)
     *factors, state, own = call(
-        functools.partial(factor_kernel, slabs), [factor_shape] * 2 + [block] * 2,
-        [VMEM] * (7 + len(earlier)),
-        kinds, gradient_table, retarded, coupling, other_c, combined, *earlier, field,
-        scratch=[pltpu.VMEM((max(slabs // 2 - 1, 1), 3, 2, size, size), F32), pltpu.VMEM((size, 2 * size), F32)],
+        functools.partial(factor_kernel, slabs), [factor_shape] * 2 + [block] * 2, [VMEM] * (2 * slabs + 3),
+        kinds, gradient_table, field, *[all_r[s] for s in range(slabs)], *[all_c[s] for s in range(slabs)],
+        scratch=[pltpu.VMEM((slabs, 2, size, size), F32)] * 2 + [pltpu.VMEM((size, 2 * size), F32)],
     )
 
     def propagate(slots):
@@ -287,6 +288,7 @@
     for bit in chip_bits:
         for key in [key for key in fields if key % 2 == 0]:
             fields[key ^ bit] = exchange(fields[key], bit)
+            fields[key ^ bit] = call(same_kernel, block, [VMEM], fields[key ^ bit])
             if bit == chip_bits[0]:
                 fields[bit], state = call(
                     functools.partial(first_kernel, slabs), [block] * 2, [VMEM] * 5,

time: 20.3 us -> 20.5 us (level)
  starting transfers between devices: 11.4 us -> 13.4 us
  waiting for transfers between devices: 4.24 us -> 2.76 us
  Pallas kernels: 4.37 us -> 4 us
    ppermute x7 -> x8, starting transfers between devices: 6.84 us -> 8.88 us  [exchange(): return lax.ppermute(value, 'space', [(i, i ^ bit) for i in range(count)])]
    ppermute x1, waiting for transfers between devices: 0.82 us -> 0.01 us  [per_device(): arrived = lax.ppermute(sums[step], 'energy', pairs)]
    ppermute x3, waiting for transfers between devices: 0.97 us -> 0.26 us  [per_device(): held.append(lax.ppermute(own, ('energy', 'space'), pairs))]
    pallas_call x7 -> x8, Pallas kernels: 4.37 us -> 4 us  [call(): pl.pallas_call(kernel, out_shape=shapes, in_specs=specs, out_specs=jax.tr...]
    ppermute x3, starting transfers between devices: 3.3 us -> 3.08 us  [per_device(): held.append(lax.ppermute(own, ('energy', 'space'), pairs))]
    ppermute x7 -> x8, waiting for transfers between devices: 2.46 us -> 2.5 us  [exchange(): return lax.ppermute(value, 'space', [(i, i ^ bit) for i in range(count)])]
  transfers between devices with their start and end apart: 11 -> 12, of which waited for: 5 -> 5; matrix products, arithmetic and copies ran while one was open for 0% -> 0% of each run, Pallas kernels for 13% -> 11%
where the time goes in v7:
time: 20.5 us; the launch traced here: 20.3 us
  starting transfers between devices  13.4 us (65%)
  Pallas kernels  4 us (20%)
  waiting for transfers between devices  2.76 us (13%)
    ppermute x8, starting transfers between devices, exchange(): return lax.ppermute(value, 'space', [(i, i ^ bit) for i in range(count)])  8.88 us
    pallas_call x8, Pallas kernels, call(): pl.pallas_call(kernel, out_shape=shapes, in_specs=specs, out_specs=jax.tr...  4 us
    ppermute x3, starting transfers between devices, per_device(): held.append(lax.ppermute(own, ('energy', 'space'), pairs))  3.08 us
    ppermute x8, waiting for transfers between devices, exchange(): return lax.ppermute(value, 'space', [(i, i ^ bit) for i in range(count)])  2.5 us
    ppermute x1, starting transfers between devices, per_device(): arrived = lax.ppermute(sums[step], 'energy', pairs)  1.44 us
  transfers between devices with their start and end apart: 12, of which 5 were waited for; matrix products, arithmetic and copies ran while one was open for 0% of the time, Pallas kernels for 11%

profile of v7, /device:TPU:1, one launch (start us, length us, event | category | flops | bytes accessed | tf_op | source)
XLA Modules:
  0.0 20.3 jit_solution(3700391104323668455)
XLA Ops:
  0.0 2.1 %collective-permute-start = (f32[2,128,128]{2,1,0:T(8,128)}, f32[2,128,128]{2,1,0:T(8,128)S(1)}, u32[]{:S(2)}, u32[]{:S(2)}) collective-permute-start(f32[2,128,128]{2,1,0:T(8,128)} %bitcast.6), channel_id=1, source_target_pairs={{0,8},{1,9},{2,10},{3,11},{4,12},{5,13},{6,14},{7,15},{8,0},{9,1},... | collective-permute-start | bytes 393224 | tf_op jit(solution)/shard_map/ppermute | solution.py:252
  2.1 1.0 %collective-permute-start.1 = (f32[2,128,128]{2,1,0:T(8,128)}, f32[2,128,128]{2,1,0:T(8,128)S(1)}, u32[]{:S(2)}, u32[]{:S(2)}) collective-permute-start(f32[2,128,128]{2,1,0:T(8,128)} %bitcast.7), channel_id=1, source_target_pairs={{0,1},{1,0},{2,3},{3,2},{4,5},{5,4},{6,7},{7,6},{8,16},{9,17},{10,... | collective-permute-start | bytes 393224 | tf_op jit(solution)/shard_map/ppermute | solution.py:252
  3.1 0.0 collective-permute-start.2
  3.1 0.0 copy-start.4
  3.1 0.0 copy-start.5
  3.1 0.0 copy-start.6
  3.1 1.3 %collective-permute-start.7 = (f32[2,128,128]{2,1,0:T(8,128)}, f32[2,128,128]{2,1,0:T(8,128)S(1)}, u32[]{:S(2)}, u32[]{:S(2)}) collective-permute-start(f32[2,128,128]{2,1,0:T(8,128)} %bitcast.13), channel_id=1, source_target_pairs={{0,2},{1,3},{2,0},{3,1},{4,6},{5,7},{6,4},{7,5},{8,10},{9,11},{10,... | collective-permute-start | bytes 393224 | tf_op jit(solution)/shard_map/ppermute | solution.py:233
  4.4 0.0 copy-start.2
  4.4 0.0 copy-start.1
  4.4 0.2 %collective-permute-start.5 = (f32[2,128,128]{2,1,0:T(8,128)}, f32[2,128,128]{2,1,0:T(8,128)S(1)}, u32[]{:S(2)}, u32[]{:S(2)}) collective-permute-start(f32[2,128,128]{2,1,0:T(8,128)} %bitcast.10), channel_id=1, source_target_pairs={{0,2},{1,3},{2,0},{3,1},{4,6},{5,7},{6,4},{7,5},{8,10},{9,11},{10,... | collective-permute-start | bytes 393224 | tf_op jit(solution)/shard_map/ppermute | solution.py:233
  4.6 0.0 copy-done.4
  4.6 0.0 copy-done.5
  4.6 0.0 copy-done.6
  4.6 0.7 %shard_map.73 = (f32[2,4,8,128]{3,2,1,0:T(8,128)S(1)}, s32[4,8,128]{2,1,0:T(8,128)S(1)}) custom-call(s32[8]{0:T(128)S(1)} %copy-done.4, f32[8]{0:T(128)S(1)} %copy-done.5, s32[4]{0:T(128)S(1)} %copy-done.6), custom_call_target="tpu_custom_call" | custom-call | flops 1000000000 | bytes 80 | tf_op jit(solution)/shard_map/pallas_call | solution.py:218
  5.3 0.3 %collective-permute-done.refs_1_ = f32[2,128,128]{2,1,0:T(8,128)S(1)} collective-permute-done((f32[2,128,128]{2,1,0:T(8,128)}, f32[2,128,128]{2,1,0:T(8,128)S(1)}, u32[]{:S(2)}, u32[]{:S(2)}) %collective-permute-start) | collective-permute-done | bytes 131104 | tf_op jit(solution)/shard_map/ppermute | solution.py:252
  5.6 0.0 copy-done.2
  5.6 1.2 %collective-permute-start.4 = (f32[2,128,128]{2,1,0:T(8,128)S(1)}, f32[2,128,128]{2,1,0:T(8,128)S(1)}, u32[]{:S(2)}, u32[]{:S(2)}) collective-permute-start(f32[2,128,128]{2,1,0:T(8,128)S(1)} %bitcast.11), channel_id=1, source_target_pairs={{0,1},{1,0},{2,3},{3,2},{4,5},{5,4},{6,7},{7,6},{8,9},{9,8},{10,11... | collective-permute-start | bytes 393224 | tf_op jit(solution)/shard_map/ppermute | solution.py:233
  6.8 0.0 collective-permute-done.1.refs_2_
  6.8 0.0 collective-permute-done.2.refs_3_
  6.8 0.0 copy-done.1
  6.8 0.0 copy-start.3
  6.8 0.1 shard_map.74
  6.9 0.0 copy-start
  6.9 1.4 %collective-permute-start.3 = (f32[2,128,128]{2,1,0:T(8,128)S(1)}, f32[2,128,128]{2,1,0:T(8,128)S(1)}, u32[]{:S(2)}, u32[]{:S(2)}) collective-permute-start(f32[2,128,128]{2,1,0:T(8,128)S(1)} %get-tuple-element.18), channel_id=1, source_target_pairs={{0,4},{4,0},{8,12},{12,8},{16,20},{20,16},{24,28},{28,24},{1,5},{5... | collective-permute-start | bytes 393224 | tf_op jit(solution)/shard_map/ppermute | solution.py:273
  8.4 0.0 collective-permute-done.7.arrived.refs_6_
  8.4 0.0 copy-done.3
  8.4 1.9 %collective-permute-start.8 = (f32[2,128,128]{2,1,0:T(8,128)S(1)}, f32[2,128,128]{2,1,0:T(8,128)S(1)}, u32[]{:S(2)}, u32[]{:S(2)}) collective-permute-start(f32[2,128,128]{2,1,0:T(8,128)S(1)} %shard_map.75), channel_id=1, source_target_pairs={{0,1},{1,0},{2,3},{3,2},{4,5},{5,4},{6,7},{7,6},{8,9},{9,8},{10,11... | collective-permute-start | bytes 393224 | tf_op jit(solution)/shard_map/ppermute | solution.py:233
  10.3 0.6 %collective-permute-done.5.refs_2_ = f32[2,128,128]{2,1,0:T(8,128)S(1)} collective-permute-done((f32[2,128,128]{2,1,0:T(8,128)}, f32[2,128,128]{2,1,0:T(8,128)S(1)}, u32[]{:S(2)}, u32[]{:S(2)}) %collective-permute-start.5) | collective-permute-done | bytes 131104 | tf_op jit(solution)/shard_map/ppermute | solution.py:233
  10.8 1.3 %collective-permute-start.6 = (f32[2,128,128]{2,1,0:T(8,128)S(1)}, f32[2,128,128]{2,1,0:T(8,128)S(1)}, u32[]{:S(2)}, u32[]{:S(2)}) collective-permute-start(f32[2,128,128]{2,1,0:T(8,128)S(1)} %collective-permute-done.5.refs_2_), channel_id=1, source_target_pairs={{0,1},{1,0},{2,3},{3,2},{4,5},{5,4},{6,7},{7,6},{8,9},{9,8},{10,11... | collective-permute-start | bytes 393224 | tf_op jit(solution)/shard_map/ppermute | solution.py:233
  12.1 0.0 collective-permute-done.3
  12.1 1.5 %collective-permute-start.9 = (f32[2,128,128]{2,1,0:T(8,128)S(1)}, f32[2,128,128]{2,1,0:T(8,128)S(1)}, u32[]{:S(2)}, u32[]{:S(2)}) collective-permute-start(f32[2,128,128]{2,1,0:T(8,128)S(1)} %add.3.field), channel_id=1, source_target_pairs={{0,2},{1,3},{2,0},{3,1},{4,6},{5,7},{6,4},{7,5},{8,10},{9,11},{10,... | collective-permute-start | bytes 393224 | tf_op jit(solution)/shard_map/ppermute | solution.py:233
  13.6 0.0 collective-permute-done.4.refs_1_
  13.6 0.0 collective-permute-done.8.refs_5_.refs_7_
  13.6 0.0 collective-permute-done.6.refs_3_
  13.6 0.0 copy-done
  13.6 1.4 %shard_map.76 = (bf16[4,384,256]{2,1,0:T(8,128)(2,1)S(1)}, bf16[4,384,256]{2,1,0:T(8,128)(2,1)S(1)}, f32[2,128,128]{2,1,0:T(8,128)S(1)}, f32[2,128,128]{2,1,0:T(8,128)S(1)}) custom-call(s32[4,8,128]{2,1,0:T(8,128)S(1)} %get-tuple-element.15.kinds, f32[4,2,128,128]{3,2,1,0:T(8,128)S(1)} %copy-done, f32[2,128,128]{2,1,0:T(8,128)S(1)} %add.3.field, ...), custom_call_target="tpu_custom_call" | custom-call | flops 1000000000 | bytes 1720320 | tf_op jit(solution)/shard_map/pallas_call | solution.py:218
  15.0 0.5 %collective-permute-start.10 = (f32[2,128,128]{2,1,0:T(8,128)S(1)}, f32[2,128,128]{2,1,0:T(8,128)S(1)}, u32[]{:S(2)}, u32[]{:S(2)}) collective-permute-start(f32[2,128,128]{2,1,0:T(8,128)S(1)} %get-tuple-element.21), channel_id=1, source_target_pairs={{0,1},{1,0},{2,3},{3,2},{4,5},{5,4},{6,7},{7,6},{8,9},{9,8},{10,11... | collective-permute-start | bytes 393224 | tf_op jit(solution)/shard_map/ppermute | solution.py:233
  15.5 0.9 %collective-permute-done.9.value = f32[2,128,128]{2,1,0:T(8,128)S(1)} collective-permute-done((f32[2,128,128]{2,1,0:T(8,128)S(1)}, f32[2,128,128]{2,1,0:T(8,128)S(1)}, u32[]{:S(2)}, u32[]{:S(2)}) %collective-permute-start.9) | collective-permute-done | bytes 131104 | tf_op jit(solution)/shard_map/ppermute | solution.py:233
  16.4 0.1 collective-permute-done.10.other.refs_0_
  16.5 0.7 %shard_map.78 = (f32[2,128,128]{2,1,0:T(8,128)S(1)}, f32[2,128,128]{2,1,0:T(8,128)S(1)}) custom-call(f32[2,128,128]{2,1,0:T(8,128)S(1)} %shard_map.77.arrived, f32[2,128,128]{2,1,0:T(8,128)S(1)} %collective-permute-done.10.other.refs_0_, bf16[4,384,256]{2,1,0:T(8,128)(2,1)S(1)} %get-tuple-element.19.high, bf16[4,384,256]{2,1,0:T(8,128)(2,1)S(1)} %get-tuple-element.20.low, ...), custom_call_target="tpu_custom_call" | custom-call | flops 1000000000 | bytes 1966080 | tf_op jit(solution)/shard_map/pallas_call | solution.py:218
  17.2 1.0 %collective-permute-start.11 = (f32[2,128,128]{2,1,0:T(8,128)S(1)}, f32[2,128,128]{2,1,0:T(8,128)S(1)}, u32[]{:S(2)}, u32[]{:S(2)}) collective-permute-start(f32[2,128,128]{2,1,0:T(8,128)S(1)} %get-tuple-element.24.refs_1_), channel_id=1, source_target_pairs={{0,1},{1,0},{2,3},{3,2},{4,5},{5,4},{6,7},{7,6},{8,9},{9,8},{10,11... | collective-permute-start | bytes 393224 | tf_op jit(solution)/shard_map/ppermute | solution.py:233
  18.2 1.0 %collective-permute-done.11.refs_0_ = f32[2,128,128]{2,1,0:T(8,128)S(1)} collective-permute-done((f32[2,128,128]{2,1,0:T(8,128)S(1)}, f32[2,128,128]{2,1,0:T(8,128)S(1)}, u32[]{:S(2)}, u32[]{:S(2)}) %collective-permute-start.11) | collective-permute-done | bytes 131104 | tf_op jit(solution)/shard_map/ppermute | solution.py:233
  19.2 1.1 %shard_map.80 = f32[2,128,128]{2,1,0:T(8,128)} custom-call(bf16[4,384,256]{2,1,0:T(8,128)(2,1)S(1)} %get-tuple-element.19.high, bf16[4,384,256]{2,1,0:T(8,128)(2,1)S(1)} %get-tuple-element.20.low, f32[2,128,128]{2,1,0:T(8,128)S(1)} %shard_map.79.before, f32[2,128,128]{2,1,0:T(8,128)S(1)} %collective-permute-done.11.refs_0_), custom_call_target="tpu_custom_call" | custom-call | flops 1000000000 | bytes 1835008 | tf_op jit(solution)/shard_map/pallas_call | solution.py:218
  (4 shorter events, 0.1 us)
Async XLA Ops:
  0.0 5.6 %collective-permute-start = (f32[2,128,128]{2,1,0:T(8,128)}, f32[2,128,128]{2,1,0:T(8,128)S(1)}, u32[]{:S(2)}, u32[]{:S(2)}) collective-permute-start(f32[2,128,128]{2,1,0:T(8,128)} %bitcast.6), channel_id=1, source_target_pairs={{0,8},{1,9},{2,10},{3,11},{4,12},{5,13},{6,14},{7,15},{8,0},{9,1},... | collective-permute-start | bytes 393224 | tf_op jit(solution)/shard_map/ppermute | solution.py:252
  2.1 4.7 %collective-permute-start.1 = (f32[2,128,128]{2,1,0:T(8,128)}, f32[2,128,128]{2,1,0:T(8,128)S(1)}, u32[]{:S(2)}, u32[]{:S(2)}) collective-permute-start(f32[2,128,128]{2,1,0:T(8,128)} %bitcast.7), channel_id=1, source_target_pairs={{0,1},{1,0},{2,3},{3,2},{4,5},{5,4},{6,7},{7,6},{8,16},{9,17},{10,... | collective-permute-start | bytes 393224 | tf_op jit(solution)/shard_map/ppermute | solution.py:252
  3.1 3.7 %collective-permute-start.2 = (f32[2,128,128]{2,1,0:T(8,128)}, f32[2,128,128]{2,1,0:T(8,128)S(1)}, u32[]{:S(2)}, u32[]{:S(2)}) collective-permute-start(f32[2,128,128]{2,1,0:T(8,128)} %bitcast.8), channel_id=1, source_target_pairs={{0,1},{1,0},{2,3},{3,2},{4,5},{5,4},{6,7},{7,6},{8,9},{9,8},{10,11... | collective-permute-start | bytes 393224 | tf_op jit(solution)/shard_map/ppermute | solution.py:252
  3.1 1.5 %copy-start.4 = (s32[8]{0:T(128)S(1)}, s32[8]{0:T(128)}, u32[]{:S(2)}) copy-start(s32[8]{0:T(128)} %offsets.1) | copy-start | bytes 100
  3.1 1.5 %copy-start.5 = (f32[8]{0:T(128)S(1)}, f32[8]{0:T(128)}, u32[]{:S(2)}) copy-start(f32[8]{0:T(128)} %weights.1) | copy-start | bytes 100
  3.1 1.5 %copy-start.6 = (s32[4]{0:T(128)S(1)}, s32[4]{0:T(128)}, u32[]{:S(2)}) copy-start(s32[4]{0:T(128)} %material.1) | copy-start | bytes 52
  3.1 5.3 %collective-permute-start.7 = (f32[2,128,128]{2,1,0:T(8,128)}, f32[2,128,128]{2,1,0:T(8,128)S(1)}, u32[]{:S(2)}, u32[]{:S(2)}) collective-permute-start(f32[2,128,128]{2,1,0:T(8,128)} %bitcast.13), channel_id=1, source_target_pairs={{0,2},{1,3},{2,0},{3,1},{4,6},{5,7},{6,4},{7,5},{8,10},{9,11},{10,... | collective-permute-start | bytes 393224 | tf_op jit(solution)/shard_map/ppermute | solution.py:233
  4.4 1.2 %copy-start.2 = (f32[2,1,1,128,128]{4,3,2,1,0:T(8,128)S(1)}, f32[2,1,1,128,128]{4,3,2,1,0:T(8,128)}, u32[]{:S(2)}) copy-start(f32[2,1,1,128,128]{4,3,2,1,0:T(8,128)} %param.8) | copy-start | bytes 393220
  4.4 2.4 %copy-start.1 = (f32[2,1,1,128,128]{4,3,2,1,0:T(8,128)S(1)}, f32[2,1,1,128,128]{4,3,2,1,0:T(8,128)}, u32[]{:S(2)}) copy-start(f32[2,1,1,128,128]{4,3,2,1,0:T(8,128)} %param.7) | copy-start | bytes 393220
  4.4 6.4 %collective-permute-start.5 = (f32[2,128,128]{2,1,0:T(8,128)}, f32[2,128,128]{2,1,0:T(8,128)S(1)}, u32[]{:S(2)}, u32[]{:S(2)}) collective-permute-start(f32[2,128,128]{2,1,0:T(8,128)} %bitcast.10), channel_id=1, source_target_pairs={{0,2},{1,3},{2,0},{3,1},{4,6},{5,7},{6,4},{7,5},{8,10},{9,11},{10,... | collective-permute-start | bytes 393224 | tf_op jit(solution)/shard_map/ppermute | solution.py:233
  5.6 8.0 %collective-permute-start.4 = (f32[2,128,128]{2,1,0:T(8,128)S(1)}, f32[2,128,128]{2,1,0:T(8,128)S(1)}, u32[]{:S(2)}, u32[]{:S(2)}) collective-permute-start(f32[2,128,128]{2,1,0:T(8,128)S(1)} %bitcast.11), channel_id=1, source_target_pairs={{0,1},{1,0},{2,3},{3,2},{4,5},{5,4},{6,7},{7,6},{8,9},{9,8},{10,11... | collective-permute-start | bytes 393224 | tf_op jit(solution)/shard_map/ppermute | solution.py:233
  6.8 1.6 %copy-start.3 = (f32[2,1,128,128]{3,2,1,0:T(8,128)S(1)}, f32[2,1,128,128]{3,2,1,0:T(8,128)}, u32[]{:S(2)}) copy-start(f32[2,1,128,128]{3,2,1,0:T(8,128)} %param.9) | copy-start | bytes 393220
  6.9 6.7 %copy-start = (f32[4,2,128,128]{3,2,1,0:T(8,128)S(1)}, f32[4,2,128,128]{3,2,1,0:T(8,128)}, u32[]{:S(2)}) copy-start(f32[4,2,128,128]{3,2,1,0:T(8,128)} %table.1) | copy-start | bytes 1572868
  6.9 5.2 %collective-permute-start.3 = (f32[2,128,128]{2,1,0:T(8,128)S(1)}, f32[2,128,128]{2,1,0:T(8,128)S(1)}, u32[]{:S(2)}, u32[]{:S(2)}) collective-permute-start(f32[2,128,128]{2,1,0:T(8,128)S(1)} %get-tuple-element.18), channel_id=1, source_target_pairs={{0,4},{4,0},{8,12},{12,8},{16,20},{20,16},{24,28},{28,24},{1,5},{5... | collective-permute-start | bytes 393224 | tf_op jit(solution)/shard_map/ppermute | solution.py:273
  8.4 5.2 %collective-permute-start.8 = (f32[2,128,128]{2,1,0:T(8,128)S(1)}, f32[2,128,128]{2,1,0:T(8,128)S(1)}, u32[]{:S(2)}, u32[]{:S(2)}) collective-permute-start(f32[2,128,128]{2,1,0:T(8,128)S(1)} %shard_map.75), channel_id=1, source_target_pairs={{0,1},{1,0},{2,3},{3,2},{4,5},{5,4},{6,7},{7,6},{8,9},{9,8},{10,11... | collective-permute-start | bytes 393224 | tf_op jit(solution)/shard_map/ppermute | solution.py:233
  10.8 2.8 %collective-permute-start.6 = (f32[2,128,128]{2,1,0:T(8,128)S(1)}, f32[2,128,128]{2,1,0:T(8,128)S(1)}, u32[]{:S(2)}, u32[]{:S(2)}) collective-permute-start(f32[2,128,128]{2,1,0:T(8,128)S(1)} %collective-permute-done.5.refs_2_), channel_id=1, source_target_pairs={{0,1},{1,0},{2,3},{3,2},{4,5},{5,4},{6,7},{7,6},{8,9},{9,8},{10,11... | collective-permute-start | bytes 393224 | tf_op jit(solution)/shard_map/ppermute | solution.py:233
  12.1 4.3 %collective-permute-start.9 = (f32[2,128,128]{2,1,0:T(8,128)S(1)}, f32[2,128,128]{2,1,0:T(8,128)S(1)}, u32[]{:S(2)}, u32[]{:S(2)}) collective-permute-start(f32[2,128,128]{2,1,0:T(8,128)S(1)} %add.3.field), channel_id=1, source_target_pairs={{0,2},{1,3},{2,0},{3,1},{4,6},{5,7},{6,4},{7,5},{8,10},{9,11},{10,... | collective-permute-start | bytes 393224 | tf_op jit(solution)/shard_map/ppermute | solution.py:233
  15.0 1.5 %collective-permute-start.10 = (f32[2,128,128]{2,1,0:T(8,128)S(1)}, f32[2,128,128]{2,1,0:T(8,128)S(1)}, u32[]{:S(2)}, u32[]{:S(2)}) collective-permute-start(f32[2,128,128]{2,1,0:T(8,128)S(1)} %get-tuple-element.21), channel_id=1, source_target_pairs={{0,1},{1,0},{2,3},{3,2},{4,5},{5,4},{6,7},{7,6},{8,9},{9,8},{10,11... | collective-permute-start | bytes 393224 | tf_op jit(solution)/shard_map/ppermute | solution.py:233
  17.2 2.0 %collective-permute-start.11 = (f32[2,128,128]{2,1,0:T(8,128)S(1)}, f32[2,128,128]{2,1,0:T(8,128)S(1)}, u32[]{:S(2)}, u32[]{:S(2)}) collective-permute-start(f32[2,128,128]{2,1,0:T(8,128)S(1)} %get-tuple-element.24.refs_1_), channel_id=1, source_target_pairs={{0,1},{1,0},{2,3},{3,2},{4,5},{5,4},{6,7},{7,6},{8,9},{9,8},{10,11... | collective-permute-start | bytes 393224 | tf_op jit(solution)/shard_map/ppermute | solution.py:233

commit v8 on v7

--- a/solution.py
+++ b/solution.py
@@ -204,6 +204,10 @@
     out[...] = value[...]
 
 
+def pass_kernel(value, after, out):
+    out[...] = value[...]
+
+
 def mix_kernel(own, arrived, out):
     odd = lax.axis_index("space") % 2 == 1
     out[...] = jnp.where(odd, arrived[...], own[...])
@@ -257,15 +261,22 @@
         [jax.ShapeDtypeStruct((group, len(held), 8, 128), F32), jax.ShapeDtypeStruct((slabs, 8, 128), jnp.int32)], [SMEM] * 3,
         offsets, weights, material,
     )
-    all_r = gather({0: retarded}, chip_bits + [1])
+    sums = call(functools.partial(smear_kernel, group), [block] * group, [VMEM] * (1 + len(held)), shares, *held)
     if len(chip_bits) == 1:
         bit = chip_bits[0]
-        arrived = exchange(coupling, bit)
+        arrived = exchange(retarded, bit)
+        later = call(pass_kernel, block, [VMEM] * 2, retarded, sums[0])
+        all_r = {0: retarded, 1: exchange(later, 1), bit: arrived, bit ^ 1: exchange(arrived, 1)}
+        pairs = [
+            (e * slabs + i, e * slabs + (i ^ bit) if i % 2 or group % 2 else (e ^ 1) * slabs + i)
+            for e in range(energies) for i in range(slabs)
+        ]
+        arrived = lax.ppermute(coupling, ("energy", "space"), pairs)
         mixed = exchange(call(mix_kernel, block, [VMEM] * 2, coupling, arrived), 1)
         all_c = {0: coupling, 1: mixed, bit: arrived, bit ^ 1: mixed}
     else:
+        all_r = gather({0: retarded}, chip_bits + [1])
         all_c = gather({0: coupling}, chip_bits + [1])
-    sums = call(functools.partial(smear_kernel, group), [block] * group, [VMEM] * (1 + len(held)), shares, *held)
 
     field = sums[0]
     for step in range(1, group):

time: 20.5 us -> 19.9 us (0.971)
  waiting for transfers between devices: 2.76 us -> 2.21 us
    ppermute x0 -> x1, starting transfers between devices: none -> 1.3 us  [per_device(): arrived = lax.ppermute(coupling, ('energy', 'space'), pairs)]
    ppermute x8 -> x7, starting transfers between devices: 8.88 us -> 7.85 us  [exchange(): return lax.ppermute(value, 'space', [(i, i ^ bit) for i in range(count)])]
    ppermute x8 -> x7, waiting for transfers between devices: 2.5 us -> 1.95 us  [exchange(): return lax.ppermute(value, 'space', [(i, i ^ bit) for i in range(count)])]
    ppermute x1, starting transfers between devices: 1.44 us -> 1.12 us  [per_device(): arrived = lax.ppermute(sums[step], 'energy', pairs)]
    pallas_call x8 -> x9, Pallas kernels: 4 us -> 4.01 us  [call(): pl.pallas_call(kernel, out_shape=shapes, in_specs=specs, out_specs=jax.tr...]
  transfers between devices with their start and end apart: 12 -> 12, of which waited for: 5 -> 4; matrix products, arithmetic and copies ran while one was open for 0% -> 0% of each run, Pallas kernels for 11% -> 11%
where the time goes in v8:
time: 19.9 us; the launch traced here: 19.7 us
  starting transfers between devices  13.4 us (67%)
  Pallas kernels  4.01 us (20%)
  waiting for transfers between devices  2.21 us (11%)
    ppermute x7, starting transfers between devices, exchange(): return lax.ppermute(value, 'space', [(i, i ^ bit) for i in range(count)])  7.85 us
    pallas_call x9, Pallas kernels, call(): pl.pallas_call(kernel, out_shape=shapes, in_specs=specs, out_specs=jax.tr...  4.01 us
    ppermute x3, starting transfers between devices, per_device(): held.append(lax.ppermute(own, ('energy', 'space'), pairs))  3.08 us
    ppermute x7, waiting for transfers between devices, exchange(): return lax.ppermute(value, 'space', [(i, i ^ bit) for i in range(count)])  1.95 us
    ppermute x1, starting transfers between devices, per_device(): arrived = lax.ppermute(coupling, ('energy', 'space'), pairs)  1.3 us
    ppermute x1, starting transfers between devices, per_device(): arrived = lax.ppermute(sums[step], 'energy', pairs)  1.12 us
  transfers between devices with their start and end apart: 12, of which 4 were waited for; matrix products, arithmetic and copies ran while one was open for 0% of the time, Pallas kernels for 11%

profile of v8, /device:TPU:1, one launch (start us, length us, event | category | flops | bytes accessed | tf_op | source)
XLA Modules:
  0.0 19.7 jit_solution(6449952739611774241)
XLA Ops:
  0.0 2.1 %collective-permute-start = (f32[2,128,128]{2,1,0:T(8,128)}, f32[2,128,128]{2,1,0:T(8,128)S(1)}, u32[]{:S(2)}, u32[]{:S(2)}) collective-permute-start(f32[2,128,128]{2,1,0:T(8,128)} %bitcast.6), channel_id=1, source_target_pairs={{0,8},{1,9},{2,10},{3,11},{4,12},{5,13},{6,14},{7,15},{8,0},{9,1},... | collective-permute-start | bytes 393224 | tf_op jit(solution)/shard_map/ppermute | solution.py:256
  2.1 1.0 %collective-permute-start.1 = (f32[2,128,128]{2,1,0:T(8,128)}, f32[2,128,128]{2,1,0:T(8,128)S(1)}, u32[]{:S(2)}, u32[]{:S(2)}) collective-permute-start(f32[2,128,128]{2,1,0:T(8,128)} %bitcast.7), channel_id=1, source_target_pairs={{0,1},{1,0},{2,3},{3,2},{4,5},{5,4},{6,7},{7,6},{8,16},{9,17},{10,... | collective-permute-start | bytes 393224 | tf_op jit(solution)/shard_map/ppermute | solution.py:256
  3.1 0.0 collective-permute-start.2
  3.1 0.0 copy-start.4
  3.1 0.0 copy-start.5
  3.1 0.0 copy-start.6
  3.1 1.3 %collective-permute-start.7 = (f32[2,128,128]{2,1,0:T(8,128)}, f32[2,128,128]{2,1,0:T(8,128)S(1)}, u32[]{:S(2)}, u32[]{:S(2)}) collective-permute-start(f32[2,128,128]{2,1,0:T(8,128)} %bitcast.13), channel_id=1, source_target_pairs={{0,4},{1,3},{2,6},{3,1},{4,0},{5,7},{6,2},{7,5},{8,12},{9,11},{10,... | collective-permute-start | bytes 393224 | tf_op jit(solution)/shard_map/ppermute | solution.py:274
  4.4 0.0 copy-start.1
  4.4 0.2 %collective-permute-start.5 = (f32[2,128,128]{2,1,0:T(8,128)}, f32[2,128,128]{2,1,0:T(8,128)S(1)}, u32[]{:S(2)}, u32[]{:S(2)}) collective-permute-start(f32[2,128,128]{2,1,0:T(8,128)} %bitcast.10), channel_id=1, source_target_pairs={{0,2},{1,3},{2,0},{3,1},{4,6},{5,7},{6,4},{7,5},{8,10},{9,11},{10,... | collective-permute-start | bytes 393224 | tf_op jit(solution)/shard_map/ppermute | solution.py:237
  4.6 0.0 copy-done.4
  4.6 0.0 copy-done.5
  4.6 0.0 copy-done.6
  4.6 0.7 %shard_map.73 = (f32[2,4,8,128]{3,2,1,0:T(8,128)S(1)}, s32[4,8,128]{2,1,0:T(8,128)S(1)}) custom-call(s32[8]{0:T(128)S(1)} %copy-done.4, f32[8]{0:T(128)S(1)} %copy-done.5, s32[4]{0:T(128)S(1)} %copy-done.6), custom_call_target="tpu_custom_call" | custom-call | flops 1000000000 | bytes 80 | tf_op jit(solution)/shard_map/pallas_call | solution.py:222
  5.3 0.3 %collective-permute-done.refs_1_ = f32[2,128,128]{2,1,0:T(8,128)S(1)} collective-permute-done((f32[2,128,128]{2,1,0:T(8,128)}, f32[2,128,128]{2,1,0:T(8,128)S(1)}, u32[]{:S(2)}, u32[]{:S(2)}) %collective-permute-start) | collective-permute-done | bytes 131104 | tf_op jit(solution)/shard_map/ppermute | solution.py:256
  5.6 0.0 collective-permute-done.1.refs_2_
  5.6 0.0 collective-permute-done.2.refs_3_
  5.6 0.0 copy-done.1
  5.6 0.0 copy-start.2
  5.6 0.1 shard_map.74
  5.7 1.1 %collective-permute-start.3 = (f32[2,128,128]{2,1,0:T(8,128)S(1)}, f32[2,128,128]{2,1,0:T(8,128)S(1)}, u32[]{:S(2)}, u32[]{:S(2)}) collective-permute-start(f32[2,128,128]{2,1,0:T(8,128)S(1)} %get-tuple-element.18), channel_id=1, source_target_pairs={{0,4},{4,0},{8,12},{12,8},{16,20},{20,16},{24,28},{28,24},{1,5},{5... | collective-permute-start | bytes 393224 | tf_op jit(solution)/shard_map/ppermute | solution.py:284
  6.8 0.0 copy-done.2
  6.8 0.0 copy-start.3
  6.8 0.0 copy-start
  6.8 1.9 %collective-permute-start.4 = (f32[2,128,128]{2,1,0:T(8,128)S(1)}, f32[2,128,128]{2,1,0:T(8,128)S(1)}, u32[]{:S(2)}, u32[]{:S(2)}) collective-permute-start(f32[2,128,128]{2,1,0:T(8,128)S(1)} %shard_map.75), channel_id=1, source_target_pairs={{0,1},{1,0},{2,3},{3,2},{4,5},{5,4},{6,7},{7,6},{8,9},{9,8},{10,11... | collective-permute-start | bytes 393224 | tf_op jit(solution)/shard_map/ppermute | solution.py:237
  8.7 0.0 collective-permute-done.7.arrived.refs_6_
  8.7 0.0 copy-done.3
  8.7 0.9 %collective-permute-start.8 = (f32[2,128,128]{2,1,0:T(8,128)S(1)}, f32[2,128,128]{2,1,0:T(8,128)S(1)}, u32[]{:S(2)}, u32[]{:S(2)}) collective-permute-start(f32[2,128,128]{2,1,0:T(8,128)S(1)} %shard_map.76), channel_id=1, source_target_pairs={{0,1},{1,0},{2,3},{3,2},{4,5},{5,4},{6,7},{7,6},{8,9},{9,8},{10,11... | collective-permute-start | bytes 393224 | tf_op jit(solution)/shard_map/ppermute | solution.py:237
  9.6 0.0 collective-permute-done.5.refs_2_
  9.6 1.1 %collective-permute-start.6 = (f32[2,128,128]{2,1,0:T(8,128)S(1)}, f32[2,128,128]{2,1,0:T(8,128)S(1)}, u32[]{:S(2)}, u32[]{:S(2)}) collective-permute-start(f32[2,128,128]{2,1,0:T(8,128)S(1)} %collective-permute-done.5.refs_2_), channel_id=1, source_target_pairs={{0,1},{1,0},{2,3},{3,2},{4,5},{5,4},{6,7},{7,6},{8,9},{9,8},{10,11... | collective-permute-start | bytes 393224 | tf_op jit(solution)/shard_map/ppermute | solution.py:237
  10.7 0.0 collective-permute-done.3
  10.7 1.3 %collective-permute-start.9 = (f32[2,128,128]{2,1,0:T(8,128)S(1)}, f32[2,128,128]{2,1,0:T(8,128)S(1)}, u32[]{:S(2)}, u32[]{:S(2)}) collective-permute-start(f32[2,128,128]{2,1,0:T(8,128)S(1)} %add.3.field), channel_id=1, source_target_pairs={{0,2},{1,3},{2,0},{3,1},{4,6},{5,7},{6,4},{7,5},{8,10},{9,11},{10,... | collective-permute-start | bytes 393224 | tf_op jit(solution)/shard_map/ppermute | solution.py:237
  12.0 0.0 collective-permute-done.4.refs_1_
  12.0 0.0 collective-permute-done.8.refs_5_.refs_7_
  12.0 0.0 collective-permute-done.6.refs_3_
  12.0 0.0 copy-done
  12.0 1.4 %shard_map.77 = (bf16[4,384,256]{2,1,0:T(8,128)(2,1)S(1)}, bf16[4,384,256]{2,1,0:T(8,128)(2,1)S(1)}, f32[2,128,128]{2,1,0:T(8,128)S(1)}, f32[2,128,128]{2,1,0:T(8,128)S(1)}) custom-call(s32[4,8,128]{2,1,0:T(8,128)S(1)} %get-tuple-element.15.kinds, f32[4,2,128,128]{3,2,1,0:T(8,128)S(1)} %copy-done, f32[2,128,128]{2,1,0:T(8,128)S(1)} %add.3.field, ...), custom_call_target="tpu_custom_call" | custom-call | flops 1000000000 | bytes 1720320 | tf_op jit(solution)/shard_map/pallas_call | solution.py:222
  13.5 1.1 %collective-permute-start.10 = (f32[2,128,128]{2,1,0:T(8,128)S(1)}, f32[2,128,128]{2,1,0:T(8,128)S(1)}, u32[]{:S(2)}, u32[]{:S(2)}) collective-permute-start(f32[2,128,128]{2,1,0:T(8,128)S(1)} %get-tuple-element.21), channel_id=1, source_target_pairs={{0,1},{1,0},{2,3},{3,2},{4,5},{5,4},{6,7},{7,6},{8,9},{9,8},{10,11... | collective-permute-start | bytes 393224 | tf_op jit(solution)/shard_map/ppermute | solution.py:237
  14.5 0.1 collective-permute-done.9.value
  14.6 0.9 %collective-permute-done.10.other.refs_0_ = f32[2,128,128]{2,1,0:T(8,128)S(1)} collective-permute-done((f32[2,128,128]{2,1,0:T(8,128)S(1)}, f32[2,128,128]{2,1,0:T(8,128)S(1)}, u32[]{:S(2)}, u32[]{:S(2)}) %collective-permute-start.10) | collective-permute-done | bytes 131104 | tf_op jit(solution)/shard_map/ppermute | solution.py:237
  15.5 0.7 %shard_map.79 = (f32[2,128,128]{2,1,0:T(8,128)S(1)}, f32[2,128,128]{2,1,0:T(8,128)S(1)}) custom-call(f32[2,128,128]{2,1,0:T(8,128)S(1)} %shard_map.78.arrived, f32[2,128,128]{2,1,0:T(8,128)S(1)} %collective-permute-done.10.other.refs_0_, bf16[4,384,256]{2,1,0:T(8,128)(2,1)S(1)} %get-tuple-element.19.high, bf16[4,384,256]{2,1,0:T(8,128)(2,1)S(1)} %get-tuple-element.20.low, ...), custom_call_target="tpu_custom_call" | custom-call | flops 1000000000 | bytes 1966080 | tf_op jit(solution)/shard_map/pallas_call | solution.py:222
  16.2 1.4 %collective-permute-start.11 = (f32[2,128,128]{2,1,0:T(8,128)S(1)}, f32[2,128,128]{2,1,0:T(8,128)S(1)}, u32[]{:S(2)}, u32[]{:S(2)}) collective-permute-start(f32[2,128,128]{2,1,0:T(8,128)S(1)} %get-tuple-element.24.refs_1_), channel_id=1, source_target_pairs={{0,1},{1,0},{2,3},{3,2},{4,5},{5,4},{6,7},{7,6},{8,9},{9,8},{10,11... | collective-permute-start | bytes 393224 | tf_op jit(solution)/shard_map/ppermute | solution.py:237
  17.7 1.0 %collective-permute-done.11.refs_0_ = f32[2,128,128]{2,1,0:T(8,128)S(1)} collective-permute-done((f32[2,128,128]{2,1,0:T(8,128)S(1)}, f32[2,128,128]{2,1,0:T(8,128)S(1)}, u32[]{:S(2)}, u32[]{:S(2)}) %collective-permute-start.11) | collective-permute-done | bytes 131104 | tf_op jit(solution)/shard_map/ppermute | solution.py:237
  18.6 1.1 %shard_map.81 = f32[2,128,128]{2,1,0:T(8,128)} custom-call(bf16[4,384,256]{2,1,0:T(8,128)(2,1)S(1)} %get-tuple-element.19.high, bf16[4,384,256]{2,1,0:T(8,128)(2,1)S(1)} %get-tuple-element.20.low, f32[2,128,128]{2,1,0:T(8,128)S(1)} %shard_map.80.before, f32[2,128,128]{2,1,0:T(8,128)S(1)} %collective-permute-done.11.refs_0_), custom_call_target="tpu_custom_call" | custom-call | flops 1000000000 | bytes 1835008 | tf_op jit(solution)/shard_map/pallas_call | solution.py:222
  (5 shorter events, 0.1 us)
Async XLA Ops:
  0.0 5.6 %collective-permute-start = (f32[2,128,128]{2,1,0:T(8,128)}, f32[2,128,128]{2,1,0:T(8,128)S(1)}, u32[]{:S(2)}, u32[]{:S(2)}) collective-permute-start(f32[2,128,128]{2,1,0:T(8,128)} %bitcast.6), channel_id=1, source_target_pairs={{0,8},{1,9},{2,10},{3,11},{4,12},{5,13},{6,14},{7,15},{8,0},{9,1},... | collective-permute-start | bytes 393224 | tf_op jit(solution)/shard_map/ppermute | solution.py:256
  2.1 3.4 %collective-permute-start.1 = (f32[2,128,128]{2,1,0:T(8,128)}, f32[2,128,128]{2,1,0:T(8,128)S(1)}, u32[]{:S(2)}, u32[]{:S(2)}) collective-permute-start(f32[2,128,128]{2,1,0:T(8,128)} %bitcast.7), channel_id=1, source_target_pairs={{0,1},{1,0},{2,3},{3,2},{4,5},{5,4},{6,7},{7,6},{8,16},{9,17},{10,... | collective-permute-start | bytes 393224 | tf_op jit(solution)/shard_map/ppermute | solution.py:256
  3.1 2.5 %collective-permute-start.2 = (f32[2,128,128]{2,1,0:T(8,128)}, f32[2,128,128]{2,1,0:T(8,128)S(1)}, u32[]{:S(2)}, u32[]{:S(2)}) collective-permute-start(f32[2,128,128]{2,1,0:T(8,128)} %bitcast.8), channel_id=1, source_target_pairs={{0,1},{1,0},{2,3},{3,2},{4,5},{5,4},{6,7},{7,6},{8,9},{9,8},{10,11... | collective-permute-start | bytes 393224 | tf_op jit(solution)/shard_map/ppermute | solution.py:256
  3.1 1.5 %copy-start.4 = (s32[8]{0:T(128)S(1)}, s32[8]{0:T(128)}, u32[]{:S(2)}) copy-start(s32[8]{0:T(128)} %offsets.1) | copy-start | bytes 100
  3.1 1.5 %copy-start.5 = (f32[8]{0:T(128)S(1)}, f32[8]{0:T(128)}, u32[]{:S(2)}) copy-start(f32[8]{0:T(128)} %weights.1) | copy-start | bytes 100
  3.1 1.5 %copy-start.6 = (s32[4]{0:T(128)S(1)}, s32[4]{0:T(128)}, u32[]{:S(2)}) copy-start(s32[4]{0:T(128)} %material.1) | copy-start | bytes 52
  3.1 5.6 %collective-permute-start.7 = (f32[2,128,128]{2,1,0:T(8,128)}, f32[2,128,128]{2,1,0:T(8,128)S(1)}, u32[]{:S(2)}, u32[]{:S(2)}) collective-permute-start(f32[2,128,128]{2,1,0:T(8,128)} %bitcast.13), channel_id=1, source_target_pairs={{0,4},{1,3},{2,6},{3,1},{4,0},{5,7},{6,2},{7,5},{8,12},{9,11},{10,... | collective-permute-start | bytes 393224 | tf_op jit(solution)/shard_map/ppermute | solution.py:274
  4.4 1.2 %copy-start.1 = (f32[2,1,1,128,128]{4,3,2,1,0:T(8,128)S(1)}, f32[2,1,1,128,128]{4,3,2,1,0:T(8,128)}, u32[]{:S(2)}) copy-start(f32[2,1,1,128,128]{4,3,2,1,0:T(8,128)} %param.7) | copy-start | bytes 393220
  4.4 5.2 %collective-permute-start.5 = (f32[2,128,128]{2,1,0:T(8,128)}, f32[2,128,128]{2,1,0:T(8,128)S(1)}, u32[]{:S(2)}, u32[]{:S(2)}) collective-permute-start(f32[2,128,128]{2,1,0:T(8,128)} %bitcast.10), channel_id=1, source_target_pairs={{0,2},{1,3},{2,0},{3,1},{4,6},{5,7},{6,4},{7,5},{8,10},{9,11},{10,... | collective-permute-start | bytes 393224 | tf_op jit(solution)/shard_map/ppermute | solution.py:237
  5.6 1.2 %copy-start.2 = (f32[2,1,1,128,128]{4,3,2,1,0:T(8,128)S(1)}, f32[2,1,1,128,128]{4,3,2,1,0:T(8,128)}, u32[]{:S(2)}) copy-start(f32[2,1,1,128,128]{4,3,2,1,0:T(8,128)} %param.8) | copy-start | bytes 393220
  5.7 5.0 %collective-permute-start.3 = (f32[2,128,128]{2,1,0:T(8,128)S(1)}, f32[2,128,128]{2,1,0:T(8,128)S(1)}, u32[]{:S(2)}, u32[]{:S(2)}) collective-permute-start(f32[2,128,128]{2,1,0:T(8,128)S(1)} %get-tuple-element.18), channel_id=1, source_target_pairs={{0,4},{4,0},{8,12},{12,8},{16,20},{20,16},{24,28},{28,24},{1,5},{5... | collective-permute-start | bytes 393224 | tf_op jit(solution)/shard_map/ppermute | solution.py:284
  6.8 1.9 %copy-start.3 = (f32[2,1,128,128]{3,2,1,0:T(8,128)S(1)}, f32[2,1,128,128]{3,2,1,0:T(8,128)}, u32[]{:S(2)}) copy-start(f32[2,1,128,128]{3,2,1,0:T(8,128)} %param.9) | copy-start | bytes 393220
  6.8 5.2 %copy-start = (f32[4,2,128,128]{3,2,1,0:T(8,128)S(1)}, f32[4,2,128,128]{3,2,1,0:T(8,128)}, u32[]{:S(2)}) copy-start(f32[4,2,128,128]{3,2,1,0:T(8,128)} %table.1) | copy-start | bytes 1572868
  6.8 5.2 %collective-permute-start.4 = (f32[2,128,128]{2,1,0:T(8,128)S(1)}, f32[2,128,128]{2,1,0:T(8,128)S(1)}, u32[]{:S(2)}, u32[]{:S(2)}) collective-permute-start(f32[2,128,128]{2,1,0:T(8,128)S(1)} %shard_map.75), channel_id=1, source_target_pairs={{0,1},{1,0},{2,3},{3,2},{4,5},{5,4},{6,7},{7,6},{8,9},{9,8},{10,11... | collective-permute-start | bytes 393224 | tf_op jit(solution)/shard_map/ppermute | solution.py:237
  8.7 3.3 %collective-permute-start.8 = (f32[2,128,128]{2,1,0:T(8,128)S(1)}, f32[2,128,128]{2,1,0:T(8,128)S(1)}, u32[]{:S(2)}, u32[]{:S(2)}) collective-permute-start(f32[2,128,128]{2,1,0:T(8,128)S(1)} %shard_map.76), channel_id=1, source_target_pairs={{0,1},{1,0},{2,3},{3,2},{4,5},{5,4},{6,7},{7,6},{8,9},{9,8},{10,11... | collective-permute-start | bytes 393224 | tf_op jit(solution)/shard_map/ppermute | solution.py:237
  9.6 2.4 %collective-permute-start.6 = (f32[2,128,128]{2,1,0:T(8,128)S(1)}, f32[2,128,128]{2,1,0:T(8,128)S(1)}, u32[]{:S(2)}, u32[]{:S(2)}) collective-permute-start(f32[2,128,128]{2,1,0:T(8,128)S(1)} %collective-permute-done.5.refs_2_), channel_id=1, source_target_pairs={{0,1},{1,0},{2,3},{3,2},{4,5},{5,4},{6,7},{7,6},{8,9},{9,8},{10,11... | collective-permute-start | bytes 393224 | tf_op jit(solution)/shard_map/ppermute | solution.py:237
  10.7 3.9 %collective-permute-start.9 = (f32[2,128,128]{2,1,0:T(8,128)S(1)}, f32[2,128,128]{2,1,0:T(8,128)S(1)}, u32[]{:S(2)}, u32[]{:S(2)}) collective-permute-start(f32[2,128,128]{2,1,0:T(8,128)S(1)} %add.3.field), channel_id=1, source_target_pairs={{0,2},{1,3},{2,0},{3,1},{4,6},{5,7},{6,4},{7,5},{8,10},{9,11},{10,... | collective-permute-start | bytes 393224 | tf_op jit(solution)/shard_map/ppermute | solution.py:237
  13.5 2.1 %collective-permute-start.10 = (f32[2,128,128]{2,1,0:T(8,128)S(1)}, f32[2,128,128]{2,1,0:T(8,128)S(1)}, u32[]{:S(2)}, u32[]{:S(2)}) collective-permute-start(f32[2,128,128]{2,1,0:T(8,128)S(1)} %get-tuple-element.21), channel_id=1, source_target_pairs={{0,1},{1,0},{2,3},{3,2},{4,5},{5,4},{6,7},{7,6},{8,9},{9,8},{10,11... | collective-permute-start | bytes 393224 | tf_op jit(solution)/shard_map/ppermute | solution.py:237
  16.2 2.4 %collective-permute-start.11 = (f32[2,128,128]{2,1,0:T(8,128)S(1)}, f32[2,128,128]{2,1,0:T(8,128)S(1)}, u32[]{:S(2)}, u32[]{:S(2)}) collective-permute-start(f32[2,128,128]{2,1,0:T(8,128)S(1)} %get-tuple-element.24.refs_1_), channel_id=1, source_target_pairs={{0,1},{1,0},{2,3},{3,2},{4,5},{5,4},{6,7},{7,6},{8,9},{9,8},{10,11... | collective-permute-start | bytes 393224 | tf_op jit(solution)/shard_map/ppermute | solution.py:237

commit v9 on v8

--- a/solution.py
+++ b/solution.py
@@ -105,7 +105,7 @@
 
 def factor_kernel(count, kinds, table, field, *refs):
     retarded, coupling, outs = refs[:count], refs[count : 2 * count], refs[2 * count : 2 * count + 2]
-    state, field_out, held_r, held_c, chain = refs[2 * count + 2 :]
+    turned, (state, field_out, held_r, held_c, chain) = refs[2 * count + 2 : 2 * count + 4], refs[2 * count + 4 :]
     mine = lax.axis_index("space")
     size = table.shape[-1]
 
@@ -127,6 +127,9 @@
                 position = sum(map(int, valid_terms(target, device, count)[:which]))
                 for out, part in zip(outs, parts):
                     out[device ^ target, position * size : (position + 1) * size] = part
+                if device ^ target == count - 1:
+                    for out, part in zip(turned, parts):
+                        out[position] = full(part).astype(F32).T.astype(BF16)
 
     def build_any():
         for slot in range(count):
@@ -167,7 +170,7 @@
     add_fields(count, {0: field}, outs, None, state)
 
 
-def add_fields(count, fields, factors, before, out, wanted=lambda slot, device: True):
+def add_fields(count, fields, factors, before, out, wanted=lambda slot, device: True, turned=None):
     size = out.shape[-1]
     mine = lax.axis_index("space")
 
@@ -178,7 +181,10 @@
             left = split(times(maps, fields[slot]))
             for term in range(terms):
                 here = slice(term * size, (term + 1) * size)
-                total = total + product([p[here] for p in left], [full(m[here]) for m in maps], NT)
+                if turned is None:
+                    total = total + product([p[here] for p in left], [full(m[here]) for m in maps], NT)
+                else:
+                    total = total + product([p[here] for p in left], [t[term] for t in turned], NN)
         out[...] = block_of(total)
 
     cases = {}
@@ -216,6 +222,10 @@
 def field_kernel(count, slots, high, low, before, *refs):
     fields = dict(zip(slots, refs))
     add_fields(count, fields, (high, low), before, refs[-1], lambda slot, device: slot != 1 or device % 2 == 0)
+
+
+def last_kernel(count, high, low, turned_high, turned_low, before, field, out):
+    add_fields(count, {count - 1: field}, (high, low), before, out, turned=(turned_high, turned_low))
 
 
 def call(kernel, shapes, specs, *args, scratch=()):
@@ -285,8 +295,9 @@
         field = field + arrived
 
     factor_shape = jax.ShapeDtypeStruct((slabs, 3 * size, 2 * size), BF16)
-    *factors, state, own = call(
-        functools.partial(factor_kernel, slabs), [factor_shape] * 2 + [block] * 2, [VMEM] * (2 * slabs + 3),
+    turned_shape = jax.ShapeDtypeStruct((3, 2 * size, 2 * size), BF16)
+    *factors, turned_high, turned_low, state, own = call(
+        functools.partial(factor_kernel, slabs), [factor_shape] * 2 + [turned_shape] * 2 + [block] * 2, [VMEM] * (2 * slabs + 3),
         kinds, gradient_table, field, *[all_r[s] for s in range(slabs)], *[all_c[s] for s in range(slabs)],
         scratch=[pltpu.VMEM((slabs, 2, size, size), F32)] * 2 + [pltpu.VMEM((size, 2 * size), F32)],
     )
@@ -308,7 +319,13 @@
     others = [key for key in sorted(fields) if key % 2 == 0 and key]
     fields |= gather({key: fields[key] for key in others}, [1])
     state = propagate([1] + others)
-    state = propagate([key ^ 1 for key in others])
+    if slabs <= 4 and len(others) == 1:
+        state = call(
+            functools.partial(last_kernel, slabs), block, [VMEM] * 6,
+            *factors, turned_high, turned_low, state, fields[slabs - 1],
+        )
+    else:
+        state = propagate([key ^ 1 for key in others])
     return state.reshape(lesser_prev.shape)
 
 

time: 19.9 us -> 19.9 us (level)
  transfers between devices with their start and end apart: 12 -> 12, of which waited for: 4 -> 3; matrix products, arithmetic and copies ran while one was open for 0% -> 0% of each run, Pallas kernels for 11% -> 11%
where the time goes in v9:
time: 19.9 us; the launch traced here: 19.7 us
  starting transfers between devices  13.4 us (67%)
  Pallas kernels  4 us (20%)
  waiting for transfers between devices  2.21 us (11%)
    ppermute x7, starting transfers between devices, exchange(): return lax.ppermute(value, 'space', [(i, i ^ bit) for i in range(count)])  7.85 us
    pallas_call x9, Pallas kernels, call(): pl.pallas_call(kernel, out_shape=shapes, in_specs=specs, out_specs=jax.tr...  4 us
    ppermute x3, starting transfers between devices, per_device(): held.append(lax.ppermute(own, ('energy', 'space'), pairs))  3.08 us
    ppermute x7, waiting for transfers between devices, exchange(): return lax.ppermute(value, 'space', [(i, i ^ bit) for i in range(count)])  1.95 us
    ppermute x1, starting transfers between devices, per_device(): arrived = lax.ppermute(coupling, ('energy', 'space'), pairs)  1.3 us
    ppermute x1, starting transfers between devices, per_device(): arrived = lax.ppermute(sums[step], 'energy', pairs)  1.12 us
  transfers between devices with their start and end apart: 12, of which 3 were waited for; matrix products, arithmetic and copies ran while one was open for 0% of the time, Pallas kernels for 11%

profile of v9, /device:TPU:1, one launch (start us, length us, event | category | flops | bytes accessed | tf_op | source)
XLA Modules:
  0.0 19.7 jit_solution(480965214967915290)
XLA Ops:
  0.0 2.1 %collective-permute-start = (f32[2,128,128]{2,1,0:T(8,128)}, f32[2,128,128]{2,1,0:T(8,128)S(1)}, u32[]{:S(2)}, u32[]{:S(2)}) collective-permute-start(f32[2,128,128]{2,1,0:T(8,128)} %bitcast.6), channel_id=1, source_target_pairs={{0,8},{1,9},{2,10},{3,11},{4,12},{5,13},{6,14},{7,15},{8,0},{9,1},... | collective-permute-start | bytes 393224 | tf_op jit(solution)/shard_map/ppermute | solution.py:266
  2.1 1.0 %collective-permute-start.1 = (f32[2,128,128]{2,1,0:T(8,128)}, f32[2,128,128]{2,1,0:T(8,128)S(1)}, u32[]{:S(2)}, u32[]{:S(2)}) collective-permute-start(f32[2,128,128]{2,1,0:T(8,128)} %bitcast.7), channel_id=1, source_target_pairs={{0,1},{1,0},{2,3},{3,2},{4,5},{5,4},{6,7},{7,6},{8,16},{9,17},{10,... | collective-permute-start | bytes 393224 | tf_op jit(solution)/shard_map/ppermute | solution.py:266
  3.1 0.0 collective-permute-start.2
  3.1 0.0 copy-start.4
  3.1 0.0 copy-start.5
  3.1 0.0 copy-start.6
  3.1 1.3 %collective-permute-start.7 = (f32[2,128,128]{2,1,0:T(8,128)}, f32[2,128,128]{2,1,0:T(8,128)S(1)}, u32[]{:S(2)}, u32[]{:S(2)}) collective-permute-start(f32[2,128,128]{2,1,0:T(8,128)} %bitcast.13), channel_id=1, source_target_pairs={{0,4},{1,3},{2,6},{3,1},{4,0},{5,7},{6,2},{7,5},{8,12},{9,11},{10,... | collective-permute-start | bytes 393224 | tf_op jit(solution)/shard_map/ppermute | solution.py:284
  4.4 0.0 copy-start.1
  4.4 0.2 %collective-permute-start.5 = (f32[2,128,128]{2,1,0:T(8,128)}, f32[2,128,128]{2,1,0:T(8,128)S(1)}, u32[]{:S(2)}, u32[]{:S(2)}) collective-permute-start(f32[2,128,128]{2,1,0:T(8,128)} %bitcast.10), channel_id=1, source_target_pairs={{0,2},{1,3},{2,0},{3,1},{4,6},{5,7},{6,4},{7,5},{8,10},{9,11},{10,... | collective-permute-start | bytes 393224 | tf_op jit(solution)/shard_map/ppermute | solution.py:247
  4.6 0.0 copy-done.4
  4.6 0.0 copy-done.5
  4.6 0.0 copy-done.6
  4.6 0.7 %shard_map.73 = (f32[2,4,8,128]{3,2,1,0:T(8,128)S(1)}, s32[4,8,128]{2,1,0:T(8,128)S(1)}) custom-call(s32[8]{0:T(128)S(1)} %copy-done.4, f32[8]{0:T(128)S(1)} %copy-done.5, s32[4]{0:T(128)S(1)} %copy-done.6), custom_call_target="tpu_custom_call" | custom-call | flops 1000000000 | bytes 80 | tf_op jit(solution)/shard_map/pallas_call | solution.py:232
  5.3 0.3 %collective-permute-done.refs_1_ = f32[2,128,128]{2,1,0:T(8,128)S(1)} collective-permute-done((f32[2,128,128]{2,1,0:T(8,128)}, f32[2,128,128]{2,1,0:T(8,128)S(1)}, u32[]{:S(2)}, u32[]{:S(2)}) %collective-permute-start) | collective-permute-done | bytes 131104 | tf_op jit(solution)/shard_map/ppermute | solution.py:266
  5.6 0.0 collective-permute-done.1.refs_2_
  5.6 0.0 collective-permute-done.2.refs_3_
  5.6 0.0 copy-done.1
  5.6 0.0 copy-start.2
  5.6 0.1 shard_map.74
  5.7 1.1 %collective-permute-start.3 = (f32[2,128,128]{2,1,0:T(8,128)S(1)}, f32[2,128,128]{2,1,0:T(8,128)S(1)}, u32[]{:S(2)}, u32[]{:S(2)}) collective-permute-start(f32[2,128,128]{2,1,0:T(8,128)S(1)} %get-tuple-element.20), channel_id=1, source_target_pairs={{0,4},{4,0},{8,12},{12,8},{16,20},{20,16},{24,28},{28,24},{1,5},{5... | collective-permute-start | bytes 393224 | tf_op jit(solution)/shard_map/ppermute | solution.py:294
  6.8 0.0 copy-done.2
  6.8 0.0 copy-start.3
  6.8 0.0 copy-start
  6.8 1.9 %collective-permute-start.4 = (f32[2,128,128]{2,1,0:T(8,128)S(1)}, f32[2,128,128]{2,1,0:T(8,128)S(1)}, u32[]{:S(2)}, u32[]{:S(2)}) collective-permute-start(f32[2,128,128]{2,1,0:T(8,128)S(1)} %shard_map.75), channel_id=1, source_target_pairs={{0,1},{1,0},{2,3},{3,2},{4,5},{5,4},{6,7},{7,6},{8,9},{9,8},{10,11... | collective-permute-start | bytes 393224 | tf_op jit(solution)/shard_map/ppermute | solution.py:247
  8.7 0.0 collective-permute-done.7.arrived.refs_6_
  8.7 0.0 copy-done.3
  8.7 0.9 %collective-permute-start.8 = (f32[2,128,128]{2,1,0:T(8,128)S(1)}, f32[2,128,128]{2,1,0:T(8,128)S(1)}, u32[]{:S(2)}, u32[]{:S(2)}) collective-permute-start(f32[2,128,128]{2,1,0:T(8,128)S(1)} %shard_map.76), channel_id=1, source_target_pairs={{0,1},{1,0},{2,3},{3,2},{4,5},{5,4},{6,7},{7,6},{8,9},{9,8},{10,11... | collective-permute-start | bytes 393224 | tf_op jit(solution)/shard_map/ppermute | solution.py:247
  9.6 0.0 collective-permute-done.5.refs_2_
  9.6 1.1 %collective-permute-start.6 = (f32[2,128,128]{2,1,0:T(8,128)S(1)}, f32[2,128,128]{2,1,0:T(8,128)S(1)}, u32[]{:S(2)}, u32[]{:S(2)}) collective-permute-start(f32[2,128,128]{2,1,0:T(8,128)S(1)} %collective-permute-done.5.refs_2_), channel_id=1, source_target_pairs={{0,1},{1,0},{2,3},{3,2},{4,5},{5,4},{6,7},{7,6},{8,9},{9,8},{10,11... | collective-permute-start | bytes 393224 | tf_op jit(solution)/shard_map/ppermute | solution.py:247
  10.7 0.0 collective-permute-done.3
  10.7 1.3 %collective-permute-start.9 = (f32[2,128,128]{2,1,0:T(8,128)S(1)}, f32[2,128,128]{2,1,0:T(8,128)S(1)}, u32[]{:S(2)}, u32[]{:S(2)}) collective-permute-start(f32[2,128,128]{2,1,0:T(8,128)S(1)} %add.3.field), channel_id=1, source_target_pairs={{0,2},{1,3},{2,0},{3,1},{4,6},{5,7},{6,4},{7,5},{8,10},{9,11},{10,... | collective-permute-start | bytes 393224 | tf_op jit(solution)/shard_map/ppermute | solution.py:247
  12.0 0.0 collective-permute-done.4.refs_1_
  12.0 0.0 collective-permute-done.8.refs_5_.refs_7_
  12.0 0.0 collective-permute-done.6.refs_3_
  12.0 0.0 copy-done
  12.0 1.4 %shard_map.77 = (bf16[4,384,256]{2,1,0:T(8,128)(2,1)S(1)}, bf16[4,384,256]{2,1,0:T(8,128)(2,1)S(1)}, bf16[3,256,256]{2,1,0:T(8,128)(2,1)S(1)}, bf16[3,256,256]{2...) custom-call(s32[4,8,128]{2,1,0:T(8,128)S(1)} %get-tuple-element.17.kinds, ...), custom_call_target="tpu_custom_call" | custom-call | flops 1000000000 | bytes 1720320 | tf_op jit(solution)/shard_map/pallas_call | solution.py:232
  13.5 1.1 %collective-permute-start.10 = (f32[2,128,128]{2,1,0:T(8,128)S(1)}, f32[2,128,128]{2,1,0:T(8,128)S(1)}, u32[]{:S(2)}, u32[]{:S(2)}) collective-permute-start(f32[2,128,128]{2,1,0:T(8,128)S(1)} %get-tuple-element.25), channel_id=1, source_target_pairs={{0,1},{1,0},{2,3},{3,2},{4,5},{5,4},{6,7},{7,6},{8,9},{9,8},{10,11... | collective-permute-start | bytes 393224 | tf_op jit(solution)/shard_map/ppermute | solution.py:247
  14.5 0.0 collective-permute-done.9.value
  14.6 0.9 %collective-permute-done.10.other.refs_0_ = f32[2,128,128]{2,1,0:T(8,128)S(1)} collective-permute-done((f32[2,128,128]{2,1,0:T(8,128)S(1)}, f32[2,128,128]{2,1,0:T(8,128)S(1)}, u32[]{:S(2)}, u32[]{:S(2)}) %collective-permute-start.10) | collective-permute-done | bytes 131104 | tf_op jit(solution)/shard_map/ppermute | solution.py:247
  15.5 0.7 %shard_map.79 = (f32[2,128,128]{2,1,0:T(8,128)S(1)}, f32[2,128,128]{2,1,0:T(8,128)S(1)}) custom-call(f32[2,128,128]{2,1,0:T(8,128)S(1)} %shard_map.78.arrived, f32[2,128,128]{2,1,0:T(8,128)S(1)} %collective-permute-done.10.other.refs_0_, bf16[4,384,256]{2,1,0:T(8,128)(2,1)S(1)} %get-tuple-element.21.high, bf16[4,384,256]{2,1,0:T(8,128)(2,1)S(1)} %get-tuple-element.22.low, ...), custom_call_target="tpu_custom_call" | custom-call | flops 1000000000 | bytes 1966080 | tf_op jit(solution)/shard_map/pallas_call | solution.py:232
  16.2 1.4 %collective-permute-start.11 = (f32[2,128,128]{2,1,0:T(8,128)S(1)}, f32[2,128,128]{2,1,0:T(8,128)S(1)}, u32[]{:S(2)}, u32[]{:S(2)}) collective-permute-start(f32[2,128,128]{2,1,0:T(8,128)S(1)} %get-tuple-element.28.refs_1_), channel_id=1, source_target_pairs={{0,1},{1,0},{2,3},{3,2},{4,5},{5,4},{6,7},{7,6},{8,9},{9,8},{10,11... | collective-permute-start | bytes 393224 | tf_op jit(solution)/shard_map/ppermute | solution.py:247
  17.7 1.0 %collective-permute-done.11.field = f32[2,128,128]{2,1,0:T(8,128)S(1)} collective-permute-done((f32[2,128,128]{2,1,0:T(8,128)S(1)}, f32[2,128,128]{2,1,0:T(8,128)S(1)}, u32[]{:S(2)}, u32[]{:S(2)}) %collective-permute-start.11) | collective-permute-done | bytes 131104 | tf_op jit(solution)/shard_map/ppermute | solution.py:247
  18.6 1.1 %shard_map.81 = f32[2,128,128]{2,1,0:T(8,128)} custom-call(bf16[4,384,256]{2,1,0:T(8,128)(2,1)S(1)} %get-tuple-element.21.high, bf16[4,384,256]{2,1,0:T(8,128)(2,1)S(1)} %get-tuple-element.22.low, bf16[3,256,256]{2,1,0:T(8,128)(2,1)S(1)} %get-tuple-element.23.turned_high, bf16[3,256,256]{2,1,0:T(8,128)(2,1)S(1)} %get-tuple-element.24.turned_low, ...), custom_call_target="tpu_custom_call" | custom-call | flops 1000000000 | bytes 2621440 | tf_op jit(solution)/shard_map/pallas_call | solution.py:232
  (5 shorter events, 0.1 us)
Async XLA Ops:
  0.0 5.6 %collective-permute-start = (f32[2,128,128]{2,1,0:T(8,128)}, f32[2,128,128]{2,1,0:T(8,128)S(1)}, u32[]{:S(2)}, u32[]{:S(2)}) collective-permute-start(f32[2,128,128]{2,1,0:T(8,128)} %bitcast.6), channel_id=1, source_target_pairs={{0,8},{1,9},{2,10},{3,11},{4,12},{5,13},{6,14},{7,15},{8,0},{9,1},... | collective-permute-start | bytes 393224 | tf_op jit(solution)/shard_map/ppermute | solution.py:266
  2.1 3.4 %collective-permute-start.1 = (f32[2,128,128]{2,1,0:T(8,128)}, f32[2,128,128]{2,1,0:T(8,128)S(1)}, u32[]{:S(2)}, u32[]{:S(2)}) collective-permute-start(f32[2,128,128]{2,1,0:T(8,128)} %bitcast.7), channel_id=1, source_target_pairs={{0,1},{1,0},{2,3},{3,2},{4,5},{5,4},{6,7},{7,6},{8,16},{9,17},{10,... | collective-permute-start | bytes 393224 | tf_op jit(solution)/shard_map/ppermute | solution.py:266
  3.1 2.5 %collective-permute-start.2 = (f32[2,128,128]{2,1,0:T(8,128)}, f32[2,128,128]{2,1,0:T(8,128)S(1)}, u32[]{:S(2)}, u32[]{:S(2)}) collective-permute-start(f32[2,128,128]{2,1,0:T(8,128)} %bitcast.8), channel_id=1, source_target_pairs={{0,1},{1,0},{2,3},{3,2},{4,5},{5,4},{6,7},{7,6},{8,9},{9,8},{10,11... | collective-permute-start | bytes 393224 | tf_op jit(solution)/shard_map/ppermute | solution.py:266
  3.1 1.5 %copy-start.4 = (s32[8]{0:T(128)S(1)}, s32[8]{0:T(128)}, u32[]{:S(2)}) copy-start(s32[8]{0:T(128)} %offsets.1) | copy-start | bytes 100
  3.1 1.5 %copy-start.5 = (f32[8]{0:T(128)S(1)}, f32[8]{0:T(128)}, u32[]{:S(2)}) copy-start(f32[8]{0:T(128)} %weights.1) | copy-start | bytes 100
  3.1 1.5 %copy-start.6 = (s32[4]{0:T(128)S(1)}, s32[4]{0:T(128)}, u32[]{:S(2)}) copy-start(s32[4]{0:T(128)} %material.1) | copy-start | bytes 52
  3.1 5.6 %collective-permute-start.7 = (f32[2,128,128]{2,1,0:T(8,128)}, f32[2,128,128]{2,1,0:T(8,128)S(1)}, u32[]{:S(2)}, u32[]{:S(2)}) collective-permute-start(f32[2,128,128]{2,1,0:T(8,128)} %bitcast.13), channel_id=1, source_target_pairs={{0,4},{1,3},{2,6},{3,1},{4,0},{5,7},{6,2},{7,5},{8,12},{9,11},{10,... | collective-permute-start | bytes 393224 | tf_op jit(solution)/shard_map/ppermute | solution.py:284
  4.4 1.2 %copy-start.1 = (f32[2,1,1,128,128]{4,3,2,1,0:T(8,128)S(1)}, f32[2,1,1,128,128]{4,3,2,1,0:T(8,128)}, u32[]{:S(2)}) copy-start(f32[2,1,1,128,128]{4,3,2,1,0:T(8,128)} %param.7) | copy-start | bytes 393220
  4.4 5.2 %collective-permute-start.5 = (f32[2,128,128]{2,1,0:T(8,128)}, f32[2,128,128]{2,1,0:T(8,128)S(1)}, u32[]{:S(2)}, u32[]{:S(2)}) collective-permute-start(f32[2,128,128]{2,1,0:T(8,128)} %bitcast.10), channel_id=1, source_target_pairs={{0,2},{1,3},{2,0},{3,1},{4,6},{5,7},{6,4},{7,5},{8,10},{9,11},{10,... | collective-permute-start | bytes 393224 | tf_op jit(solution)/shard_map/ppermute | solution.py:247
  5.6 1.2 %copy-start.2 = (f32[2,1,1,128,128]{4,3,2,1,0:T(8,128)S(1)}, f32[2,1,1,128,128]{4,3,2,1,0:T(8,128)}, u32[]{:S(2)}) copy-start(f32[2,1,1,128,128]{4,3,2,1,0:T(8,128)} %param.8) | copy-start | bytes 393220
  5.7 5.0 %collective-permute-start.3 = (f32[2,128,128]{2,1,0:T(8,128)S(1)}, f32[2,128,128]{2,1,0:T(8,128)S(1)}, u32[]{:S(2)}, u32[]{:S(2)}) collective-permute-start(f32[2,128,128]{2,1,0:T(8,128)S(1)} %get-tuple-element.20), channel_id=1, source_target_pairs={{0,4},{4,0},{8,12},{12,8},{16,20},{20,16},{24,28},{28,24},{1,5},{5... | collective-permute-start | bytes 393224 | tf_op jit(solution)/shard_map/ppermute | solution.py:294
  6.8 1.9 %copy-start.3 = (f32[2,1,128,128]{3,2,1,0:T(8,128)S(1)}, f32[2,1,128,128]{3,2,1,0:T(8,128)}, u32[]{:S(2)}) copy-start(f32[2,1,128,128]{3,2,1,0:T(8,128)} %param.9) | copy-start | bytes 393220
  6.8 5.2 %copy-start = (f32[4,2,128,128]{3,2,1,0:T(8,128)S(1)}, f32[4,2,128,128]{3,2,1,0:T(8,128)}, u32[]{:S(2)}) copy-start(f32[4,2,128,128]{3,2,1,0:T(8,128)} %table.1) | copy-start | bytes 1572868
  6.8 5.2 %collective-permute-start.4 = (f32[2,128,128]{2,1,0:T(8,128)S(1)}, f32[2,128,128]{2,1,0:T(8,128)S(1)}, u32[]{:S(2)}, u32[]{:S(2)}) collective-permute-start(f32[2,128,128]{2,1,0:T(8,128)S(1)} %shard_map.75), channel_id=1, source_target_pairs={{0,1},{1,0},{2,3},{3,2},{4,5},{5,4},{6,7},{7,6},{8,9},{9,8},{10,11... | collective-permute-start | bytes 393224 | tf_op jit(solution)/shard_map/ppermute | solution.py:247
  8.7 3.3 %collective-permute-start.8 = (f32[2,128,128]{2,1,0:T(8,128)S(1)}, f32[2,128,128]{2,1,0:T(8,128)S(1)}, u32[]{:S(2)}, u32[]{:S(2)}) collective-permute-start(f32[2,128,128]{2,1,0:T(8,128)S(1)} %shard_map.76), channel_id=1, source_target_pairs={{0,1},{1,0},{2,3},{3,2},{4,5},{5,4},{6,7},{7,6},{8,9},{9,8},{10,11... | collective-permute-start | bytes 393224 | tf_op jit(solution)/shard_map/ppermute | solution.py:247
  9.6 2.4 %collective-permute-start.6 = (f32[2,128,128]{2,1,0:T(8,128)S(1)}, f32[2,128,128]{2,1,0:T(8,128)S(1)}, u32[]{:S(2)}, u32[]{:S(2)}) collective-permute-start(f32[2,128,128]{2,1,0:T(8,128)S(1)} %collective-permute-done.5.refs_2_), channel_id=1, source_target_pairs={{0,1},{1,0},{2,3},{3,2},{4,5},{5,4},{6,7},{7,6},{8,9},{9,8},{10,11... | collective-permute-start | bytes 393224 | tf_op jit(solution)/shard_map/ppermute | solution.py:247
  10.7 3.9 %collective-permute-start.9 = (f32[2,128,128]{2,1,0:T(8,128)S(1)}, f32[2,128,128]{2,1,0:T(8,128)S(1)}, u32[]{:S(2)}, u32[]{:S(2)}) collective-permute-start(f32[2,128,128]{2,1,0:T(8,128)S(1)} %add.3.field), channel_id=1, source_target_pairs={{0,2},{1,3},{2,0},{3,1},{4,6},{5,7},{6,4},{7,5},{8,10},{9,11},{10,... | collective-permute-start | bytes 393224 | tf_op jit(solution)/shard_map/ppermute | solution.py:247
  13.5 2.1 %collective-permute-start.10 = (f32[2,128,128]{2,1,0:T(8,128)S(1)}, f32[2,128,128]{2,1,0:T(8,128)S(1)}, u32[]{:S(2)}, u32[]{:S(2)}) collective-permute-start(f32[2,128,128]{2,1,0:T(8,128)S(1)} %get-tuple-element.25), channel_id=1, source_target_pairs={{0,1},{1,0},{2,3},{3,2},{4,5},{5,4},{6,7},{7,6},{8,9},{9,8},{10,11... | collective-permute-start | bytes 393224 | tf_op jit(solution)/shard_map/ppermute | solution.py:247
  16.2 2.4 %collective-permute-start.11 = (f32[2,128,128]{2,1,0:T(8,128)S(1)}, f32[2,128,128]{2,1,0:T(8,128)S(1)}, u32[]{:S(2)}, u32[]{:S(2)}) collective-permute-start(f32[2,128,128]{2,1,0:T(8,128)S(1)} %get-tuple-element.28.refs_1_), channel_id=1, source_target_pairs={{0,1},{1,0},{2,3},{3,2},{4,5},{5,4},{6,7},{7,6},{8,9},{9,8},{10,11... | collective-permute-start | bytes 393224 | tf_op jit(solution)/shard_map/ppermute | solution.py:247
